TPU v7x, 512 devices: a whole 4x8x8 slice. The times are simulated.
512 devices in a mesh: row: 16 (over z, core), col: 8 (over y), layer: 4 (over x).
Axes of the slice: x: 4, y: 8, z: 8, core: 2. Of those that a mesh axis runs over, the one named last changes fastest.
Arguments:
- left_slab: float32 [4, 8192, 2048], P('layer', 'row', 'col'), may hold values from -6 to 6
- right_window: float32 [4, 2048, 8192], P('layer', 'row', 'col'), may hold values from -0.0625 to 0.0625
- left_pattern: int32 [4, 128, 32], P('layer', 'row', 'col'), may hold values 0 or 1
- right_pattern: int32 [4, 32, 128], P('layer', 'row', 'col'), may hold values from 0 to 1, as said below
- square_blocks: float32 [8192, 8192], P(('row', 'layer'), 'col'), may hold values from -6 to 6
- result_pattern: int32 [128, 128], P('row', 'col'), may hold values 0 or 1
Outputs:
- purified: float32 [8192, 8192], P(('row', 'layer'), 'col')
Inputs may be any that keep to these rules, and one draw needn't show every extreme that they name: `right_pattern`: for each group and each tile of 32 // 16 inner blocks by 16 block columns (the tiles aligned with those sizes), exactly three quarters of the tile's blocks are 1.
All inputs are finite; a program needn't handle non-finite values. No bound on the sum of `left_pattern` or of `result_pattern` on one device may be relied on, other than what follows from the above.
Results may differ from a plain program's by a relative error of at most 0.0001.
Values sent between devices are 32-bit elements; how exact they have to be, the bound alone decides.
No kernel may reach another device: no remote copies, remote signals or barrier semaphores. Data moves between devices by JAX's collectives and lax.ppermute only.
A program may use at most 128 MiB of HBM per device.

v0:
```python
import jax
import jax.numpy as jnp
from jax import lax
from jax.sharding import PartitionSpec as P

BS = 64


def widen(pattern, size):
    height, breadth = pattern.shape
    flags = pattern.astype(jnp.float32)[:, None, :, None]
    flags = jnp.broadcast_to(flags, (height, size, breadth, size))
    return flags.reshape((height * size, breadth * size))


def multiply(block_left, block_right):
    return jnp.dot(
        block_left, block_right, precision=lax.Precision.HIGHEST, preferred_element_type=jnp.float32
    )


def local(left_slab, right_window, left_pattern, right_pattern, square_blocks, result_pattern):
    masked_left = left_slab[0] * widen(left_pattern[0], BS)
    whole_left = lax.all_gather(masked_left, "col", axis=1, tiled=True)
    masked_right = right_window[0] * widen(right_pattern[0], BS)
    cube = multiply(whole_left, lax.all_gather(masked_right, "row", axis=0, tiled=True))
    share = square_blocks.shape[0]
    offset = lax.axis_index("layer") * share
    mine = lax.psum_scatter(cube, "layer", scatter_dimension=0, tiled=True)
    keeper = lax.dynamic_slice_in_dim(widen(result_pattern, BS), offset, share, 0)
    return keeper * (3.0 * square_blocks - 2.0 * mine)


def solution(mesh):
    in_specs = (
        P("layer", "row", "col"),
        P("layer", "row", "col"),
        P("layer", "row", "col"),
        P("layer", "row", "col"),
        P(("row", "layer"), "col"),
        P("row", "col"),
    )
    out_specs = P(("row", "layer"), "col")
    return jax.shard_map(local, mesh=mesh, in_specs=in_specs, out_specs=out_specs, check_vma=False)
```

profile of v0, /device:TPU:1, one launch (start us, length us, event | category | flops | bytes accessed | tf_op | source)
XLA Modules:
  0.0 192.7 jit_solution(16301829390151068417)
XLA Ops:
  6.5 0.0 copy-start.3
  6.5 0.0 copy-start
  6.5 0.0 all-gather.3.cloned.1.call-start
  6.5 0.7 convert_bitcast_fusion
  7.3 0.1 copy.7
  7.4 0.2 broadcast_in_dim.7
  7.6 0.6 reshape.23
  8.2 1.9 bitcast_multiply_fusion.1
  10.1 0.0 all-gather.3.cloned.1.call-update
  10.1 0.0 all-gather.5.cloned.1.call-start
  10.2 0.0 copy-done.3
  10.2 0.1 broadcast_in_dim.8
  10.3 0.3 reshape.24
  10.7 0.0 copy-done
  10.7 0.9 bitcast_multiply_fusion
  11.5 0.0 all-gather.5.cloned.1.call-update
  11.6 0.0 copy-start.2
  11.6 0.0 reduce-scatter.2.cloned.1.call-start
  11.6 61.3 %all-gather.3.cloned.1.call-done = f32[512,2048]{1,0:T(8,128)} async-done(((f32[512,256]{1,0:T(8,128)}), f32[512,2048]{1,0:T(8,128)}) %all-gather.3.cloned.1.call-update) | async-done | bytes 4194320 | tf_op jit(solution)/shard_map/all_gather | solution.py:24
  72.9 61.0 %all-gather.5.cloned.1.call-done = f32[2048,1024]{1,0:T(8,128)} async-done(((f32[128,1024]{1,0:T(8,128)}), f32[2048,1024]{1,0:T(8,128)}) %all-gather.5.cloned.1.call-update) | async-done | bytes 8388624 | tf_op jit(solution)/shard_map/all_gather | solution.py:26
  133.9 17.6 %fusion = f32[512,1024]{1,0:T(8,128)} fusion(f32[512,2048]{1,0:T(8,128)} %all-gather.3.cloned.1.call-done, f32[2048,1024]{1,0:T(8,128)} %all-gather.5.cloned.1.call-done), kind=kOutput, calls=%fused_computation.5 | convolution fusion | flops 12884901888 | bytes 14680064 | tf_op jit(solution)/shard_map/dot_general | solution.py:17
  151.4 0.0 reduce-scatter.2.cloned.1.call-update
  151.4 0.0 copy-done.2
  151.5 2.3 %broadcast_in_dim.6 = f32[8,64,16,64]{3,2,1,0:T(8,128)} broadcast(f32[8,16]{1,0:T(8,128)S(1)} %convert_element_type.23), dimensions={0,2} | broadcast | bytes 2097664 | tf_op jit(solution)/shard_map/broadcast_in_dim | solution.py:12
  153.8 0.0 copy-start.1
  153.8 3.6 %reshape.22 = f32[512,1024]{1,0:T(8,128)S(1)} reshape(f32[8,64,16,64]{3,2,1,0:T(8,128)} %broadcast_in_dim.6) | data formatting | bytes 4194304 | tf_op jit(solution)/shard_map/reshape | solution.py:13
  157.3 26.9 %reduce-scatter.2.cloned.1.call-done = f32[128,1024]{1,0:T(8,128)} async-done(((f32[512,1024]{1,0:T(8,128)}), f32[128,1024]{1,0:T(8,128)}) %reduce-scatter.2.cloned.1.call-update) | async-done | bytes 524304 | tf_op jit(solution)/shard_map/reduce_scatter | solution.py:29
  184.3 0.0 copy-done.1
  184.3 1.9 %subtract_multiply_fusion = f32[128,1024]{1,0:T(8,128)} fusion(f32[128,1024]{1,0:T(8,128)} %reduce-scatter.2.cloned.1.call-done, f32[128,1024]{1,0:T(8,128)S(1)} %copy-done.1, f32[512,1024]{1,0:T(8,128)S(1)} %reshape.22, s32[]{:T(128)S(6)} %select_n.3), kind=kLoop, calls=%fused_computation.2 | loop fusion | flops 524288 | bytes 2097156 | tf_op jit(solution)/shard_map/mul | solution.py:31
  (2 shorter events, 0.0 us)
Async XLA Ops:
  6.5 3.7 %copy-start.3 = (s32[1,2,16]{2,1,0:T(2,128)S(1)}, s32[1,2,16]{2,1,0:T(2,128)}, u32[]{:S(2)}) copy-start(s32[1,2,16]{2,1,0:T(2,128)} %param.9) | copy-start | bytes 388
  6.5 4.1 %copy-start = (f32[1,128,1024]{2,1,0:T(8,128)S(1)}, f32[1,128,1024]{2,1,0:T(8,128)}, u32[]{:S(2)}) copy-start(f32[1,128,1024]{2,1,0:T(8,128)} %param.7) | copy-start | bytes 1572868
  6.5 66.4 %all-gather.3.cloned.1.call-start = ((), (), s32[]{:S(2)}) async-start(), calls=%async_computation.1 | async-start | bytes 4718592 | tf_op jit(solution)/shard_map/all_gather | solution.py:24
  10.1 123.7 %all-gather.5.cloned.1.call-start = ((), (), s32[]{:S(2)}) async-start(), calls=%async_computation.2 | async-start | bytes 8912896 | tf_op jit(solution)/shard_map/all_gather | solution.py:26
  11.6 139.9 %copy-start.2 = (s32[8,16]{1,0:T(8,128)S(1)}, s32[8,16]{1,0:T(8,128)}, u32[]{:S(2)}) copy-start(s32[8,16]{1,0:T(8,128)} %param.11) | copy-start | bytes 1540
  11.6 172.7 %reduce-scatter.2.cloned.1.call-start = ((), (), s32[]{:S(2)}) async-start(), calls=%async_computation.3 | async-start | bytes 2621440 | tf_op jit(solution)/shard_map/reduce_scatter | solution.py:29
  153.8 30.5 %copy-start.1 = (f32[128,1024]{1,0:T(8,128)S(1)}, f32[128,1024]{1,0:T(8,128)}, u32[]{:S(2)}) copy-start(f32[128,1024]{1,0:T(8,128)} %param.10) | copy-start | bytes 1572868
Sparse Core Ops, SparseCore 0:
  10.3 62.6 all-gather.2
  75.0 58.7 all-gather.4
  151.6 32.6 reduce-scatter.1
where the time goes:
time: 193 us
  waiting for transfers between devices  149 us (77%)
  matrix products  17.6 us (9%)
  between operations  13.2 us (7%)
  local copies, waits for them, and re-layouts  7.21 us (4%)
  other arithmetic  5.47 us (3%)
    all_gather x1, waiting for transfers between devices, local(): whole_left = lax.all_gather(masked_left, 'col', axis=1, tiled=True)  61.3 us
    all_gather x1, waiting for transfers between devices, local(): lax.all_gather(masked_right, 'row', axis=0, tiled=True)  61 us
    reduce_scatter x1, waiting for transfers between devices, local(): mine = lax.psum_scatter(cube, 'layer', scatter_dimension=0, tiled=True)  26.9 us
    dot_general x1, matrix products, multiply(): jnp.dot(block_left, block_right, precision=lax.Precision.HIGHEST, preferr...  17.6 us
    reshape x3, local copies, waits for them, and re-layouts, widen(): return flags.reshape((height * size, breadth * size))  4.49 us
  transfers between devices with their start and end apart: 3, of which 3 were waited for; matrix products, arithmetic and copies ran while one was open for 4% of the time, Pallas kernels for 0%

commit v1 on v0

v1 whole, which is shorter than its diff:
```python
import jax
import jax.numpy as jnp
from jax import lax
from jax.experimental import pallas as pl
from jax.experimental.pallas import tpu as pltpu
from jax.sharding import PartitionSpec as P

BS = 64
LANES = 128
MAIN = 24
EXTRA = 8
ROWS_MAIN = 6 * LANES
PACKED = ROWS_MAIN + 16
BF = jnp.bfloat16
F32 = jnp.float32


def lane_half():
    return lax.broadcasted_iota(jnp.int32, (BS, LANES), 1) // BS


def pair_mask(low, high):
    return jnp.where(lane_half() == 0, low.astype(F32), high.astype(F32))


def mask_left_kernel(flags, x, out):
    for i in range(8):
        for c in range(2):
            mask = pair_mask(flags[i, 2 * c], flags[i, 2 * c + 1])
            at = (pl.ds(i * BS, BS), pl.ds(c * LANES, LANES))
            out[at] = x[at] * mask


def mask_left(x, flags):
    return pl.pallas_call(
        mask_left_kernel,
        out_shape=jax.ShapeDtypeStruct(x.shape, F32),
        in_specs=[pl.BlockSpec(memory_space=pltpu.SMEM), pl.BlockSpec(memory_space=pltpu.VMEM)],
        out_specs=pl.BlockSpec(memory_space=pltpu.VMEM),
    )(flags, x)


def pack_kernel(flags, x, out, holes, homes):
    for c in range(6):
        out[pl.ds(c * LANES, LANES), :] = x[:, pl.ds(c * LANES, LANES)]
    count = jnp.int32(0)
    for s in range(MAIN):
        holes[count] = s
        count = count + jnp.where(flags[s // 12, s % 12] == 0, 1, 0)
    used = jnp.int32(0)
    half = lane_half()
    for e in range(EXTRA):
        kept = flags[e // 4, 12 + e % 4] != 0
        slot = holes[jnp.minimum(used, EXTRA)]
        homes[e] = jnp.where(kept, slot, MAIN)
        used = used + jnp.where(kept, 1, 0)

        @pl.when(kept)
        def _():
            column = slot % 12
            at = pl.ds(pl.multiple_of((column // 2) * LANES + (slot // 12) * BS, BS), BS)
            block = x[pl.ds((e // 4) * BS, BS), pl.ds((6 + (e % 4) // 2) * LANES, LANES)]
            turned = pltpu.roll(block, BS, 1)
            side = column % 2
            block = jnp.where(side == e % 2, block, turned)
            out[at, :] = jnp.where(half == side, block, out[at, :])

    lane = lax.broadcasted_iota(jnp.int32, (1, LANES), 1)
    row = jnp.zeros((1, LANES), F32)
    for e in range(EXTRA):
        row = jnp.where(lane == e, homes[e].astype(F32), row)
    out[pl.ds(ROWS_MAIN, 1), :] = row
    for b in range(2):
        for c in range(6):
            mask = jnp.where(lane < BS, flags[b, 2 * c].astype(F32), flags[b, 2 * c + 1].astype(F32))
            out[pl.ds(ROWS_MAIN + 1 + b * 6 + c, 1), :] = mask
    out[pl.ds(ROWS_MAIN + 13, 3), :] = jnp.zeros((3, LANES), F32)


def pack_right(x, flags):
    return pl.pallas_call(
        pack_kernel,
        out_shape=jax.ShapeDtypeStruct((PACKED, LANES), F32),
        in_specs=[pl.BlockSpec(memory_space=pltpu.SMEM), pl.BlockSpec(memory_space=pltpu.VMEM)],
        out_specs=pl.BlockSpec(memory_space=pltpu.VMEM),
        scratch_shapes=[pltpu.SMEM((MAIN + 1,), jnp.int32), pltpu.SMEM((EXTRA,), jnp.int32)],
    )(flags, x)


def split(x):
    high = x.astype(BF)
    return high, (x - high.astype(F32)).astype(BF)


def unpack_kernel(homes, x, high, low):
    z = pl.program_id(0)
    half = lane_half()

    def store(b, c, value):
        at = (pl.ds(b * BS, BS), pl.ds(c * LANES, LANES))
        high[at], low[at] = split(value)

    for b in range(2):
        for c in range(6):
            mask = x[0, pl.ds(ROWS_MAIN + 1 + b * 6 + c, 1), :]
            store(b, c, x[0, pl.ds(c * LANES + b * BS, BS), :] * mask)
        for c in range(2):
            sides = []
            for k in range(2):
                slot = homes[z, b * 4 + 2 * c + k]
                kept = slot < MAIN
                slot = jnp.minimum(slot, MAIN - 1)
                column = slot % 12
                at = pl.ds(pl.multiple_of((column // 2) * LANES + (slot // 12) * BS, BS), BS)
                block = x[0, at, :]
                block = jnp.where(column % 2 == k, block, pltpu.roll(block, BS, 1))
                sides.append(jnp.where(kept, block, 0.0))
            store(b, 6 + c, jnp.where(half == 0, sides[0], sides[1]))


def unpack_right(packed, homes):
    shape = jax.ShapeDtypeStruct((16 * LANES, 1024), BF)
    block = pl.BlockSpec((LANES, 1024), lambda z, *_: (z, 0))
    return pl.pallas_call(
        unpack_kernel,
        out_shape=(shape, shape),
        grid_spec=pltpu.PrefetchScalarGridSpec(
            num_scalar_prefetch=1,
            grid=(16,),
            in_specs=[pl.BlockSpec((1, PACKED, LANES), lambda z, *_: (z, 0, 0))],
            out_specs=(block, block),
        ),
    )(homes, packed)


def product_kernel(where, *refs):
    parts, (right_high, right_low, out, left_high, left_low) = refs[:9], refs[9:]

    @pl.when(pl.program_id(0) == 0)
    def _():
        for n, part in enumerate(parts):
            first = 256 if n == 8 else 0
            at = (pl.ds(first, part.shape[0]), pl.ds(pl.multiple_of(where[min(n, 7)] * 256, 256), 256))
            left_high[at], left_low[at] = split(part[...])

    total = jnp.dot(left_low[...], right_high[...], preferred_element_type=F32)
    total += jnp.dot(left_high[...], right_low[...], preferred_element_type=F32)
    total += jnp.dot(left_high[...], right_high[...], preferred_element_type=F32)
    out[...] = total


def product(parts, where, right_high, right_low):
    width = 256
    right = pl.BlockSpec((2048, width), lambda j, *_: (0, j))
    return pl.pallas_call(
        product_kernel,
        out_shape=jax.ShapeDtypeStruct((512, 1024), F32),
        grid_spec=pltpu.PrefetchScalarGridSpec(
            num_scalar_prefetch=1,
            grid=(1024 // width,),
            in_specs=[pl.BlockSpec(p.shape, lambda j, *_: (0, 0)) for p in parts] + [right, right],
            out_specs=pl.BlockSpec((512, width), lambda j, *_: (0, j)),
            scratch_shapes=[pltpu.VMEM((512, 2048), BF)] * 2,
        ),
        compiler_params=pltpu.CompilerParams(vmem_limit_bytes=40 << 20),
    )(where, *parts, right_high, right_low)


def finish_kernel(where, flags, terms, square, out):
    for b in range(2):
        for c in range(8):
            at = (pl.ds(b * BS, BS), pl.ds(c * LANES, LANES))
            total = (terms[(0,) + at] + terms[(1,) + at]) + (terms[(2,) + at] + terms[(3,) + at])
            line = where[0] * 2 + b
            mask = pair_mask(flags[line, 2 * c], flags[line, 2 * c + 1])
            out[at] = mask * (3.0 * square[at] - 2.0 * total)


def finish(terms, square, flags, where):
    smem = pl.BlockSpec(memory_space=pltpu.SMEM)
    vmem = pl.BlockSpec(memory_space=pltpu.VMEM)
    return pl.pallas_call(
        finish_kernel,
        out_shape=jax.ShapeDtypeStruct(square.shape, F32),
        in_specs=[smem, smem, vmem, vmem],
        out_specs=vmem,
    )(where, flags, terms, square)


def shift(n, by):
    return [(i, (i + by) % n) for i in range(n)]


def gather_left(own):
    def send(x, by):
        return lax.ppermute(x, "col", shift(8, by))

    up1, down1 = send(own, 1), send(own, -1)
    up2, down2 = send(own, 2), send(own, -2)
    up3, down3 = send(up2, 1), send(down2, -1)
    far_a, far_b = send(up2[:256], 2), send(down2[256:], -2)
    return [own, up1, down1, up2, down2, up3, down3, far_a, far_b]


def local(left_slab, right_window, left_pattern, right_pattern, square_blocks, result_pattern):
    packed = pack_right(right_window[0], right_pattern[0])
    packed = lax.all_gather(packed, "row", axis=0, tiled=False)
    parts = gather_left(mask_left(left_slab[0], left_pattern[0]))
    homes = packed[:, ROWS_MAIN, :EXTRA].astype(jnp.int32)
    right_high, right_low = unpack_right(packed, homes)
    me = lax.axis_index("col")
    where = jnp.stack([lax.rem(me + d, 8) for d in (8, 7, 9, 6, 10, 5, 11, 12)])
    cube = product(parts, where, right_high, right_low)
    terms = lax.all_to_all(cube.reshape(4, 128, 1024), "layer", 0, 0)
    layer = lax.axis_index("layer").reshape((1,))
    return finish(terms, square_blocks, result_pattern, layer)


def solution(mesh):
    in_specs = (
        P("layer", "row", "col"),
        P("layer", "row", "col"),
        P("layer", "row", "col"),
        P("layer", "row", "col"),
        P(("row", "layer"), "col"),
        P("row", "col"),
    )
    out_specs = P(("row", "layer"), "col")
    return jax.shard_map(local, mesh=mesh, in_specs=in_specs, out_specs=out_specs, check_vma=False)
```

time: 193 us -> 135 us (0.70)
  the two profiles are of different devices: /device:TPU:1 before, /device:TPU:8 now
where the time goes in v1:
time: 135 us; the launch traced here: 134 us
  waiting for transfers between devices  43.3 us (32%)
  starting transfers between devices  38.3 us (28%)
  Pallas kernels  31.5 us (23%)
  between operations  13.5 us (10%)
  local copies, waits for them, and re-layouts  6.38 us (5%)
  other arithmetic  1.44 us (1%)
    ppermute x8, starting transfers between devices, send(): return lax.ppermute(x, 'col', shift(8, by))  33.8 us
    all_to_all x1, waiting for transfers between devices, local(): terms = lax.all_to_all(cube.reshape(4, 128, 1024), 'layer', 0, 0)  25.5 us
    pallas_call x1, Pallas kernels, unpack_right(): pl.pallas_call(unpack_kernel, out_shape=(shape, shape), grid_spec=pltpu.P...  13.4 us
    ppermute x8, waiting for transfers between devices, send(): return lax.ppermute(x, 'col', shift(8, by))  13 us
    pallas_call x1, Pallas kernels, product(): pl.pallas_call(product_kernel, out_shape=jax.ShapeDtypeStruct((512, 1024)...  11.3 us
    all_gather x1, waiting for transfers between devices, local(): packed = lax.all_gather(packed, 'row', axis=0, tiled=False)  4.8 us
    all_to_all x1, starting transfers between devices, local(): terms = lax.all_to_all(cube.reshape(4, 128, 1024), 'layer', 0, 0)  4.46 us
    unnamed x6, local copies, waits for them, and re-layouts  3.51 us
  transfers between devices with their start and end apart: 10, of which 5 were waited for; matrix products, arithmetic and copies ran while one was open for 3% of the time, Pallas kernels for 11%

profile of v1, /device:TPU:8, one launch (start us, length us, event | category | flops | bytes accessed | tf_op | source)
XLA Modules:
  0.0 134.4 jit_solution(11693435391475654121)
XLA Ops:
  6.5 2.3 %shard_map.65 = f32[784,128]{1,0:T(8,128)} custom-call(s32[2,16]{1,0:T(2,128)} %bitcast.22, f32[128,1024]{1,0:T(8,128)} %bitcast.18), custom_call_target="tpu_custom_call" | custom-call | tf_op jit(solution)/shard_map/pallas_call | solution.py:81
  8.8 0.0 all-gather.3.cloned.1.call-update
  8.8 1.3 %copy.10.flags = s32[8,4]{1,0:T(8,128)} copy(s32[8,4]{0,1:T(4,128)} %bitcast.21) | data formatting | bytes 256 | tf_op jit(solution)/shard_map/squeeze | solution.py:208
  10.2 1.9 %shard_map.64.refs_0_ = f32[512,256]{1,0:T(8,128)} custom-call(s32[8,4]{1,0:T(8,128)} %copy.10.flags, f32[512,256]{1,0:T(8,128)} %bitcast.19), custom_call_target="tpu_custom_call" | custom-call | tf_op jit(solution)/shard_map/pallas_call | solution.py:35
  12.1 5.5 %collective-permute-start.3 = (f32[512,256]{1,0:T(8,128)}, f32[512,256]{1,0:T(8,128)S(1)}, u32[]{:S(2)}, u32[]{:S(2)}) collective-permute-start(f32[512,256]{1,0:T(8,128)} %shard_map.64.refs_0_), channel_id=1, source_target_pairs={{0,24},{4,28},{8,0},{12,4},{16,8},{20,12},{24,16},{28,20},{1,25},{... | collective-permute-start | bytes 1572872 | tf_op jit(solution)/shard_map/ppermute | solution.py:196
  17.5 1.9 %collective-permute-start.2 = (f32[512,256]{1,0:T(8,128)}, f32[512,256]{1,0:T(8,128)S(1)}, u32[]{:S(2)}, u32[]{:S(2)}) collective-permute-start(f32[512,256]{1,0:T(8,128)} %shard_map.64.refs_0_), channel_id=1, source_target_pairs={{0,8},{4,12},{8,16},{12,20},{16,24},{20,28},{24,0},{28,4},{1,9},{5... | collective-permute-start | bytes 1572872 | tf_op jit(solution)/shard_map/ppermute | solution.py:196
  19.5 7.4 %collective-permute-start.1 = (f32[512,256]{1,0:T(8,128)}, f32[512,256]{1,0:T(8,128)S(1)}, u32[]{:S(2)}, u32[]{:S(2)}) collective-permute-start(f32[512,256]{1,0:T(8,128)} %shard_map.64.refs_0_), channel_id=1, source_target_pairs={{0,28},{4,0},{8,4},{12,8},{16,12},{20,16},{24,20},{28,24},{1,29},{... | collective-permute-start | bytes 1572872 | tf_op jit(solution)/shard_map/ppermute | solution.py:196
  26.8 1.9 %collective-permute-start = (f32[512,256]{1,0:T(8,128)}, f32[512,256]{1,0:T(8,128)S(1)}, u32[]{:S(2)}, u32[]{:S(2)}) collective-permute-start(f32[512,256]{1,0:T(8,128)} %shard_map.64.refs_0_), channel_id=1, source_target_pairs={{0,4},{4,8},{8,12},{12,16},{16,20},{20,24},{24,28},{28,0},{1,5},{5... | collective-permute-start | bytes 1572872 | tf_op jit(solution)/shard_map/ppermute | solution.py:196
  28.8 10.2 %collective-permute-done.3.refs_4_ = f32[512,256]{1,0:T(8,128)S(1)} collective-permute-done((f32[512,256]{1,0:T(8,128)}, f32[512,256]{1,0:T(8,128)S(1)}, u32[]{:S(2)}, u32[]{:S(2)}) %collective-permute-start.3) | collective-permute-done | bytes 524320 | tf_op jit(solution)/shard_map/ppermute | solution.py:196
  39.0 6.1 %collective-permute-start.5 = (f32[512,256]{1,0:T(8,128)S(1)}, f32[512,256]{1,0:T(8,128)S(1)}, u32[]{:S(2)}, u32[]{:S(2)}) collective-permute-start(f32[512,256]{1,0:T(8,128)S(1)} %collective-permute-done.3.refs_4_), channel_id=1, source_target_pairs={{0,28},{4,0},{8,4},{12,8},{16,12},{20,16},{24,20},{28,24},{1,29},{... | collective-permute-start | bytes 1572872 | tf_op jit(solution)/shard_map/ppermute | solution.py:196
  45.1 1.7 %collective-permute-done.2.refs_3_ = f32[512,256]{1,0:T(8,128)S(1)} collective-permute-done((f32[512,256]{1,0:T(8,128)}, f32[512,256]{1,0:T(8,128)S(1)}, u32[]{:S(2)}, u32[]{:S(2)}) %collective-permute-start.2) | collective-permute-done | bytes 524320 | tf_op jit(solution)/shard_map/ppermute | solution.py:196
  46.8 4.3 %collective-permute-start.4 = (f32[512,256]{1,0:T(8,128)S(1)}, f32[512,256]{1,0:T(8,128)}, u32[]{:S(2)}, u32[]{:S(2)}) collective-permute-start(f32[512,256]{1,0:T(8,128)S(1)} %collective-permute-done.2.refs_3_), channel_id=1, source_target_pairs={{0,4},{4,8},{8,12},{12,16},{16,20},{20,24},{24,28},{28,0},{1,5},{5... | collective-permute-start | bytes 1572872 | tf_op jit(solution)/shard_map/ppermute | solution.py:196
  51.1 0.7 slice.13
  51.8 4.7 %collective-permute-start.7 = (f32[256,256]{1,0:T(8,128)}, f32[256,256]{1,0:T(8,128)S(1)}, u32[]{:S(2)}, u32[]{:S(2)}) collective-permute-start(f32[256,256]{1,0:T(8,128)} %slice.13), channel_id=1, source_target_pairs={{0,24},{4,28},{8,0},{12,4},{16,8},{20,12},{24,16},{28,20},{1,25},{... | collective-permute-start | bytes 786440 | tf_op jit(solution)/shard_map/ppermute | solution.py:196
  56.5 0.7 slice.12
  57.2 0.0 collective-permute-done.1.refs_2_
  57.2 2.0 %collective-permute-start.6 = (f32[256,256]{1,0:T(8,128)}, f32[256,256]{1,0:T(8,128)}, u32[]{:S(2)}, u32[]{:S(2)}) collective-permute-start(f32[256,256]{1,0:T(8,128)} %slice.12), channel_id=1, source_target_pairs={{0,8},{4,12},{8,16},{12,20},{16,24},{20,28},{24,0},{28,4},{1,9},{5... | collective-permute-start | bytes 786440 | tf_op jit(solution)/shard_map/ppermute | solution.py:196
  59.3 0.1 stack.35.where
  59.4 4.8 %all-gather.3.cloned.1.call-done = f32[12544,128]{1,0:T(8,128)} async-done(((f32[784,128]{1,0:T(8,128)}), f32[12544,128]{1,0:T(8,128)}) %all-gather.3.cloned.1.call-update) | async-done | bytes 6422544 | tf_op jit(solution)/shard_map/all_gather | solution.py:207
  64.2 1.4 %slice_convert_fusion = s32[16,1,8]{2,1,0:T(1,128)} fusion(f32[16,784,128]{2,1,0:T(8,128)} %bitcast.16), kind=kLoop, calls=%fused_computation | loop fusion | flops 128 | bytes 1024 | tf_op jit(solution)/shard_map/convert_element_type | solution.py:209
  65.6 13.4 %shard_map.66 = (bf16[2048,1024]{1,0:T(8,128)(2,1)}, bf16[2048,1024]{1,0:T(8,128)(2,1)}) custom-call(s32[16,8]{1,0:T(8,128)} %bitcast.20, f32[16,784,128]{2,1,0:T(8,128)} %bitcast.17), custom_call_target="tpu_custom_call" | custom-call | tf_op jit(solution)/shard_map/pallas_call | solution.py:124
  79.0 0.0 collective-permute-done.refs_1_
  79.0 0.0 collective-permute-done.7.refs_8_
  79.0 1.1 collective-permute-done.6.refs_7_
  80.1 0.0 collective-permute-done.5.refs_6_
  80.1 0.0 collective-permute-done.4.refs_5_
  80.1 2.2 %copy-done = bf16[2048,1024]{1,0:T(8,128)(2,1)S(1)} copy-done((bf16[2048,1024]{1,0:T(8,128)(2,1)S(1)}, bf16[2048,1024]{1,0:T(8,128)(2,1)}, u32[]{:S(2)}) %copy-start) | copy-done | bytes 4194328
  82.3 11.3 %shard_map.67 = f32[512,1024]{1,0:T(8,128)} custom-call(s32[8]{0:T(128)S(1)} %stack.35.where, f32[512,256]{1,0:T(8,128)S(1)} %copy-done.1, f32[512,256]{1,0:T(8,128)S(1)} %collective-permute-done.refs_1_, f32[512,256]{1,0:T(8,128)S(1)} %collective-permute-done.1.refs_2_, f32[512,256]{1,0:T(8,128)S(1)} %collective-permute-done.2.refs_3_, ...), custom_call_target="tpu_custom_call" | custom-call | tf_op jit(solution)/shard_map/pallas_call | solution.py:155
  93.6 4.5 %all-to-all-start = ((f32[4,128,1024]{2,1,0:T(8,128)}), f32[4,128,1024]{2,1,0:T(8,128)S(1)}, u32[]{:S(2)}, u32[]{:S(2)}) async-start(f32[4,128,1024]{2,1,0:T(8,128)} %bitcast.15), calls=%async_computation | async-start | bytes 4194304 | tf_op jit(solution)/shard_map/all_to_all | solution.py:214
  98.1 25.5 %all-to-all-done.terms = f32[4,128,1024]{2,1,0:T(8,128)S(1)} async-done(((f32[4,128,1024]{2,1,0:T(8,128)}), f32[4,128,1024]{2,1,0:T(8,128)S(1)}, u32[]{:S(2)}, u32[]{:S(2)}) %all-to-all-start) | async-done | bytes 2097184 | tf_op jit(solution)/shard_map/all_to_all | solution.py:214
  123.6 1.3 copy-done.2
  124.9 2.6 %shard_map.68 = f32[128,1024]{1,0:T(8,128)} custom-call(s32[1]{0:T(128)} %bitcast.where, s32[8,16]{1,0:T(8,128)} %flags.1, f32[4,128,1024]{2,1,0:T(8,128)} %copy-done.2, f32[128,1024]{1,0:T(8,128)} %square.1), custom_call_target="tpu_custom_call" | custom-call | tf_op jit(solution)/shard_map/pallas_call | solution.py:182
  (5 shorter events, 0.0 us)
Async XLA Ops:
  6.5 57.6 %all-gather.3.cloned.1.call-start = ((), (), s32[]{:S(2)}) async-start(), calls=%async_computation.1 | async-start | bytes 6823936 | tf_op jit(solution)/shard_map/all_gather | solution.py:207
  12.1 68.0 %copy-start.1 = (f32[512,256]{1,0:T(8,128)S(1)}, f32[512,256]{1,0:T(8,128)}, u32[]{:S(2)}) copy-start(f32[512,256]{1,0:T(8,128)} %shard_map.64.refs_0_) | copy-start | bytes 1572868
  12.1 26.9 %collective-permute-start.3 = (f32[512,256]{1,0:T(8,128)}, f32[512,256]{1,0:T(8,128)S(1)}, u32[]{:S(2)}, u32[]{:S(2)}) collective-permute-start(f32[512,256]{1,0:T(8,128)} %shard_map.64.refs_0_), channel_id=1, source_target_pairs={{0,24},{4,28},{8,0},{12,4},{16,8},{20,12},{24,16},{28,20},{1,25},{... | collective-permute-start | bytes 1572872 | tf_op jit(solution)/shard_map/ppermute | solution.py:196
  17.5 29.2 %collective-permute-start.2 = (f32[512,256]{1,0:T(8,128)}, f32[512,256]{1,0:T(8,128)S(1)}, u32[]{:S(2)}, u32[]{:S(2)}) collective-permute-start(f32[512,256]{1,0:T(8,128)} %shard_map.64.refs_0_), channel_id=1, source_target_pairs={{0,8},{4,12},{8,16},{12,20},{16,24},{20,28},{24,0},{28,4},{1,9},{5... | collective-permute-start | bytes 1572872 | tf_op jit(solution)/shard_map/ppermute | solution.py:196
  19.5 37.8 %collective-permute-start.1 = (f32[512,256]{1,0:T(8,128)}, f32[512,256]{1,0:T(8,128)S(1)}, u32[]{:S(2)}, u32[]{:S(2)}) collective-permute-start(f32[512,256]{1,0:T(8,128)} %shard_map.64.refs_0_), channel_id=1, source_target_pairs={{0,28},{4,0},{8,4},{12,8},{16,12},{20,16},{24,20},{28,24},{1,29},{... | collective-permute-start | bytes 1572872 | tf_op jit(solution)/shard_map/ppermute | solution.py:196
  26.8 52.2 %collective-permute-start = (f32[512,256]{1,0:T(8,128)}, f32[512,256]{1,0:T(8,128)S(1)}, u32[]{:S(2)}, u32[]{:S(2)}) collective-permute-start(f32[512,256]{1,0:T(8,128)} %shard_map.64.refs_0_), channel_id=1, source_target_pairs={{0,4},{4,8},{8,12},{12,16},{16,20},{20,24},{24,28},{28,0},{1,5},{5... | collective-permute-start | bytes 1572872 | tf_op jit(solution)/shard_map/ppermute | solution.py:196
  39.0 41.1 %collective-permute-start.5 = (f32[512,256]{1,0:T(8,128)S(1)}, f32[512,256]{1,0:T(8,128)S(1)}, u32[]{:S(2)}, u32[]{:S(2)}) collective-permute-start(f32[512,256]{1,0:T(8,128)S(1)} %collective-permute-done.3.refs_4_), channel_id=1, source_target_pairs={{0,28},{4,0},{8,4},{12,8},{16,12},{20,16},{24,20},{28,24},{1,29},{... | collective-permute-start | bytes 1572872 | tf_op jit(solution)/shard_map/ppermute | solution.py:196
  46.8 33.3 %collective-permute-start.4 = (f32[512,256]{1,0:T(8,128)S(1)}, f32[512,256]{1,0:T(8,128)}, u32[]{:S(2)}, u32[]{:S(2)}) collective-permute-start(f32[512,256]{1,0:T(8,128)S(1)} %collective-permute-done.2.refs_3_), channel_id=1, source_target_pairs={{0,4},{4,8},{8,12},{12,16},{16,20},{20,24},{24,28},{28,0},{1,5},{5... | collective-permute-start | bytes 1572872 | tf_op jit(solution)/shard_map/ppermute | solution.py:196
  51.8 27.2 %collective-permute-start.7 = (f32[256,256]{1,0:T(8,128)}, f32[256,256]{1,0:T(8,128)S(1)}, u32[]{:S(2)}, u32[]{:S(2)}) collective-permute-start(f32[256,256]{1,0:T(8,128)} %slice.13), channel_id=1, source_target_pairs={{0,24},{4,28},{8,0},{12,4},{16,8},{20,12},{24,16},{28,20},{1,25},{... | collective-permute-start | bytes 786440 | tf_op jit(solution)/shard_map/ppermute | solution.py:196
  57.2 22.9 %collective-permute-start.6 = (f32[256,256]{1,0:T(8,128)}, f32[256,256]{1,0:T(8,128)}, u32[]{:S(2)}, u32[]{:S(2)}) collective-permute-start(f32[256,256]{1,0:T(8,128)} %slice.12), channel_id=1, source_target_pairs={{0,8},{4,12},{8,16},{12,20},{16,24},{20,28},{24,0},{28,4},{1,9},{5... | collective-permute-start | bytes 786440 | tf_op jit(solution)/shard_map/ppermute | solution.py:196
  80.1 2.2 %copy-start = (bf16[2048,1024]{1,0:T(8,128)(2,1)S(1)}, bf16[2048,1024]{1,0:T(8,128)(2,1)}, u32[]{:S(2)}) copy-start(bf16[2048,1024]{1,0:T(8,128)(2,1)} %get-tuple-element.7.refs_9_) | copy-start | bytes 12582916
  93.6 29.9 %all-to-all-start = ((f32[4,128,1024]{2,1,0:T(8,128)}), f32[4,128,1024]{2,1,0:T(8,128)S(1)}, u32[]{:S(2)}, u32[]{:S(2)}) async-start(f32[4,128,1024]{2,1,0:T(8,128)} %bitcast.15), calls=%async_computation | async-start | bytes 4194304 | tf_op jit(solution)/shard_map/all_to_all | solution.py:214
  123.6 1.3 copy-start.2
Sparse Core Ops, SparseCore 0:
  9.5 54.6 all-gather.2

commit v2 on v0

v2 whole, which is shorter than its diff:
```python
import functools

import jax
import jax.numpy as jnp
from jax import lax
from jax.experimental import pallas as pl
from jax.experimental.pallas import tpu as pltpu
from jax.sharding import PartitionSpec as P

BS = 64
LANES = 128
MAIN = 24
EXTRA = 8
META = 16
PACKED = META + 6 * LANES
BF = jnp.bfloat16
F32 = jnp.float32


def lane_half():
    return lax.broadcasted_iota(jnp.int32, (BS, LANES), 1) // BS


def pair_mask(low, high):
    return jnp.where(lane_half() == 0, low.astype(F32), high.astype(F32))


def mask_left_kernel(flags, x, out):
    for i in range(8):
        for c in range(2):
            mask = pair_mask(flags[2 * c, i], flags[2 * c + 1, i])
            at = (pl.ds(i * BS, BS), pl.ds(c * LANES, LANES))
            out[at] = x[at] * mask


def mask_left(x, flags):
    return pl.pallas_call(
        mask_left_kernel,
        out_shape=jax.ShapeDtypeStruct(x.shape, F32),
        in_specs=[pl.BlockSpec(memory_space=pltpu.SMEM), pl.BlockSpec(memory_space=pltpu.VMEM)],
        out_specs=pl.BlockSpec(memory_space=pltpu.VMEM),
    )(flags, x)


def pack_kernel(flags, x, out, holes):
    for c in range(6):
        out[pl.ds(META + c * LANES, LANES), :] = x[:, pl.ds(c * LANES, LANES)]
    count = jnp.int32(0)
    for s in range(MAIN):
        holes[count] = s
        count = count + jnp.where(flags[(s >> 1) & 1, 2 * (s >> 2) + (s & 1)] == 0, 1, 0)
    used = jnp.int32(0)
    half = lane_half()
    lane = lax.broadcasted_iota(jnp.int32, (1, LANES), 1)
    row = jnp.zeros((1, LANES), F32)
    for e in range(EXTRA):
        kept = flags[e >> 2, 12 + (e & 3)] != 0
        slot = holes[jnp.minimum(used, EXTRA)]
        row = jnp.where(lane == e, jnp.where(kept, slot, -1).astype(F32), row)
        used = used + jnp.where(kept, 1, 0)

        @pl.when(kept)
        def _():
            at = pl.ds(pl.multiple_of(META + (slot >> 1) * BS, 16), BS)
            block = x[pl.ds((e >> 2) * BS, BS), pl.ds((6 + ((e >> 1) & 1)) * LANES, LANES)]
            side = slot & 1
            block = jnp.where(side == (e & 1), block, pltpu.roll(block, BS, 1))
            out[at, :] = jnp.where(half == side, block, out[at, :])

    out[pl.ds(0, 1), :] = row
    for c in range(6):
        for b in range(2):
            mask = jnp.where(lane < BS, flags[b, 2 * c].astype(F32), flags[b, 2 * c + 1].astype(F32))
            out[pl.ds(1 + c * 2 + b, 1), :] = mask
    out[pl.ds(13, 3), :] = jnp.zeros((3, LANES), F32)


def pack_right(x, flags):
    return pl.pallas_call(
        pack_kernel,
        out_shape=jax.ShapeDtypeStruct((PACKED, LANES), F32),
        in_specs=[pl.BlockSpec(memory_space=pltpu.SMEM), pl.BlockSpec(memory_space=pltpu.VMEM)],
        out_specs=pl.BlockSpec(memory_space=pltpu.VMEM),
        scratch_shapes=[pltpu.SMEM((MAIN + 1,), jnp.int32)],
    )(flags, x)


def split(x):
    high = x.astype(BF)
    return high, (x - high.astype(F32)).astype(BF)


def product_kernel(side, where, packed, *refs):
    parts, (out, tiles, lefts, high0, high1, low0, low1, homes, tile_sems, left_sems, home_sem) = refs[:9], refs[9:]
    need = tiles.shape[2]
    copies = []
    if side:
        home_copy = pltpu.make_async_copy(packed.at[:, pl.ds(0, 8), :], homes, home_sem)
        home_copy.start()
    for k in range(8):
        tile = pltpu.make_async_copy(packed.at[pl.ds(where[k] * 2, 2), pl.ds(0, need), :], tiles.at[k], tile_sems.at[k])
        tile.start()
        if k < 7:
            pieces = [pltpu.make_async_copy(parts[k], lefts.at[k], left_sems.at[k])]
        else:
            pieces = [
                pltpu.make_async_copy(parts[7 + h], lefts.at[7, pl.ds(h * 256, 256)], left_sems.at[7 + h]) for h in range(2)
            ]
        for piece in pieces:
            piece.start()
        copies.append([tile] + pieces)
    half = lane_half()
    if side:
        home_copy.wait()

    def unpack(k):
        high, low = (high0, low0) if k % 2 == 0 else (high1, low1)
        for z in range(2):
            for b in range(2):
                for c in range(4):
                    pair = 4 * side + c
                    if pair < 6:
                        mask = tiles[k, z, pl.ds(1 + pair * 2 + b, 1), :]
                        value = tiles[k, z, pl.ds(META + pair * LANES + b * BS, BS), :] * mask
                    else:
                        halves = []
                        for h in range(2):
                            slot = homes[where[k] * 2 + z, 0, b * 4 + 2 * (pair - 6) + h].astype(jnp.int32)
                            kept = slot >= 0
                            slot = jnp.maximum(slot, 0)
                            block = tiles[k, z, pl.ds(pl.multiple_of(META + (slot >> 1) * BS, 16), BS), :]
                            block = jnp.where((slot & 1) == h, block, pltpu.roll(block, BS, 1))
                            halves.append(jnp.where(kept, block, 0.0))
                        value = jnp.where(half == 0, halves[0], halves[1])
                    at = (pl.ds(z * LANES + b * BS, BS), pl.ds(c * LANES, LANES))
                    high[at], low[at] = split(value)
        return high, low

    for k in range(8):
        for copy in copies[k]:
            copy.wait()
        high, low = unpack(k)
        left_high, left_low = split(lefts[k])
        total = jnp.dot(left_low, high[...], preferred_element_type=F32)
        total += jnp.dot(left_high, low[...], preferred_element_type=F32)
        total += jnp.dot(left_high, high[...], preferred_element_type=F32)
        if k:
            total += out[...]
        out[...] = total


def product(side, parts, where, packed):
    smem = pl.BlockSpec(memory_space=pltpu.SMEM)
    hbm = pl.BlockSpec(memory_space=pltpu.HBM)
    need = PACKED if side else META + 4 * LANES
    return pl.pallas_call(
        functools.partial(product_kernel, side),
        out_shape=jax.ShapeDtypeStruct((512, 512), F32),
        in_specs=[smem] + [hbm] * 10,
        out_specs=pl.BlockSpec(memory_space=pltpu.VMEM),
        scratch_shapes=[
            pltpu.VMEM((8, 2, need, LANES), F32),
            pltpu.VMEM((8, 512, 256), F32),
            pltpu.VMEM((256, 512), BF),
            pltpu.VMEM((256, 512), BF),
            pltpu.VMEM((256, 512), BF),
            pltpu.VMEM((256, 512), BF),
            pltpu.SMEM((16, 8, LANES), F32),
            pltpu.SemaphoreType.DMA((8,)),
            pltpu.SemaphoreType.DMA((9,)),
            pltpu.SemaphoreType.DMA,
        ],
        cost_estimate=pl.CostEstimate(flops=6 * 512 * 512 * 2048, bytes_accessed=9 << 20, transcendentals=0),
        compiler_params=pltpu.CompilerParams(vmem_limit_bytes=56 << 20),
    )(where, packed, *parts)


def finish_kernel(side, where, flags, terms, square, *refs):
    out = refs[-1]
    for b in range(2):
        for c in range(4):
            at = (pl.ds(b * BS, BS), pl.ds(c * LANES, LANES))
            total = (terms[(0,) + at] + terms[(1,) + at]) + (terms[(2,) + at] + terms[(3,) + at])
            line, column = where[0] * 2 + b, 8 * side + 2 * c
            mask = pair_mask(flags[line, column], flags[line, column + 1])
            out[at] = mask * (3.0 * square[at] - 2.0 * total)


def finish(side, terms, square, flags, where, *before):
    smem = pl.BlockSpec(memory_space=pltpu.SMEM)
    half = pl.BlockSpec((128, 512), lambda i: (0, side))
    return pl.pallas_call(
        functools.partial(finish_kernel, side),
        out_shape=jax.ShapeDtypeStruct(square.shape, F32),
        grid=(1,),
        in_specs=[smem, smem, pl.BlockSpec((4, 128, 512), lambda i: (0, 0, 0)), half]
        + [pl.BlockSpec(memory_space=pltpu.HBM)] * len(before),
        out_specs=half,
        input_output_aliases={4: 0} if before else {},
        cost_estimate=pl.CostEstimate(flops=1 << 20, bytes_accessed=2 << 20, transcendentals=0),
    )(where, flags, terms, square, *before)


def shift(n, by):
    return [(i, (i + by) % n) for i in range(n)]


def gather_left(own):
    def send(x, by):
        return lax.ppermute(x, "col", shift(8, by))

    up1, down1 = send(own, 1), send(own, -1)
    up2, down2 = send(own, 2), send(own, -2)
    up3, down3 = send(up2, 1), send(down2, -1)
    far_a, far_b = send(up2[:256], 2), send(down2[256:], -2)
    return [own, up1, down1, up2, down2, up3, down3, far_a, far_b]


def local(left_slab, right_window, left_pattern, right_pattern, square_blocks, result_pattern):
    packed = pack_right(right_window[0], right_pattern[0])
    packed = lax.all_gather(packed, "row", axis=0, tiled=False)
    parts = gather_left(mask_left(left_slab[0], left_pattern[0].T))
    me = lax.axis_index("col")
    where = lax.rem(me + jnp.array([8, 7, 9, 6, 10, 5, 11, 12], jnp.int32), 8)
    layer = lax.axis_index("layer").reshape((1,))
    out = ()
    for side in range(2):
        cube = product(side, parts, where, packed)
        terms = lax.all_to_all(cube.reshape(4, 128, 512), "layer", 0, 0)
        out = (finish(side, terms, square_blocks, result_pattern, layer, *out),)
    return out[0]


def solution(mesh):
    in_specs = (
        P("layer", "row", "col"),
        P("layer", "row", "col"),
        P("layer", "row", "col"),
        P("layer", "row", "col"),
        P(("row", "layer"), "col"),
        P("row", "col"),
    )
    out_specs = P(("row", "layer"), "col")
    return jax.shard_map(local, mesh=mesh, in_specs=in_specs, out_specs=out_specs, check_vma=False)
```

time: 193 us -> 134 us (0.69)
  the two profiles are of different devices: /device:TPU:1 before, /device:TPU:8 now
where the time goes in v2:
time: 134 us; the launch traced here: 133 us
  waiting for transfers between devices  49.2 us (37%)
  starting transfers between devices  41.5 us (31%)
  Pallas kernels  25.6 us (19%)
  between operations  13.6 us (10%)
  local copies, waits for them, and re-layouts  1.77 us (1%)
    ppermute x8, starting transfers between devices, send(): return lax.ppermute(x, 'col', shift(8, by))  33.5 us
    ppermute x8, waiting for transfers between devices, send(): return lax.ppermute(x, 'col', shift(8, by))  32.9 us
    pallas_call x2, Pallas kernels, product(): pl.pallas_call(functools.partial(product_kernel, side), out_shape=jax.Sha...  17.2 us
    all_to_all x2, waiting for transfers between devices, local(): terms = lax.all_to_all(cube.reshape(4, 128, 512), 'layer', 0, 0)  16.3 us
    all_to_all x2, starting transfers between devices, local(): terms = lax.all_to_all(cube.reshape(4, 128, 512), 'layer', 0, 0)  7.97 us
    pallas_call x2, Pallas kernels, finish(): pl.pallas_call(functools.partial(finish_kernel, side), out_shape=jax.Shap...  4.14 us
  transfers between devices with their start and end apart: 11, of which 6 were waited for; matrix products, arithmetic and copies ran while one was open for 1% of the time, Pallas kernels for 10%

profile of v2, /device:TPU:8, one launch (start us, length us, event | category | flops | bytes accessed | tf_op | source)
XLA Modules:
  0.0 132.9 jit_solution(9772390671731167454)
XLA Ops:
  6.5 2.3 %shard_map.73 = f32[784,128]{1,0:T(8,128)} custom-call(s32[2,16]{1,0:T(2,128)} %bitcast.15, f32[128,1024]{1,0:T(8,128)} %bitcast.12), custom_call_target="tpu_custom_call" | custom-call | tf_op jit(solution)/shard_map/pallas_call | solution.py:79
  8.9 0.0 all-gather.3.cloned.1.call-update
  8.9 1.9 %shard_map.74.refs_0_ = f32[512,256]{1,0:T(8,128)} custom-call(s32[4,8]{1,0:T(4,128)} %bitcast.14, f32[512,256]{1,0:T(8,128)} %bitcast.13), custom_call_target="tpu_custom_call" | custom-call | tf_op jit(solution)/shard_map/pallas_call | solution.py:37
  10.8 5.3 %collective-permute-start.3 = (f32[512,256]{1,0:T(8,128)}, f32[512,256]{1,0:T(8,128)S(1)}, u32[]{:S(2)}, u32[]{:S(2)}) collective-permute-start(f32[512,256]{1,0:T(8,128)} %shard_map.74.refs_0_), channel_id=1, source_target_pairs={{0,24},{4,28},{8,0},{12,4},{16,8},{20,12},{24,16},{28,20},{1,25},{... | collective-permute-start | bytes 1572872 | tf_op jit(solution)/shard_map/ppermute | solution.py:210
  16.1 1.9 %collective-permute-start.2 = (f32[512,256]{1,0:T(8,128)}, f32[512,256]{1,0:T(8,128)S(1)}, u32[]{:S(2)}, u32[]{:S(2)}) collective-permute-start(f32[512,256]{1,0:T(8,128)} %shard_map.74.refs_0_), channel_id=1, source_target_pairs={{0,8},{4,12},{8,16},{12,20},{16,24},{20,28},{24,0},{28,4},{1,9},{5... | collective-permute-start | bytes 1572872 | tf_op jit(solution)/shard_map/ppermute | solution.py:210
  18.1 7.1 %collective-permute-start.1 = (f32[512,256]{1,0:T(8,128)}, f32[512,256]{1,0:T(8,128)S(1)}, u32[]{:S(2)}, u32[]{:S(2)}) collective-permute-start(f32[512,256]{1,0:T(8,128)} %shard_map.74.refs_0_), channel_id=1, source_target_pairs={{0,28},{4,0},{8,4},{12,8},{16,12},{20,16},{24,20},{28,24},{1,29},{... | collective-permute-start | bytes 1572872 | tf_op jit(solution)/shard_map/ppermute | solution.py:210
  25.2 1.9 %collective-permute-start = (f32[512,256]{1,0:T(8,128)}, f32[512,256]{1,0:T(8,128)S(1)}, u32[]{:S(2)}, u32[]{:S(2)}) collective-permute-start(f32[512,256]{1,0:T(8,128)} %shard_map.74.refs_0_), channel_id=1, source_target_pairs={{0,4},{4,8},{8,12},{12,16},{16,20},{20,24},{24,28},{28,0},{1,5},{5... | collective-permute-start | bytes 1572872 | tf_op jit(solution)/shard_map/ppermute | solution.py:210
  27.1 10.5 %collective-permute-done.3.refs_4_ = f32[512,256]{1,0:T(8,128)S(1)} collective-permute-done((f32[512,256]{1,0:T(8,128)}, f32[512,256]{1,0:T(8,128)S(1)}, u32[]{:S(2)}, u32[]{:S(2)}) %collective-permute-start.3) | collective-permute-done | bytes 524320 | tf_op jit(solution)/shard_map/ppermute | solution.py:210
  37.6 6.0 %collective-permute-start.5 = (f32[512,256]{1,0:T(8,128)S(1)}, f32[512,256]{1,0:T(8,128)S(1)}, u32[]{:S(2)}, u32[]{:S(2)}) collective-permute-start(f32[512,256]{1,0:T(8,128)S(1)} %collective-permute-done.3.refs_4_), channel_id=1, source_target_pairs={{0,28},{4,0},{8,4},{12,8},{16,12},{20,16},{24,20},{28,24},{1,29},{... | collective-permute-start | bytes 1572872 | tf_op jit(solution)/shard_map/ppermute | solution.py:210
  43.6 1.5 %collective-permute-done.2.refs_3_ = f32[512,256]{1,0:T(8,128)S(1)} collective-permute-done((f32[512,256]{1,0:T(8,128)}, f32[512,256]{1,0:T(8,128)S(1)}, u32[]{:S(2)}, u32[]{:S(2)}) %collective-permute-start.2) | collective-permute-done | bytes 524320 | tf_op jit(solution)/shard_map/ppermute | solution.py:210
  45.2 4.5 %collective-permute-start.4 = (f32[512,256]{1,0:T(8,128)S(1)}, f32[512,256]{1,0:T(8,128)}, u32[]{:S(2)}, u32[]{:S(2)}) collective-permute-start(f32[512,256]{1,0:T(8,128)S(1)} %collective-permute-done.2.refs_3_), channel_id=1, source_target_pairs={{0,4},{4,8},{8,12},{12,16},{16,20},{20,24},{24,28},{28,0},{1,5},{5... | collective-permute-start | bytes 1572872 | tf_op jit(solution)/shard_map/ppermute | solution.py:210
  49.7 4.7 %collective-permute-start.7 = (f32[256,256]{1,0:T(8,128)S(1)}, f32[256,256]{1,0:T(8,128)S(1)}, u32[]{:S(2)}, u32[]{:S(2)}) collective-permute-start(f32[256,256]{1,0:T(8,128)S(1)} %slice.9), channel_id=1, source_target_pairs={{0,24},{4,28},{8,0},{12,4},{16,8},{20,12},{24,16},{28,20},{1,25},{... | collective-permute-start | bytes 786440 | tf_op jit(solution)/shard_map/ppermute | solution.py:210
  54.4 0.0 collective-permute-done.1.refs_2_
  54.4 0.0 copy-start.4
  54.4 2.1 %collective-permute-start.6 = (f32[256,256]{1,0:T(8,128)S(1)}, f32[256,256]{1,0:T(8,128)}, u32[]{:S(2)}, u32[]{:S(2)}) collective-permute-start(f32[256,256]{1,0:T(8,128)S(1)} %slice.8), channel_id=1, source_target_pairs={{0,8},{4,12},{8,16},{12,20},{16,24},{20,28},{24,0},{28,4},{1,9},{5... | collective-permute-start | bytes 786440 | tf_op jit(solution)/shard_map/ppermute | solution.py:210
  56.5 1.2 compare_select_fusion.where
  57.7 0.0 collective-permute-done.refs_1_
  57.7 13.4 %collective-permute-done.7.refs_8_ = f32[256,256]{1,0:T(8,128)S(1)} collective-permute-done((f32[256,256]{1,0:T(8,128)S(1)}, f32[256,256]{1,0:T(8,128)S(1)}, u32[]{:S(2)}, u32[]{:S(2)}) %collective-permute-start.7) | collective-permute-done | bytes 262176 | tf_op jit(solution)/shard_map/ppermute | solution.py:210
  71.1 7.5 %collective-permute-done.6.refs_7_ = f32[256,256]{1,0:T(8,128)} collective-permute-done((f32[256,256]{1,0:T(8,128)S(1)}, f32[256,256]{1,0:T(8,128)}, u32[]{:S(2)}, u32[]{:S(2)}) %collective-permute-start.6) | collective-permute-done | bytes 262176 | tf_op jit(solution)/shard_map/ppermute | solution.py:210
  78.6 0.0 collective-permute-done.5.refs_6_
  78.6 0.0 collective-permute-done.4.refs_5_
  78.6 0.0 all-gather.3.cloned.1.call-done
  78.7 0.7 copy-done.6
  79.4 7.9 %shard_map.76 = f32[512,512]{1,0:T(8,128)} custom-call(s32[8]{0:T(128)} %compare_select_fusion.where, f32[16,784,128]{2,1,0:T(8,128)} %bitcast.16, f32[512,256]{1,0:T(8,128)} %shard_map.74.refs_0_, f32[512,256]{1,0:T(8,128)} %copy-done.5, f32[512,256]{1,0:T(8,128)} %copy-done.4, f32[512,256]{1,0:T(8,128)} %copy-done.3, f32[512,256]{1,0:T(8,128)} %copy-done.2, ...), custom_call_target="tpu_custom_call" | custom-call | flops 3221225472 | bytes 9437184 | tf_op jit(solution)/shard_map/pallas_call | solution.py:156
  87.3 4.5 %all-to-all-start.1 = ((f32[4,128,512]{2,1,0:T(8,128)}), f32[4,128,512]{2,1,0:T(8,128)S(1)}, u32[]{:S(2)}, u32[]{:S(2)}) async-start(f32[4,128,512]{2,1,0:T(8,128)} %bitcast.11), calls=%async_computation.1 | async-start | bytes 2097152 | tf_op jit(solution)/shard_map/all_to_all | solution.py:229
  91.8 9.3 %shard_map.75 = f32[512,512]{1,0:T(8,128)} custom-call(s32[8]{0:T(128)} %compare_select_fusion.where, f32[16,784,128]{2,1,0:T(8,128)} %bitcast.17, f32[512,256]{1,0:T(8,128)} %shard_map.74.refs_0_, f32[512,256]{1,0:T(8,128)} %copy-done.5, f32[512,256]{1,0:T(8,128)} %copy-done.4, f32[512,256]{1,0:T(8,128)} %copy-done.3, f32[512,256]{1,0:T(8,128)} %copy-done.2, ...), custom_call_target="tpu_custom_call" | custom-call | flops 3221225472 | bytes 9437184 | tf_op jit(solution)/shard_map/pallas_call | solution.py:156
  101.1 5.0 %all-to-all-done.1.terms = f32[4,128,512]{2,1,0:T(8,128)S(1)} async-done(((f32[4,128,512]{2,1,0:T(8,128)}), f32[4,128,512]{2,1,0:T(8,128)S(1)}, u32[]{:S(2)}, u32[]{:S(2)}) %all-to-all-start.1) | async-done | bytes 1048608 | tf_op jit(solution)/shard_map/all_to_all | solution.py:229
  106.1 3.5 %all-to-all-start = ((f32[4,128,512]{2,1,0:T(8,128)}), f32[4,128,512]{2,1,0:T(8,128)S(1)}, u32[]{:S(2)}, u32[]{:S(2)}) async-start(f32[4,128,512]{2,1,0:T(8,128)} %bitcast.10), calls=%async_computation | async-start | bytes 2097152 | tf_op jit(solution)/shard_map/all_to_all | solution.py:229
  109.7 2.1 %shard_map.77.refs_0_ = f32[128,1024]{1,0:T(8,128)} custom-call(s32[1]{0:T(128)} %bitcast.where, s32[8,16]{1,0:T(8,128)} %flags.3, f32[4,128,512]{2,1,0:T(8,128)} %copy-done, f32[128,1024]{1,0:T(8,128)} %square.3), custom_call_target="tpu_custom_call" | custom-call | flops 1048576 | bytes 2097152 | tf_op jit(solution)/shard_map/pallas_call | solution.py:192
  111.7 11.3 %all-to-all-done.terms = f32[4,128,512]{2,1,0:T(8,128)S(1)} async-done(((f32[4,128,512]{2,1,0:T(8,128)}), f32[4,128,512]{2,1,0:T(8,128)S(1)}, u32[]{:S(2)}, u32[]{:S(2)}) %all-to-all-start) | async-done | bytes 1048608 | tf_op jit(solution)/shard_map/all_to_all | solution.py:229
  123.0 1.0 copy-done.1
  124.0 2.1 %shard_map.78 = f32[128,1024]{1,0:T(8,128)} custom-call(s32[1]{0:T(128)} %bitcast.where, s32[8,16]{1,0:T(8,128)} %flags.3, f32[4,128,512]{2,1,0:T(8,128)} %copy-done.1, f32[128,1024]{1,0:T(8,128)} %square.3, f32[128,1024]{1,0:T(8,128)} %shard_map.77.refs_0_), custom_call_target="tpu_custom_call", output_to_operand_aliasing={{}: (4, {})} | custom-call | flops 1048576 | bytes 2097152 | tf_op jit(solution)/shard_map/pallas_call | solution.py:192
  (16 shorter events, 0.1 us)
Async XLA Ops:
  6.5 72.1 %all-gather.3.cloned.1.call-start = ((), (), s32[]{:S(2)}) async-start(), calls=%async_computation.2 | async-start | bytes 6823936 | tf_op jit(solution)/shard_map/all_gather | solution.py:221
  10.8 26.8 %collective-permute-start.3 = (f32[512,256]{1,0:T(8,128)}, f32[512,256]{1,0:T(8,128)S(1)}, u32[]{:S(2)}, u32[]{:S(2)}) collective-permute-start(f32[512,256]{1,0:T(8,128)} %shard_map.74.refs_0_), channel_id=1, source_target_pairs={{0,24},{4,28},{8,0},{12,4},{16,8},{20,12},{24,16},{28,20},{1,25},{... | collective-permute-start | bytes 1572872 | tf_op jit(solution)/shard_map/ppermute | solution.py:210
  16.1 29.0 %collective-permute-start.2 = (f32[512,256]{1,0:T(8,128)}, f32[512,256]{1,0:T(8,128)S(1)}, u32[]{:S(2)}, u32[]{:S(2)}) collective-permute-start(f32[512,256]{1,0:T(8,128)} %shard_map.74.refs_0_), channel_id=1, source_target_pairs={{0,8},{4,12},{8,16},{12,20},{16,24},{20,28},{24,0},{28,4},{1,9},{5... | collective-permute-start | bytes 1572872 | tf_op jit(solution)/shard_map/ppermute | solution.py:210
  18.1 36.3 %collective-permute-start.1 = (f32[512,256]{1,0:T(8,128)}, f32[512,256]{1,0:T(8,128)S(1)}, u32[]{:S(2)}, u32[]{:S(2)}) collective-permute-start(f32[512,256]{1,0:T(8,128)} %shard_map.74.refs_0_), channel_id=1, source_target_pairs={{0,28},{4,0},{8,4},{12,8},{16,12},{20,16},{24,20},{28,24},{1,29},{... | collective-permute-start | bytes 1572872 | tf_op jit(solution)/shard_map/ppermute | solution.py:210
  25.2 32.5 %collective-permute-start = (f32[512,256]{1,0:T(8,128)}, f32[512,256]{1,0:T(8,128)S(1)}, u32[]{:S(2)}, u32[]{:S(2)}) collective-permute-start(f32[512,256]{1,0:T(8,128)} %shard_map.74.refs_0_), channel_id=1, source_target_pairs={{0,4},{4,8},{8,12},{12,16},{16,20},{20,24},{24,28},{28,0},{1,5},{5... | collective-permute-start | bytes 1572872 | tf_op jit(solution)/shard_map/ppermute | solution.py:210
  37.6 41.1 %copy-start.2 = (f32[512,256]{1,0:T(8,128)}, f32[512,256]{1,0:T(8,128)S(1)}, u32[]{:S(2)}) copy-start(f32[512,256]{1,0:T(8,128)S(1)} %collective-permute-done.3.refs_4_) | copy-start | bytes 1572868
  37.6 41.0 %collective-permute-start.5 = (f32[512,256]{1,0:T(8,128)S(1)}, f32[512,256]{1,0:T(8,128)S(1)}, u32[]{:S(2)}, u32[]{:S(2)}) collective-permute-start(f32[512,256]{1,0:T(8,128)S(1)} %collective-permute-done.3.refs_4_), channel_id=1, source_target_pairs={{0,28},{4,0},{8,4},{12,8},{16,12},{20,16},{24,20},{28,24},{1,29},{... | collective-permute-start | bytes 1572872 | tf_op jit(solution)/shard_map/ppermute | solution.py:210
  45.2 33.5 %copy-start.3 = (f32[512,256]{1,0:T(8,128)}, f32[512,256]{1,0:T(8,128)S(1)}, u32[]{:S(2)}) copy-start(f32[512,256]{1,0:T(8,128)S(1)} %collective-permute-done.2.refs_3_) | copy-start | bytes 1572868
  45.2 33.5 %collective-permute-start.4 = (f32[512,256]{1,0:T(8,128)S(1)}, f32[512,256]{1,0:T(8,128)}, u32[]{:S(2)}, u32[]{:S(2)}) collective-permute-start(f32[512,256]{1,0:T(8,128)S(1)} %collective-permute-done.2.refs_3_), channel_id=1, source_target_pairs={{0,4},{4,8},{8,12},{12,16},{16,20},{20,24},{24,28},{28,0},{1,5},{5... | collective-permute-start | bytes 1572872 | tf_op jit(solution)/shard_map/ppermute | solution.py:210
  49.7 21.5 %collective-permute-start.7 = (f32[256,256]{1,0:T(8,128)S(1)}, f32[256,256]{1,0:T(8,128)S(1)}, u32[]{:S(2)}, u32[]{:S(2)}) collective-permute-start(f32[256,256]{1,0:T(8,128)S(1)} %slice.9), channel_id=1, source_target_pairs={{0,24},{4,28},{8,0},{12,4},{16,8},{20,12},{24,16},{28,20},{1,25},{... | collective-permute-start | bytes 786440 | tf_op jit(solution)/shard_map/ppermute | solution.py:210
  54.4 24.3 %copy-start.4 = (f32[512,256]{1,0:T(8,128)}, f32[512,256]{1,0:T(8,128)S(1)}, u32[]{:S(2)}) copy-start(f32[512,256]{1,0:T(8,128)S(1)} %collective-permute-done.1.refs_2_) | copy-start | bytes 1572868
  54.4 24.2 %collective-permute-start.6 = (f32[256,256]{1,0:T(8,128)S(1)}, f32[256,256]{1,0:T(8,128)}, u32[]{:S(2)}, u32[]{:S(2)}) collective-permute-start(f32[256,256]{1,0:T(8,128)S(1)} %slice.8), channel_id=1, source_target_pairs={{0,8},{4,12},{8,16},{12,20},{16,24},{20,28},{24,0},{28,4},{1,9},{5... | collective-permute-start | bytes 786440 | tf_op jit(solution)/shard_map/ppermute | solution.py:210
  57.7 21.0 %copy-start.5 = (f32[512,256]{1,0:T(8,128)}, f32[512,256]{1,0:T(8,128)S(1)}, u32[]{:S(2)}) copy-start(f32[512,256]{1,0:T(8,128)S(1)} %collective-permute-done.refs_1_) | copy-start | bytes 1572868
  71.1 7.6 %copy-start.7 = (f32[256,256]{1,0:T(8,128)}, f32[256,256]{1,0:T(8,128)S(1)}, u32[]{:S(2)}) copy-start(f32[256,256]{1,0:T(8,128)S(1)} %collective-permute-done.7.refs_8_) | copy-start | bytes 786436
  78.6 0.8 copy-start.6
  87.3 18.8 %all-to-all-start.1 = ((f32[4,128,512]{2,1,0:T(8,128)}), f32[4,128,512]{2,1,0:T(8,128)S(1)}, u32[]{:S(2)}, u32[]{:S(2)}) async-start(f32[4,128,512]{2,1,0:T(8,128)} %bitcast.11), calls=%async_computation.1 | async-start | bytes 2097152 | tf_op jit(solution)/shard_map/all_to_all | solution.py:229
  106.1 3.5 %copy-start = (f32[4,128,512]{2,1,0:T(8,128)}, f32[4,128,512]{2,1,0:T(8,128)S(1)}, u32[]{:S(2)}) copy-start(f32[4,128,512]{2,1,0:T(8,128)S(1)} %all-to-all-done.1.terms) | copy-start | bytes 3145732
  106.1 16.9 %all-to-all-start = ((f32[4,128,512]{2,1,0:T(8,128)}), f32[4,128,512]{2,1,0:T(8,128)S(1)}, u32[]{:S(2)}, u32[]{:S(2)}) async-start(f32[4,128,512]{2,1,0:T(8,128)} %bitcast.10), calls=%async_computation | async-start | bytes 2097152 | tf_op jit(solution)/shard_map/all_to_all | solution.py:229
  123.0 1.0 copy-start.1
Sparse Core Ops, SparseCore 0:
  9.5 54.6 all-gather.2

commit v3 on v2

--- a/solution.py
+++ b/solution.py
@@ -25,24 +25,12 @@
     return jnp.where(lane_half() == 0, low.astype(F32), high.astype(F32))
 
 
-def mask_left_kernel(flags, x, out):
+def prepare_kernel(left_flags, left, flags, x, left_out, out, holes):
     for i in range(8):
         for c in range(2):
-            mask = pair_mask(flags[2 * c, i], flags[2 * c + 1, i])
+            mask = pair_mask(left_flags[2 * c, i], left_flags[2 * c + 1, i])
             at = (pl.ds(i * BS, BS), pl.ds(c * LANES, LANES))
-            out[at] = x[at] * mask
-
-
-def mask_left(x, flags):
-    return pl.pallas_call(
-        mask_left_kernel,
-        out_shape=jax.ShapeDtypeStruct(x.shape, F32),
-        in_specs=[pl.BlockSpec(memory_space=pltpu.SMEM), pl.BlockSpec(memory_space=pltpu.VMEM)],
-        out_specs=pl.BlockSpec(memory_space=pltpu.VMEM),
-    )(flags, x)
-
-
-def pack_kernel(flags, x, out, holes):
+            left_out[at] = left[at] * mask
     for c in range(6):
         out[pl.ds(META + c * LANES, LANES), :] = x[:, pl.ds(c * LANES, LANES)]
     count = jnp.int32(0)
@@ -75,14 +63,16 @@
     out[pl.ds(13, 3), :] = jnp.zeros((3, LANES), F32)
 
 
-def pack_right(x, flags):
+def prepare(left, left_flags, right, right_flags):
+    smem = pl.BlockSpec(memory_space=pltpu.SMEM)
+    vmem = pl.BlockSpec(memory_space=pltpu.VMEM)
     return pl.pallas_call(
-        pack_kernel,
-        out_shape=jax.ShapeDtypeStruct((PACKED, LANES), F32),
-        in_specs=[pl.BlockSpec(memory_space=pltpu.SMEM), pl.BlockSpec(memory_space=pltpu.VMEM)],
-        out_specs=pl.BlockSpec(memory_space=pltpu.VMEM),
+        prepare_kernel,
+        out_shape=(jax.ShapeDtypeStruct(left.shape, F32), jax.ShapeDtypeStruct((PACKED, LANES), F32)),
+        in_specs=[smem, vmem, smem, vmem],
+        out_specs=(vmem, vmem),
         scratch_shapes=[pltpu.SMEM((MAIN + 1,), jnp.int32)],
-    )(flags, x)
+    )(left_flags, left, right_flags, right)
 
 
 def split(x):
@@ -90,45 +80,52 @@
     return high, (x - high.astype(F32)).astype(BF)
 
 
-def product_kernel(side, where, packed, *refs):
-    parts, (out, tiles, lefts, high0, high1, low0, low1, homes, tile_sems, left_sems, home_sem) = refs[:9], refs[9:]
+def product_kernel(side, first, last, where, packed, *refs):
+    steps = range(first, last)
+    count = sum(2 if k == 7 else 1 for k in steps)
+    parts, refs = refs[:count], refs[count:]
+    if first:
+        before, refs = refs[0], refs[1:]
+    out, tiles, lefts, high0, high1, low0, low1, homes, tile_sems, left_sems, home_sem = refs
     need = tiles.shape[2]
-    copies = []
+    copies = {}
     if side:
         home_copy = pltpu.make_async_copy(packed.at[:, pl.ds(0, 8), :], homes, home_sem)
         home_copy.start()
-    for k in range(8):
-        tile = pltpu.make_async_copy(packed.at[pl.ds(where[k] * 2, 2), pl.ds(0, need), :], tiles.at[k], tile_sems.at[k])
+    for k in steps:
+        n = k - first
+        tile = pltpu.make_async_copy(packed.at[pl.ds(where[k] * 2, 2), pl.ds(0, need), :], tiles.at[n], tile_sems.at[n])
         tile.start()
         if k < 7:
-            pieces = [pltpu.make_async_copy(parts[k], lefts.at[k], left_sems.at[k])]
+            pieces = [pltpu.make_async_copy(parts[n], lefts.at[n], left_sems.at[n])]
         else:
             pieces = [
-                pltpu.make_async_copy(parts[7 + h], lefts.at[7, pl.ds(h * 256, 256)], left_sems.at[7 + h]) for h in range(2)
+                pltpu.make_async_copy(parts[n + h], lefts.at[n, pl.ds(h * 256, 256)], left_sems.at[n + h]) for h in range(2)
             ]
         for piece in pieces:
             piece.start()
-        copies.append([tile] + pieces)
+        copies[k] = [tile] + pieces
     half = lane_half()
     if side:
         home_copy.wait()
 
     def unpack(k):
-        high, low = (high0, low0) if k % 2 == 0 else (high1, low1)
+        n = k - first
+        high, low = (high0, low0) if n % 2 == 0 else (high1, low1)
         for z in range(2):
             for b in range(2):
                 for c in range(4):
                     pair = 4 * side + c
                     if pair < 6:
-                        mask = tiles[k, z, pl.ds(1 + pair * 2 + b, 1), :]
-                        value = tiles[k, z, pl.ds(META + pair * LANES + b * BS, BS), :] * mask
+                        mask = tiles[n, z, pl.ds(1 + pair * 2 + b, 1), :]
+                        value = tiles[n, z, pl.ds(META + pair * LANES + b * BS, BS), :] * mask
                     else:
                         halves = []
                         for h in range(2):
                             slot = homes[where[k] * 2 + z, 0, b * 4 + 2 * (pair - 6) + h].astype(jnp.int32)
                             kept = slot >= 0
                             slot = jnp.maximum(slot, 0)
-                            block = tiles[k, z, pl.ds(pl.multiple_of(META + (slot >> 1) * BS, 16), BS), :]
+                            block = tiles[n, z, pl.ds(pl.multiple_of(META + (slot >> 1) * BS, 16), BS), :]
                             block = jnp.where((slot & 1) == h, block, pltpu.roll(block, BS, 1))
                             halves.append(jnp.where(kept, block, 0.0))
                         value = jnp.where(half == 0, halves[0], halves[1])
@@ -136,43 +133,48 @@
                     high[at], low[at] = split(value)
         return high, low
 
-    for k in range(8):
+    for k in steps:
         for copy in copies[k]:
             copy.wait()
         high, low = unpack(k)
-        left_high, left_low = split(lefts[k])
+        left_high, left_low = split(lefts[k - first])
         total = jnp.dot(left_low, high[...], preferred_element_type=F32)
         total += jnp.dot(left_high, low[...], preferred_element_type=F32)
         total += jnp.dot(left_high, high[...], preferred_element_type=F32)
-        if k:
+        if k > first:
             total += out[...]
+        elif first:
+            total += before[...]
         out[...] = total
 
 
-def product(side, parts, where, packed):
+def product(side, first, last, parts, where, packed, *before):
     smem = pl.BlockSpec(memory_space=pltpu.SMEM)
     hbm = pl.BlockSpec(memory_space=pltpu.HBM)
+    vmem = pl.BlockSpec(memory_space=pltpu.VMEM)
     need = PACKED if side else META + 4 * LANES
+    steps = last - first
+    half = pltpu.VMEM((256, 512), BF)
     return pl.pallas_call(
-        functools.partial(product_kernel, side),
+        functools.partial(product_kernel, side, first, last),
         out_shape=jax.ShapeDtypeStruct((512, 512), F32),
-        in_specs=[smem] + [hbm] * 10,
-        out_specs=pl.BlockSpec(memory_space=pltpu.VMEM),
+        in_specs=[smem] + [hbm] * (1 + len(parts)) + [vmem] * len(before),
+        out_specs=vmem,
         scratch_shapes=[
-            pltpu.VMEM((8, 2, need, LANES), F32),
-            pltpu.VMEM((8, 512, 256), F32),
-            pltpu.VMEM((256, 512), BF),
-            pltpu.VMEM((256, 512), BF),
-            pltpu.VMEM((256, 512), BF),
-            pltpu.VMEM((256, 512), BF),
+            pltpu.VMEM((steps, 2, need, LANES), F32),
+            pltpu.VMEM((steps, 512, 256), F32),
+            half,
+            half,
+            half,
+            half,
             pltpu.SMEM((16, 8, LANES), F32),
-            pltpu.SemaphoreType.DMA((8,)),
-            pltpu.SemaphoreType.DMA((9,)),
+            pltpu.SemaphoreType.DMA((steps,)),
+            pltpu.SemaphoreType.DMA((steps + 1,)),
             pltpu.SemaphoreType.DMA,
         ],
-        cost_estimate=pl.CostEstimate(flops=6 * 512 * 512 * 2048, bytes_accessed=9 << 20, transcendentals=0),
+        cost_estimate=pl.CostEstimate(flops=6 * 512 * 512 * 256 * steps, bytes_accessed=steps << 20, transcendentals=0),
         compiler_params=pltpu.CompilerParams(vmem_limit_bytes=56 << 20),
-    )(where, packed, *parts)
+    )(where, packed, *parts, *before)
 
 
 def finish_kernel(side, where, flags, terms, square, *refs):
@@ -210,22 +212,26 @@
         return lax.ppermute(x, "col", shift(8, by))
 
     up1, down1 = send(own, 1), send(own, -1)
-    up2, down2 = send(own, 2), send(own, -2)
+    up2, down2 = send(up1, 1), send(down1, -1)
     up3, down3 = send(up2, 1), send(down2, -1)
-    far_a, far_b = send(up2[:256], 2), send(down2[256:], -2)
+    far_a, far_b = send(up3[:256], 1), send(down3[256:], -1)
     return [own, up1, down1, up2, down2, up3, down3, far_a, far_b]
 
 
 def local(left_slab, right_window, left_pattern, right_pattern, square_blocks, result_pattern):
-    packed = pack_right(right_window[0], right_pattern[0])
+    left, packed = prepare(left_slab[0], left_pattern[0].T, right_window[0], right_pattern[0])
     packed = lax.all_gather(packed, "row", axis=0, tiled=False)
-    parts = gather_left(mask_left(left_slab[0], left_pattern[0].T))
+    parts = gather_left(left)
     me = lax.axis_index("col")
     where = lax.rem(me + jnp.array([8, 7, 9, 6, 10, 5, 11, 12], jnp.int32), 8)
     layer = lax.axis_index("layer").reshape((1,))
     out = ()
     for side in range(2):
-        cube = product(side, parts, where, packed)
+        if side:
+            cube = product(side, 0, 8, parts, where, packed)
+        else:
+            cube = product(side, 0, 7, parts[:7], where, packed)
+            cube = product(side, 7, 8, parts[7:], where, packed, cube)
         terms = lax.all_to_all(cube.reshape(4, 128, 512), "layer", 0, 0)
         out = (finish(side, terms, square_blocks, result_pattern, layer, *out),)
     return out[0]

time: 134 us -> 125 us (0.933)
  waiting for transfers between devices: 49.2 us -> 42.9 us
  starting transfers between devices: 41.5 us -> 35.7 us
  Pallas kernels: 25.6 us -> 27.4 us
  local copies, waits for them, and re-layouts: 1.77 us -> 3.26 us
    ppermute x8, waiting for transfers between devices: 32.9 us -> 23.2 us  [send(): return lax.ppermute(x, 'col', shift(8, by))]
    ppermute x8, starting transfers between devices: 33.5 us -> 27.9 us  [send(): return lax.ppermute(x, 'col', shift(8, by))]
    all_to_all x2, waiting for transfers between devices: 16.3 us -> 18.7 us  [local(): terms = lax.all_to_all(cube.reshape(4, 128, 512), 'layer', 0, 0)]
    pallas_call x4, Pallas kernels: 21.5 us -> 23.2 us  [the longest x3 20.6 us: product(): pl.pallas_call(functools.partial(product_kernel, side, first, last), out_...]
    slice x2, local copies, waits for them, and re-layouts: 0.04 us -> 1.55 us  [gather_left(): far_a, far_b = (send(up3[:256], 1), send(down3[256:], -1))]
  transfers between devices with their start and end apart: 11 -> 11, of which waited for: 6 -> 8; matrix products, arithmetic and copies ran while one was open for 1% -> 2% of each run, Pallas kernels for 10% -> 15%
where the time goes in v3:
time: 125 us; the launch traced here: 124 us
  waiting for transfers between devices  42.9 us (34%)
  starting transfers between devices  35.7 us (29%)
  Pallas kernels  27.4 us (22%)
  between operations  13.6 us (11%)
  local copies, waits for them, and re-layouts  3.26 us (3%)
    ppermute x8, starting transfers between devices, send(): return lax.ppermute(x, 'col', shift(8, by))  27.9 us
    ppermute x8, waiting for transfers between devices, send(): return lax.ppermute(x, 'col', shift(8, by))  23.2 us
    pallas_call x3, Pallas kernels, product(): pl.pallas_call(functools.partial(product_kernel, side, first, last), out_...  20.6 us
    all_to_all x2, waiting for transfers between devices, local(): terms = lax.all_to_all(cube.reshape(4, 128, 512), 'layer', 0, 0)  18.7 us
    all_to_all x2, starting transfers between devices, local(): terms = lax.all_to_all(cube.reshape(4, 128, 512), 'layer', 0, 0)  7.78 us
    pallas_call x2, Pallas kernels, finish(): pl.pallas_call(functools.partial(finish_kernel, side), out_shape=jax.Shap...  4.13 us
    pallas_call x1, Pallas kernels, prepare(): pl.pallas_call(prepare_kernel, out_shape=(jax.ShapeDtypeStruct(left.shape...  2.65 us
  transfers between devices with their start and end apart: 11, of which 8 were waited for; matrix products, arithmetic and copies ran while one was open for 2% of the time, Pallas kernels for 15%

profile of v3, /device:TPU:8, one launch (start us, length us, event | category | flops | bytes accessed | tf_op | source)
XLA Modules:
  0.0 124.0 jit_solution(11333485078555153556)
XLA Ops:
  6.5 2.6 %shard_map.73 = (f32[512,256]{1,0:T(8,128)}, f32[784,128]{1,0:T(8,128)}) custom-call(s32[4,8]{1,0:T(4,128)} %bitcast.17, f32[512,256]{1,0:T(8,128)} %bitcast.15, s32[2,16]{1,0:T(2,128)} %bitcast.18, f32[128,1024]{1,0:T(8,128)} %bitcast.16), custom_call_target="tpu_custom_call" | custom-call | tf_op jit(solution)/shard_map/pallas_call | solution.py:69
  9.2 0.0 all-gather.3.cloned.1.call-update
  9.2 7.8 %collective-permute-start.1 = (f32[512,256]{1,0:T(8,128)}, f32[512,256]{1,0:T(8,128)S(1)}, u32[]{:S(2)}, u32[]{:S(2)}) collective-permute-start(f32[512,256]{1,0:T(8,128)} %get-tuple-element.8.refs_0_), channel_id=1, source_target_pairs={{0,28},{4,0},{8,4},{12,8},{16,12},{20,16},{24,20},{28,24},{1,29},{... | collective-permute-start | bytes 1572872 | tf_op jit(solution)/shard_map/ppermute | solution.py:212
  17.0 1.9 %collective-permute-start = (f32[512,256]{1,0:T(8,128)}, f32[512,256]{1,0:T(8,128)S(1)}, u32[]{:S(2)}, u32[]{:S(2)}) collective-permute-start(f32[512,256]{1,0:T(8,128)} %get-tuple-element.8.refs_0_), channel_id=1, source_target_pairs={{0,4},{4,8},{8,12},{12,16},{16,20},{20,24},{24,28},{28,0},{1,5},{5... | collective-permute-start | bytes 1572872 | tf_op jit(solution)/shard_map/ppermute | solution.py:212
  18.9 6.0 %collective-permute-done.1.refs_2_ = f32[512,256]{1,0:T(8,128)S(1)} collective-permute-done((f32[512,256]{1,0:T(8,128)}, f32[512,256]{1,0:T(8,128)S(1)}, u32[]{:S(2)}, u32[]{:S(2)}) %collective-permute-start.1) | collective-permute-done | bytes 524320 | tf_op jit(solution)/shard_map/ppermute | solution.py:212
  25.0 3.4 %collective-permute-start.3 = (f32[512,256]{1,0:T(8,128)S(1)}, f32[512,256]{1,0:T(8,128)S(1)}, u32[]{:S(2)}, u32[]{:S(2)}) collective-permute-start(f32[512,256]{1,0:T(8,128)S(1)} %collective-permute-done.1.refs_2_), channel_id=1, source_target_pairs={{0,28},{4,0},{8,4},{12,8},{16,12},{20,16},{24,20},{28,24},{1,29},{... | collective-permute-start | bytes 1572872 | tf_op jit(solution)/shard_map/ppermute | solution.py:212
  28.4 0.4 collective-permute-done.refs_1_
  28.8 2.0 %collective-permute-start.2 = (f32[512,256]{1,0:T(8,128)S(1)}, f32[512,256]{1,0:T(8,128)S(1)}, u32[]{:S(2)}, u32[]{:S(2)}) collective-permute-start(f32[512,256]{1,0:T(8,128)S(1)} %collective-permute-done.refs_1_), channel_id=1, source_target_pairs={{0,4},{4,8},{8,12},{12,16},{16,20},{20,24},{24,28},{28,0},{1,5},{5... | collective-permute-start | bytes 1572872 | tf_op jit(solution)/shard_map/ppermute | solution.py:212
  30.8 8.8 %collective-permute-done.3.refs_4_ = f32[512,256]{1,0:T(8,128)S(1)} collective-permute-done((f32[512,256]{1,0:T(8,128)S(1)}, f32[512,256]{1,0:T(8,128)S(1)}, u32[]{:S(2)}, u32[]{:S(2)}) %collective-permute-start.3) | collective-permute-done | bytes 524320 | tf_op jit(solution)/shard_map/ppermute | solution.py:212
  39.7 2.5 %collective-permute-start.5 = (f32[512,256]{1,0:T(8,128)S(1)}, f32[512,256]{1,0:T(8,128)S(1)}, u32[]{:S(2)}, u32[]{:S(2)}) collective-permute-start(f32[512,256]{1,0:T(8,128)S(1)} %collective-permute-done.3.refs_4_), channel_id=1, source_target_pairs={{0,28},{4,0},{8,4},{12,8},{16,12},{20,16},{24,20},{28,24},{1,29},{... | collective-permute-start | bytes 1572872 | tf_op jit(solution)/shard_map/ppermute | solution.py:212
  42.2 0.5 collective-permute-done.2.refs_3_
  42.7 3.7 %collective-permute-start.4 = (f32[512,256]{1,0:T(8,128)S(1)}, f32[512,256]{1,0:T(8,128)S(1)}, u32[]{:S(2)}, u32[]{:S(2)}) collective-permute-start(f32[512,256]{1,0:T(8,128)S(1)} %collective-permute-done.2.refs_3_), channel_id=1, source_target_pairs={{0,4},{4,8},{8,12},{12,16},{16,20},{20,24},{24,28},{28,0},{1,5},{5... | collective-permute-start | bytes 1572872 | tf_op jit(solution)/shard_map/ppermute | solution.py:212
  46.4 1.2 %compare_select_fusion.where = s32[8]{0:T(128)} fusion(s32[8]{0:T(128)} %constant.16.clone, s32[]{:T(128)S(6)} %axis_index.25), kind=kLoop, calls=%fused_computation | loop fusion | flops 56 | bytes 68 | tf_op jit(solution)/shard_map/rem | solution.py:226
  47.7 7.4 %collective-permute-done.5.refs_6_ = f32[512,256]{1,0:T(8,128)S(1)} collective-permute-done((f32[512,256]{1,0:T(8,128)S(1)}, f32[512,256]{1,0:T(8,128)S(1)}, u32[]{:S(2)}, u32[]{:S(2)}) %collective-permute-start.5) | collective-permute-done | bytes 524320 | tf_op jit(solution)/shard_map/ppermute | solution.py:212
  55.1 0.8 slice.9
  55.9 1.9 %collective-permute-start.7 = (f32[256,256]{1,0:T(8,128)}, f32[256,256]{1,0:T(8,128)S(1)}, u32[]{:S(2)}, u32[]{:S(2)}) collective-permute-start(f32[256,256]{1,0:T(8,128)} %slice.9), channel_id=1, source_target_pairs={{0,28},{4,0},{8,4},{12,8},{16,12},{20,16},{24,20},{28,24},{1,29},{... | collective-permute-start | bytes 786440 | tf_op jit(solution)/shard_map/ppermute | solution.py:212
  57.8 0.0 collective-permute-done.4.refs_5_
  57.8 0.8 slice.8
  58.6 4.6 %collective-permute-start.6 = (f32[256,256]{1,0:T(8,128)}, f32[256,256]{1,0:T(8,128)}, u32[]{:S(2)}, u32[]{:S(2)}) collective-permute-start(f32[256,256]{1,0:T(8,128)} %slice.8), channel_id=1, source_target_pairs={{0,4},{4,8},{8,12},{12,16},{16,20},{20,24},{24,28},{28,0},{1,5},{5... | collective-permute-start | bytes 786440 | tf_op jit(solution)/shard_map/ppermute | solution.py:212
  63.2 1.0 all-gather.3.cloned.1.call-done
  64.2 7.1 %shard_map.75.refs_2_ = f32[512,512]{1,0:T(8,128)} custom-call(s32[8]{0:T(128)} %compare_select_fusion.where, f32[16,784,128]{2,1,0:T(8,128)} %bitcast.10, f32[512,256]{1,0:T(8,128)} %get-tuple-element.8.refs_0_, f32[512,256]{1,0:T(8,128)} %copy-done.5, f32[512,256]{1,0:T(8,128)} %copy-done.4, f32[512,256]{1,0:T(8,128)} %copy-done.7, f32[512,256]{1,0:T(8,128)} %copy-done.6, ...), custom_call_target="tpu_custom_call" | custom-call | flops 2818572288 | bytes 7340032 | tf_op jit(solution)/shard_map/pallas_call | solution.py:158
  71.3 0.0 collective-permute-done.7.refs_8_.refs_1_
  71.3 0.7 copy-done.8
  72.0 4.2 %shard_map.76 = f32[512,512]{1,0:T(8,128)} custom-call(s32[8]{0:T(128)} %compare_select_fusion.where, f32[16,784,128]{2,1,0:T(8,128)} %bitcast.11, f32[256,256]{1,0:T(8,128)} %collective-permute-done.6.refs_7_.refs_0_, f32[256,256]{1,0:T(8,128)} %copy-done.8, f32[512,512]{1,0:T(8,128)} %shard_map.75.refs_2_), custom_call_target="tpu_custom_call" | custom-call | flops 402653184 | bytes 1048576 | tf_op jit(solution)/shard_map/pallas_call | solution.py:158
  76.2 4.3 %all-to-all-start.1 = ((f32[4,128,512]{2,1,0:T(8,128)}), f32[4,128,512]{2,1,0:T(8,128)S(1)}, u32[]{:S(2)}, u32[]{:S(2)}) async-start(f32[4,128,512]{2,1,0:T(8,128)} %bitcast.13), calls=%async_computation.1 | async-start | bytes 2097152 | tf_op jit(solution)/shard_map/all_to_all | solution.py:235
  80.5 9.3 %shard_map.74 = f32[512,512]{1,0:T(8,128)} custom-call(s32[8]{0:T(128)} %compare_select_fusion.where, f32[16,784,128]{2,1,0:T(8,128)} %bitcast.12, f32[512,256]{1,0:T(8,128)} %get-tuple-element.8.refs_0_, f32[512,256]{1,0:T(8,128)} %copy-done.5, f32[512,256]{1,0:T(8,128)} %copy-done.4, f32[512,256]{1,0:T(8,128)} %copy-done.7, f32[512,256]{1,0:T(8,128)} %copy-done.6, ...), custom_call_target="tpu_custom_call" | custom-call | flops 3221225472 | bytes 8388608 | tf_op jit(solution)/shard_map/pallas_call | solution.py:158
  89.8 6.2 %all-to-all-done.1.terms = f32[4,128,512]{2,1,0:T(8,128)S(1)} async-done(((f32[4,128,512]{2,1,0:T(8,128)}), f32[4,128,512]{2,1,0:T(8,128)S(1)}, u32[]{:S(2)}, u32[]{:S(2)}) %all-to-all-start.1) | async-done | bytes 1048608 | tf_op jit(solution)/shard_map/all_to_all | solution.py:235
  96.0 3.5 %all-to-all-start = ((f32[4,128,512]{2,1,0:T(8,128)}), f32[4,128,512]{2,1,0:T(8,128)S(1)}, u32[]{:S(2)}, u32[]{:S(2)}) async-start(f32[4,128,512]{2,1,0:T(8,128)} %bitcast.14), calls=%async_computation | async-start | bytes 2097152 | tf_op jit(solution)/shard_map/all_to_all | solution.py:235
  99.5 2.1 %shard_map.77.refs_0_ = f32[128,1024]{1,0:T(8,128)} custom-call(s32[1]{0:T(128)} %bitcast.where, s32[8,16]{1,0:T(8,128)} %flags.3, f32[4,128,512]{2,1,0:T(8,128)} %copy-done, f32[128,1024]{1,0:T(8,128)} %square.3), custom_call_target="tpu_custom_call" | custom-call | flops 1048576 | bytes 2097152 | tf_op jit(solution)/shard_map/pallas_call | solution.py:194
  101.6 12.5 %all-to-all-done.terms = f32[4,128,512]{2,1,0:T(8,128)S(1)} async-done(((f32[4,128,512]{2,1,0:T(8,128)}), f32[4,128,512]{2,1,0:T(8,128)S(1)}, u32[]{:S(2)}, u32[]{:S(2)}) %all-to-all-start) | async-done | bytes 1048608 | tf_op jit(solution)/shard_map/all_to_all | solution.py:235
  114.1 1.0 copy-done.1
  115.1 2.1 %shard_map.78 = f32[128,1024]{1,0:T(8,128)} custom-call(s32[1]{0:T(128)} %bitcast.where, s32[8,16]{1,0:T(8,128)} %flags.3, f32[4,128,512]{2,1,0:T(8,128)} %copy-done.1, f32[128,1024]{1,0:T(8,128)} %square.3, f32[128,1024]{1,0:T(8,128)} %shard_map.77.refs_0_), custom_call_target="tpu_custom_call", output_to_operand_aliasing={{}: (4, {})} | custom-call | flops 1048576 | bytes 2097152 | tf_op jit(solution)/shard_map/pallas_call | solution.py:194
  (18 shorter events, 0.0 us)
Async XLA Ops:
  6.5 57.6 %all-gather.3.cloned.1.call-start = ((), (), s32[]{:S(2)}) async-start(), calls=%async_computation.2 | async-start | bytes 6823936 | tf_op jit(solution)/shard_map/all_gather | solution.py:223
  9.2 15.8 %collective-permute-start.1 = (f32[512,256]{1,0:T(8,128)}, f32[512,256]{1,0:T(8,128)S(1)}, u32[]{:S(2)}, u32[]{:S(2)}) collective-permute-start(f32[512,256]{1,0:T(8,128)} %get-tuple-element.8.refs_0_), channel_id=1, source_target_pairs={{0,28},{4,0},{8,4},{12,8},{16,12},{20,16},{24,20},{28,24},{1,29},{... | collective-permute-start | bytes 1572872 | tf_op jit(solution)/shard_map/ppermute | solution.py:212
  17.0 11.8 %collective-permute-start = (f32[512,256]{1,0:T(8,128)}, f32[512,256]{1,0:T(8,128)S(1)}, u32[]{:S(2)}, u32[]{:S(2)}) collective-permute-start(f32[512,256]{1,0:T(8,128)} %get-tuple-element.8.refs_0_), channel_id=1, source_target_pairs={{0,4},{4,8},{8,12},{12,16},{16,20},{20,24},{24,28},{28,0},{1,5},{5... | collective-permute-start | bytes 1572872 | tf_op jit(solution)/shard_map/ppermute | solution.py:212
  25.0 39.2 %copy-start.4 = (f32[512,256]{1,0:T(8,128)}, f32[512,256]{1,0:T(8,128)S(1)}, u32[]{:S(2)}) copy-start(f32[512,256]{1,0:T(8,128)S(1)} %collective-permute-done.1.refs_2_) | copy-start | bytes 1572868
  25.0 14.7 %collective-permute-start.3 = (f32[512,256]{1,0:T(8,128)S(1)}, f32[512,256]{1,0:T(8,128)S(1)}, u32[]{:S(2)}, u32[]{:S(2)}) collective-permute-start(f32[512,256]{1,0:T(8,128)S(1)} %collective-permute-done.1.refs_2_), channel_id=1, source_target_pairs={{0,28},{4,0},{8,4},{12,8},{16,12},{20,16},{24,20},{28,24},{1,29},{... | collective-permute-start | bytes 1572872 | tf_op jit(solution)/shard_map/ppermute | solution.py:212
  28.8 35.4 %copy-start.5 = (f32[512,256]{1,0:T(8,128)}, f32[512,256]{1,0:T(8,128)S(1)}, u32[]{:S(2)}) copy-start(f32[512,256]{1,0:T(8,128)S(1)} %collective-permute-done.refs_1_) | copy-start | bytes 1572868
  28.8 13.9 %collective-permute-start.2 = (f32[512,256]{1,0:T(8,128)S(1)}, f32[512,256]{1,0:T(8,128)S(1)}, u32[]{:S(2)}, u32[]{:S(2)}) collective-permute-start(f32[512,256]{1,0:T(8,128)S(1)} %collective-permute-done.refs_1_), channel_id=1, source_target_pairs={{0,4},{4,8},{8,12},{12,16},{16,20},{20,24},{24,28},{28,0},{1,5},{5... | collective-permute-start | bytes 1572872 | tf_op jit(solution)/shard_map/ppermute | solution.py:212
  39.7 24.5 %copy-start.6 = (f32[512,256]{1,0:T(8,128)}, f32[512,256]{1,0:T(8,128)S(1)}, u32[]{:S(2)}) copy-start(f32[512,256]{1,0:T(8,128)S(1)} %collective-permute-done.3.refs_4_) | copy-start | bytes 1572868
  39.7 15.4 %collective-permute-start.5 = (f32[512,256]{1,0:T(8,128)S(1)}, f32[512,256]{1,0:T(8,128)S(1)}, u32[]{:S(2)}, u32[]{:S(2)}) collective-permute-start(f32[512,256]{1,0:T(8,128)S(1)} %collective-permute-done.3.refs_4_), channel_id=1, source_target_pairs={{0,28},{4,0},{8,4},{12,8},{16,12},{20,16},{24,20},{28,24},{1,29},{... | collective-permute-start | bytes 1572872 | tf_op jit(solution)/shard_map/ppermute | solution.py:212
  42.7 21.5 %copy-start.7 = (f32[512,256]{1,0:T(8,128)}, f32[512,256]{1,0:T(8,128)S(1)}, u32[]{:S(2)}) copy-start(f32[512,256]{1,0:T(8,128)S(1)} %collective-permute-done.2.refs_3_) | copy-start | bytes 1572868
  42.7 15.1 %collective-permute-start.4 = (f32[512,256]{1,0:T(8,128)S(1)}, f32[512,256]{1,0:T(8,128)S(1)}, u32[]{:S(2)}, u32[]{:S(2)}) collective-permute-start(f32[512,256]{1,0:T(8,128)S(1)} %collective-permute-done.2.refs_3_), channel_id=1, source_target_pairs={{0,4},{4,8},{8,12},{12,16},{16,20},{20,24},{24,28},{28,0},{1,5},{5... | collective-permute-start | bytes 1572872 | tf_op jit(solution)/shard_map/ppermute | solution.py:212
  55.1 9.1 %copy-start.2 = (f32[512,256]{1,0:T(8,128)}, f32[512,256]{1,0:T(8,128)S(1)}, u32[]{:S(2)}) copy-start(f32[512,256]{1,0:T(8,128)S(1)} %collective-permute-done.5.refs_6_) | copy-start | bytes 1572868
  55.9 15.4 %collective-permute-start.7 = (f32[256,256]{1,0:T(8,128)}, f32[256,256]{1,0:T(8,128)S(1)}, u32[]{:S(2)}, u32[]{:S(2)}) collective-permute-start(f32[256,256]{1,0:T(8,128)} %slice.9), channel_id=1, source_target_pairs={{0,28},{4,0},{8,4},{12,8},{16,12},{20,16},{24,20},{28,24},{1,29},{... | collective-permute-start | bytes 786440 | tf_op jit(solution)/shard_map/ppermute | solution.py:212
  57.8 6.4 %copy-start.3 = (f32[512,256]{1,0:T(8,128)}, f32[512,256]{1,0:T(8,128)S(1)}, u32[]{:S(2)}) copy-start(f32[512,256]{1,0:T(8,128)S(1)} %collective-permute-done.4.refs_5_) | copy-start | bytes 1572868
  58.6 12.7 %collective-permute-start.6 = (f32[256,256]{1,0:T(8,128)}, f32[256,256]{1,0:T(8,128)}, u32[]{:S(2)}, u32[]{:S(2)}) collective-permute-start(f32[256,256]{1,0:T(8,128)} %slice.8), channel_id=1, source_target_pairs={{0,4},{4,8},{8,12},{12,16},{16,20},{20,24},{24,28},{28,0},{1,5},{5... | collective-permute-start | bytes 786440 | tf_op jit(solution)/shard_map/ppermute | solution.py:212
  71.3 0.7 copy-start.8
  76.2 19.8 %all-to-all-start.1 = ((f32[4,128,512]{2,1,0:T(8,128)}), f32[4,128,512]{2,1,0:T(8,128)S(1)}, u32[]{:S(2)}, u32[]{:S(2)}) async-start(f32[4,128,512]{2,1,0:T(8,128)} %bitcast.13), calls=%async_computation.1 | async-start | bytes 2097152 | tf_op jit(solution)/shard_map/all_to_all | solution.py:235
  96.0 3.5 %copy-start = (f32[4,128,512]{2,1,0:T(8,128)}, f32[4,128,512]{2,1,0:T(8,128)S(1)}, u32[]{:S(2)}) copy-start(f32[4,128,512]{2,1,0:T(8,128)S(1)} %all-to-all-done.1.terms) | copy-start | bytes 3145732
  96.0 18.1 %all-to-all-start = ((f32[4,128,512]{2,1,0:T(8,128)}), f32[4,128,512]{2,1,0:T(8,128)S(1)}, u32[]{:S(2)}, u32[]{:S(2)}) async-start(f32[4,128,512]{2,1,0:T(8,128)} %bitcast.14), calls=%async_computation | async-start | bytes 2097152 | tf_op jit(solution)/shard_map/all_to_all | solution.py:235
  114.1 1.0 copy-start.1
Sparse Core Ops, SparseCore 0:
  9.5 54.6 all-gather.2

commit v4 on v3

--- a/solution.py
+++ b/solution.py
@@ -89,8 +89,11 @@
     out, tiles, lefts, high0, high1, low0, low1, homes, tile_sems, left_sems, home_sem = refs
     need = tiles.shape[2]
     copies = {}
+    if first:
+        sum_copy = pltpu.make_async_copy(before, out, home_sem)
+        sum_copy.start()
     if side:
-        home_copy = pltpu.make_async_copy(packed.at[:, pl.ds(0, 8), :], homes, home_sem)
+        home_copy = pltpu.make_async_copy(packed.at[:, pl.ds(0, 1), :], homes, home_sem)
         home_copy.start()
     for k in steps:
         n = k - first
@@ -141,10 +144,10 @@
         total = jnp.dot(left_low, high[...], preferred_element_type=F32)
         total += jnp.dot(left_high, low[...], preferred_element_type=F32)
         total += jnp.dot(left_high, high[...], preferred_element_type=F32)
-        if k > first:
+        if k == first and first:
+            sum_copy.wait()
+        if k:
             total += out[...]
-        elif first:
-            total += before[...]
         out[...] = total
 
 
@@ -158,7 +161,7 @@
     return pl.pallas_call(
         functools.partial(product_kernel, side, first, last),
         out_shape=jax.ShapeDtypeStruct((512, 512), F32),
-        in_specs=[smem] + [hbm] * (1 + len(parts)) + [vmem] * len(before),
+        in_specs=[smem] + [hbm] * (1 + len(parts)) + [hbm] * len(before),
         out_specs=vmem,
         scratch_shapes=[
             pltpu.VMEM((steps, 2, need, LANES), F32),
@@ -167,7 +170,7 @@
             half,
             half,
             half,
-            pltpu.SMEM((16, 8, LANES), F32),
+            pltpu.SMEM((16, 1, LANES), F32),
             pltpu.SemaphoreType.DMA((steps,)),
             pltpu.SemaphoreType.DMA((steps + 1,)),
             pltpu.SemaphoreType.DMA,
@@ -177,30 +180,31 @@
     )(where, packed, *parts, *before)
 
 
-def finish_kernel(side, where, flags, terms, square, *refs):
-    out = refs[-1]
+def finish_kernel(where, flags, summed, terms, square, out):
     for b in range(2):
-        for c in range(4):
+        for c in range(8):
             at = (pl.ds(b * BS, BS), pl.ds(c * LANES, LANES))
-            total = (terms[(0,) + at] + terms[(1,) + at]) + (terms[(2,) + at] + terms[(3,) + at])
-            line, column = where[0] * 2 + b, 8 * side + 2 * c
-            mask = pair_mask(flags[line, column], flags[line, column + 1])
+            near = (pl.ds(b * BS, BS), pl.ds(c % 4 * LANES, LANES))
+            if c < 4:
+                total = summed[near]
+            else:
+                total = (terms[(0,) + near] + terms[(1,) + near]) + (terms[(2,) + near] + terms[(3,) + near])
+            line = where[0] * 2 + b
+            mask = pair_mask(flags[line, 2 * c], flags[line, 2 * c + 1])
             out[at] = mask * (3.0 * square[at] - 2.0 * total)
 
 
-def finish(side, terms, square, flags, where, *before):
+def finish(summed, terms, square, flags, where):
     smem = pl.BlockSpec(memory_space=pltpu.SMEM)
-    half = pl.BlockSpec((128, 512), lambda i: (0, side))
+    vmem = pl.BlockSpec(memory_space=pltpu.VMEM)
     return pl.pallas_call(
-        functools.partial(finish_kernel, side),
+        finish_kernel,
         out_shape=jax.ShapeDtypeStruct(square.shape, F32),
-        grid=(1,),
-        in_specs=[smem, smem, pl.BlockSpec((4, 128, 512), lambda i: (0, 0, 0)), half]
-        + [pl.BlockSpec(memory_space=pltpu.HBM)] * len(before),
-        out_specs=half,
-        input_output_aliases={4: 0} if before else {},
+        in_specs=[smem, smem, vmem, vmem, vmem],
+        out_specs=vmem,
         cost_estimate=pl.CostEstimate(flops=1 << 20, bytes_accessed=2 << 20, transcendentals=0),
-    )(where, flags, terms, square, *before)
+        compiler_params=pltpu.CompilerParams(vmem_limit_bytes=56 << 20),
+    )(where, flags, summed, terms, square)
 
 
 def shift(n, by):
@@ -225,16 +229,12 @@
     me = lax.axis_index("col")
     where = lax.rem(me + jnp.array([8, 7, 9, 6, 10, 5, 11, 12], jnp.int32), 8)
     layer = lax.axis_index("layer").reshape((1,))
-    out = ()
-    for side in range(2):
-        if side:
-            cube = product(side, 0, 8, parts, where, packed)
-        else:
-            cube = product(side, 0, 7, parts[:7], where, packed)
-            cube = product(side, 7, 8, parts[7:], where, packed, cube)
-        terms = lax.all_to_all(cube.reshape(4, 128, 512), "layer", 0, 0)
-        out = (finish(side, terms, square_blocks, result_pattern, layer, *out),)
-    return out[0]
+    cube = product(0, 0, 7, parts[:7], where, packed)
+    cube = product(0, 7, 8, parts[7:], where, packed, cube)
+    summed = lax.psum_scatter(cube, "layer", scatter_dimension=0, tiled=True)
+    cube = product(1, 0, 8, parts, where, packed)
+    terms = lax.all_to_all(cube.reshape(4, 128, 512), "layer", 0, 0)
+    return finish(summed, terms, square_blocks, result_pattern, layer)
 
 
 def solution(mesh):

time: 125 us -> 124 us (level)
  the two profiles are of different devices: /device:TPU:8 before, /device:TPU:1 now
where the time goes in v4:
time: 124 us
  waiting for transfers between devices  48.4 us (39%)
  starting transfers between devices  33.3 us (27%)
  Pallas kernels  25.2 us (20%)
  between operations  13.6 us (11%)
  local copies, waits for them, and re-layouts  2.27 us (2%)
    ppermute x8, starting transfers between devices, send(): return lax.ppermute(x, 'col', shift(8, by))  29.3 us
    pallas_call x3, Pallas kernels, product(): pl.pallas_call(functools.partial(product_kernel, side, first, last), out_...  20.1 us
    ppermute x8, waiting for transfers between devices, send(): return lax.ppermute(x, 'col', shift(8, by))  19.4 us
    all_to_all x1, waiting for transfers between devices, local(): terms = lax.all_to_all(cube.reshape(4, 128, 512), 'layer', 0, 0)  15.7 us
    reduce_scatter x1, waiting for transfers between devices, local(): summed = lax.psum_scatter(cube, 'layer', scatter_dimension=0, tiled=True)  8.64 us
    all_gather x1, waiting for transfers between devices, local(): packed = lax.all_gather(packed, 'row', axis=0, tiled=False)  4.6 us
    all_to_all x1, starting transfers between devices, local(): terms = lax.all_to_all(cube.reshape(4, 128, 512), 'layer', 0, 0)  3.98 us
    pallas_call x1, Pallas kernels, prepare(): pl.pallas_call(prepare_kernel, out_shape=(jax.ShapeDtypeStruct(left.shape...  2.7 us
  transfers between devices with their start and end apart: 11, of which 6 were waited for; matrix products, arithmetic and copies ran while one was open for 2% of the time, Pallas kernels for 13%

profile of v4, /device:TPU:1, one launch (start us, length us, event | category | flops | bytes accessed | tf_op | source)
XLA Modules:
  0.0 123.9 jit_solution(4370337781149250801)
XLA Ops:
  6.5 2.7 %shard_map.73 = (f32[512,256]{1,0:T(8,128)}, f32[784,128]{1,0:T(8,128)}) custom-call(s32[4,8]{1,0:T(4,128)} %bitcast.15, f32[512,256]{1,0:T(8,128)} %bitcast.13, s32[2,16]{1,0:T(2,128)} %bitcast.16, f32[128,1024]{1,0:T(8,128)} %bitcast.14), custom_call_target="tpu_custom_call" | custom-call | tf_op jit(solution)/shard_map/pallas_call | solution.py:69
  9.2 0.0 all-gather.3.cloned.1.call-update
  9.3 0.0 reduce-scatter.2.cloned.1.call-start
  9.3 5.8 %collective-permute-start.4 = (f32[512,256]{1,0:T(8,128)}, f32[512,256]{1,0:T(8,128)S(1)}, u32[]{:S(2)}, u32[]{:S(2)}) collective-permute-start(f32[512,256]{1,0:T(8,128)} %get-tuple-element.8.refs_0_), channel_id=1, source_target_pairs={{0,28},{4,0},{8,4},{12,8},{16,12},{20,16},{24,20},{28,24},{1,29},{... | collective-permute-start | bytes 1572872 | tf_op jit(solution)/shard_map/ppermute | solution.py:216
  15.2 1.9 %collective-permute-start = (f32[512,256]{1,0:T(8,128)}, f32[512,256]{1,0:T(8,128)S(1)}, u32[]{:S(2)}, u32[]{:S(2)}) collective-permute-start(f32[512,256]{1,0:T(8,128)} %get-tuple-element.8.refs_0_), channel_id=1, source_target_pairs={{0,4},{4,8},{8,12},{12,16},{16,20},{20,24},{24,28},{28,0},{1,5},{5... | collective-permute-start | bytes 1572872 | tf_op jit(solution)/shard_map/ppermute | solution.py:216
  17.1 7.0 %collective-permute-done.4.refs_2_ = f32[512,256]{1,0:T(8,128)S(1)} collective-permute-done((f32[512,256]{1,0:T(8,128)}, f32[512,256]{1,0:T(8,128)S(1)}, u32[]{:S(2)}, u32[]{:S(2)}) %collective-permute-start.4) | collective-permute-done | bytes 524320 | tf_op jit(solution)/shard_map/ppermute | solution.py:216
  24.1 5.2 %collective-permute-start.5 = (f32[512,256]{1,0:T(8,128)S(1)}, f32[512,256]{1,0:T(8,128)S(1)}, u32[]{:S(2)}, u32[]{:S(2)}) collective-permute-start(f32[512,256]{1,0:T(8,128)S(1)} %collective-permute-done.4.refs_2_), channel_id=1, source_target_pairs={{0,28},{4,0},{8,4},{12,8},{16,12},{20,16},{24,20},{28,24},{1,29},{... | collective-permute-start | bytes 1572872 | tf_op jit(solution)/shard_map/ppermute | solution.py:216
  29.3 0.0 collective-permute-done.refs_1_
  29.3 1.9 %collective-permute-start.1 = (f32[512,256]{1,0:T(8,128)S(1)}, f32[512,256]{1,0:T(8,128)S(1)}, u32[]{:S(2)}, u32[]{:S(2)}) collective-permute-start(f32[512,256]{1,0:T(8,128)S(1)} %collective-permute-done.refs_1_), channel_id=1, source_target_pairs={{0,4},{4,8},{8,12},{12,16},{16,20},{20,24},{24,28},{28,0},{1,5},{5... | collective-permute-start | bytes 1572872 | tf_op jit(solution)/shard_map/ppermute | solution.py:216
  31.2 6.5 %collective-permute-done.5.refs_4_ = f32[512,256]{1,0:T(8,128)S(1)} collective-permute-done((f32[512,256]{1,0:T(8,128)S(1)}, f32[512,256]{1,0:T(8,128)S(1)}, u32[]{:S(2)}, u32[]{:S(2)}) %collective-permute-start.5) | collective-permute-done | bytes 524320 | tf_op jit(solution)/shard_map/ppermute | solution.py:216
  37.8 5.0 %collective-permute-start.6 = (f32[512,256]{1,0:T(8,128)S(1)}, f32[512,256]{1,0:T(8,128)S(1)}, u32[]{:S(2)}, u32[]{:S(2)}) collective-permute-start(f32[512,256]{1,0:T(8,128)S(1)} %collective-permute-done.5.refs_4_), channel_id=1, source_target_pairs={{0,28},{4,0},{8,4},{12,8},{16,12},{20,16},{24,20},{28,24},{1,29},{... | collective-permute-start | bytes 1572872 | tf_op jit(solution)/shard_map/ppermute | solution.py:216
  42.8 0.0 collective-permute-done.1.refs_3_
  42.8 1.9 %collective-permute-start.2 = (f32[512,256]{1,0:T(8,128)S(1)}, f32[512,256]{1,0:T(8,128)S(1)}, u32[]{:S(2)}, u32[]{:S(2)}) collective-permute-start(f32[512,256]{1,0:T(8,128)S(1)} %collective-permute-done.1.refs_3_), channel_id=1, source_target_pairs={{0,4},{4,8},{8,12},{12,16},{16,20},{20,24},{24,28},{28,0},{1,5},{5... | collective-permute-start | bytes 1572872 | tf_op jit(solution)/shard_map/ppermute | solution.py:216
  44.7 1.2 compare_select_fusion.where
  46.0 5.9 %collective-permute-done.6.refs_6_ = f32[512,256]{1,0:T(8,128)S(1)} collective-permute-done((f32[512,256]{1,0:T(8,128)S(1)}, f32[512,256]{1,0:T(8,128)S(1)}, u32[]{:S(2)}, u32[]{:S(2)}) %collective-permute-start.6) | collective-permute-done | bytes 524320 | tf_op jit(solution)/shard_map/ppermute | solution.py:216
  51.9 0.8 slice.9
  52.6 4.0 %collective-permute-start.7 = (f32[256,256]{1,0:T(8,128)}, f32[256,256]{1,0:T(8,128)S(1)}, u32[]{:S(2)}, u32[]{:S(2)}) collective-permute-start(f32[256,256]{1,0:T(8,128)} %slice.9), channel_id=1, source_target_pairs={{0,28},{4,0},{8,4},{12,8},{16,12},{20,16},{24,20},{28,24},{1,29},{... | collective-permute-start | bytes 786440 | tf_op jit(solution)/shard_map/ppermute | solution.py:216
  56.7 0.0 collective-permute-done.2.refs_5_
  56.7 0.8 slice.8
  57.5 3.4 %collective-permute-start.3 = (f32[256,256]{1,0:T(8,128)}, f32[256,256]{1,0:T(8,128)}, u32[]{:S(2)}, u32[]{:S(2)}) collective-permute-start(f32[256,256]{1,0:T(8,128)} %slice.8), channel_id=1, source_target_pairs={{0,4},{4,8},{8,12},{12,16},{16,20},{20,24},{24,28},{28,0},{1,5},{5... | collective-permute-start | bytes 786440 | tf_op jit(solution)/shard_map/ppermute | solution.py:216
  60.9 4.6 %all-gather.3.cloned.1.call-done = f32[12544,128]{1,0:T(8,128)} async-done(((f32[784,128]{1,0:T(8,128)}), f32[12544,128]{1,0:T(8,128)}) %all-gather.3.cloned.1.call-update) | async-done | bytes 6422544 | tf_op jit(solution)/shard_map/all_gather | solution.py:227
  65.5 7.2 %shard_map.74.refs_2_ = f32[512,512]{1,0:T(8,128)} custom-call(s32[8]{0:T(128)} %compare_select_fusion.where, f32[16,784,128]{2,1,0:T(8,128)} %bitcast.9, f32[512,256]{1,0:T(8,128)} %get-tuple-element.8.refs_0_, f32[512,256]{1,0:T(8,128)} %copy-done.4, f32[512,256]{1,0:T(8,128)} %copy-done.3, f32[512,256]{1,0:T(8,128)} %copy-done.6, f32[512,256]{1,0:T(8,128)} %copy-done.5, ...), custom_call_target="tpu_custom_call" | custom-call | flops 2818572288 | bytes 7340032 | tf_op jit(solution)/shard_map/pallas_call | solution.py:161
  72.7 0.0 collective-permute-done.7.refs_1_.refs_8_
  72.7 0.0 collective-permute-done.3.refs_0_.refs_7_
  72.8 0.7 copy-done.7
  73.4 4.0 %shard_map.75 = f32[512,512]{1,0:T(8,128)} custom-call(s32[8]{0:T(128)} %compare_select_fusion.where, f32[16,784,128]{2,1,0:T(8,128)} %bitcast.10, f32[256,256]{1,0:T(8,128)} %collective-permute-done.3.refs_0_.refs_7_, f32[256,256]{1,0:T(8,128)} %copy-done.7, f32[512,512]{1,0:T(8,128)} %shard_map.74.refs_2_), custom_call_target="tpu_custom_call" | custom-call | flops 402653184 | bytes 1048576 | tf_op jit(solution)/shard_map/pallas_call | solution.py:161
  77.4 0.0 reduce-scatter.2.cloned.1.call-update
  77.4 9.0 %shard_map.76 = f32[512,512]{1,0:T(8,128)} custom-call(s32[8]{0:T(128)} %compare_select_fusion.where, f32[16,784,128]{2,1,0:T(8,128)} %bitcast.11, f32[512,256]{1,0:T(8,128)} %get-tuple-element.8.refs_0_, f32[512,256]{1,0:T(8,128)} %copy-done.4, f32[512,256]{1,0:T(8,128)} %copy-done.3, f32[512,256]{1,0:T(8,128)} %copy-done.6, f32[512,256]{1,0:T(8,128)} %copy-done.5, ...), custom_call_target="tpu_custom_call" | custom-call | flops 3221225472 | bytes 8388608 | tf_op jit(solution)/shard_map/pallas_call | solution.py:161
  86.4 4.0 %all-to-all-start = ((f32[4,128,512]{2,1,0:T(8,128)}), f32[4,128,512]{2,1,0:T(8,128)S(1)}, u32[]{:S(2)}, u32[]{:S(2)}) async-start(f32[4,128,512]{2,1,0:T(8,128)} %bitcast.12), calls=%async_computation.1 | async-start | bytes 2097152 | tf_op jit(solution)/shard_map/all_to_all | solution.py:236
  90.4 15.7 %all-to-all-done.terms = f32[4,128,512]{2,1,0:T(8,128)S(1)} async-done(((f32[4,128,512]{2,1,0:T(8,128)}), f32[4,128,512]{2,1,0:T(8,128)S(1)}, u32[]{:S(2)}, u32[]{:S(2)}) %all-to-all-start) | async-done | bytes 1048608 | tf_op jit(solution)/shard_map/all_to_all | solution.py:236
  106.1 8.6 %reduce-scatter.2.cloned.1.call-done.summed = f32[128,512]{1,0:T(8,128)} async-done(((f32[512,512]{1,0:T(8,128)}), f32[128,512]{1,0:T(8,128)}) %reduce-scatter.2.cloned.1.call-update) | async-done | bytes 262160 | tf_op jit(solution)/shard_map/reduce_scatter | solution.py:234
  114.7 2.4 %shard_map.77 = f32[128,1024]{1,0:T(8,128)} custom-call(s32[1]{0:T(128)} %bitcast.where, s32[8,16]{1,0:T(8,128)} %flags.1, f32[128,512]{1,0:T(8,128)} %reduce-scatter.2.cloned.1.call-done.summed, f32[4,128,512]{2,1,0:T(8,128)} %copy-done, f32[128,1024]{1,0:T(8,128)} %square.1), custom_call_target="tpu_custom_call" | custom-call | flops 1048576 | bytes 2097152 | tf_op jit(solution)/shard_map/pallas_call | solution.py:200
  (16 shorter events, 0.0 us)
Async XLA Ops:
  6.5 59.0 %all-gather.3.cloned.1.call-start = ((), (), s32[]{:S(2)}) async-start(), calls=%async_computation.3 | async-start | bytes 6823936 | tf_op jit(solution)/shard_map/all_gather | solution.py:227
  9.3 105.5 %reduce-scatter.2.cloned.1.call-start = ((), (), s32[]{:S(2)}) async-start(), calls=%async_computation.2 | async-start | bytes 1310720 | tf_op jit(solution)/shard_map/reduce_scatter | solution.py:234
  9.3 14.7 %collective-permute-start.4 = (f32[512,256]{1,0:T(8,128)}, f32[512,256]{1,0:T(8,128)S(1)}, u32[]{:S(2)}, u32[]{:S(2)}) collective-permute-start(f32[512,256]{1,0:T(8,128)} %get-tuple-element.8.refs_0_), channel_id=1, source_target_pairs={{0,28},{4,0},{8,4},{12,8},{16,12},{20,16},{24,20},{28,24},{1,29},{... | collective-permute-start | bytes 1572872 | tf_op jit(solution)/shard_map/ppermute | solution.py:216
  15.2 14.1 %collective-permute-start = (f32[512,256]{1,0:T(8,128)}, f32[512,256]{1,0:T(8,128)S(1)}, u32[]{:S(2)}, u32[]{:S(2)}) collective-permute-start(f32[512,256]{1,0:T(8,128)} %get-tuple-element.8.refs_0_), channel_id=1, source_target_pairs={{0,4},{4,8},{8,12},{12,16},{16,20},{20,24},{24,28},{28,0},{1,5},{5... | collective-permute-start | bytes 1572872 | tf_op jit(solution)/shard_map/ppermute | solution.py:216
  24.1 41.4 %copy-start.3 = (f32[512,256]{1,0:T(8,128)}, f32[512,256]{1,0:T(8,128)S(1)}, u32[]{:S(2)}) copy-start(f32[512,256]{1,0:T(8,128)S(1)} %collective-permute-done.4.refs_2_) | copy-start | bytes 1572868
  24.1 13.7 %collective-permute-start.5 = (f32[512,256]{1,0:T(8,128)S(1)}, f32[512,256]{1,0:T(8,128)S(1)}, u32[]{:S(2)}, u32[]{:S(2)}) collective-permute-start(f32[512,256]{1,0:T(8,128)S(1)} %collective-permute-done.4.refs_2_), channel_id=1, source_target_pairs={{0,28},{4,0},{8,4},{12,8},{16,12},{20,16},{24,20},{28,24},{1,29},{... | collective-permute-start | bytes 1572872 | tf_op jit(solution)/shard_map/ppermute | solution.py:216
  29.3 36.2 %copy-start.4 = (f32[512,256]{1,0:T(8,128)}, f32[512,256]{1,0:T(8,128)S(1)}, u32[]{:S(2)}) copy-start(f32[512,256]{1,0:T(8,128)S(1)} %collective-permute-done.refs_1_) | copy-start | bytes 1572868
  29.3 13.5 %collective-permute-start.1 = (f32[512,256]{1,0:T(8,128)S(1)}, f32[512,256]{1,0:T(8,128)S(1)}, u32[]{:S(2)}, u32[]{:S(2)}) collective-permute-start(f32[512,256]{1,0:T(8,128)S(1)} %collective-permute-done.refs_1_), channel_id=1, source_target_pairs={{0,4},{4,8},{8,12},{12,16},{16,20},{20,24},{24,28},{28,0},{1,5},{5... | collective-permute-start | bytes 1572872 | tf_op jit(solution)/shard_map/ppermute | solution.py:216
  37.8 27.8 %copy-start.5 = (f32[512,256]{1,0:T(8,128)}, f32[512,256]{1,0:T(8,128)S(1)}, u32[]{:S(2)}) copy-start(f32[512,256]{1,0:T(8,128)S(1)} %collective-permute-done.5.refs_4_) | copy-start | bytes 1572868
  37.8 14.1 %collective-permute-start.6 = (f32[512,256]{1,0:T(8,128)S(1)}, f32[512,256]{1,0:T(8,128)S(1)}, u32[]{:S(2)}, u32[]{:S(2)}) collective-permute-start(f32[512,256]{1,0:T(8,128)S(1)} %collective-permute-done.5.refs_4_), channel_id=1, source_target_pairs={{0,28},{4,0},{8,4},{12,8},{16,12},{20,16},{24,20},{28,24},{1,29},{... | collective-permute-start | bytes 1572872 | tf_op jit(solution)/shard_map/ppermute | solution.py:216
  42.8 22.7 %copy-start.6 = (f32[512,256]{1,0:T(8,128)}, f32[512,256]{1,0:T(8,128)S(1)}, u32[]{:S(2)}) copy-start(f32[512,256]{1,0:T(8,128)S(1)} %collective-permute-done.1.refs_3_) | copy-start | bytes 1572868
  42.8 13.9 %collective-permute-start.2 = (f32[512,256]{1,0:T(8,128)S(1)}, f32[512,256]{1,0:T(8,128)S(1)}, u32[]{:S(2)}, u32[]{:S(2)}) collective-permute-start(f32[512,256]{1,0:T(8,128)S(1)} %collective-permute-done.1.refs_3_), channel_id=1, source_target_pairs={{0,4},{4,8},{8,12},{12,16},{16,20},{20,24},{24,28},{28,0},{1,5},{5... | collective-permute-start | bytes 1572872 | tf_op jit(solution)/shard_map/ppermute | solution.py:216
  51.9 13.7 %copy-start.1 = (f32[512,256]{1,0:T(8,128)}, f32[512,256]{1,0:T(8,128)S(1)}, u32[]{:S(2)}) copy-start(f32[512,256]{1,0:T(8,128)S(1)} %collective-permute-done.6.refs_6_) | copy-start | bytes 1572868
  52.6 20.1 %collective-permute-start.7 = (f32[256,256]{1,0:T(8,128)}, f32[256,256]{1,0:T(8,128)S(1)}, u32[]{:S(2)}, u32[]{:S(2)}) collective-permute-start(f32[256,256]{1,0:T(8,128)} %slice.9), channel_id=1, source_target_pairs={{0,28},{4,0},{8,4},{12,8},{16,12},{20,16},{24,20},{28,24},{1,29},{... | collective-permute-start | bytes 786440 | tf_op jit(solution)/shard_map/ppermute | solution.py:216
  56.7 8.9 %copy-start.2 = (f32[512,256]{1,0:T(8,128)}, f32[512,256]{1,0:T(8,128)S(1)}, u32[]{:S(2)}) copy-start(f32[512,256]{1,0:T(8,128)S(1)} %collective-permute-done.2.refs_5_) | copy-start | bytes 1572868
  57.5 15.3 %collective-permute-start.3 = (f32[256,256]{1,0:T(8,128)}, f32[256,256]{1,0:T(8,128)}, u32[]{:S(2)}, u32[]{:S(2)}) collective-permute-start(f32[256,256]{1,0:T(8,128)} %slice.8), channel_id=1, source_target_pairs={{0,4},{4,8},{8,12},{12,16},{16,20},{20,24},{24,28},{28,0},{1,5},{5... | collective-permute-start | bytes 786440 | tf_op jit(solution)/shard_map/ppermute | solution.py:216
  72.7 0.7 copy-start.7
  86.4 19.6 %all-to-all-start = ((f32[4,128,512]{2,1,0:T(8,128)}), f32[4,128,512]{2,1,0:T(8,128)S(1)}, u32[]{:S(2)}, u32[]{:S(2)}) async-start(f32[4,128,512]{2,1,0:T(8,128)} %bitcast.12), calls=%async_computation.1 | async-start | bytes 2097152 | tf_op jit(solution)/shard_map/all_to_all | solution.py:236
  106.1 8.6 %copy-start = (f32[4,128,512]{2,1,0:T(8,128)}, f32[4,128,512]{2,1,0:T(8,128)S(1)}, u32[]{:S(2)}) copy-start(f32[4,128,512]{2,1,0:T(8,128)S(1)} %all-to-all-done.terms) | copy-start | bytes 3145732
Sparse Core Ops, SparseCore 0:
  9.5 55.9 all-gather.2
  77.5 37.1 reduce-scatter.1

commit v5 on v4

v5 whole, which is shorter than its diff:
```python
import functools

import jax
import jax.numpy as jnp
from jax import lax
from jax.experimental import pallas as pl
from jax.experimental.pallas import tpu as pltpu
from jax.sharding import PartitionSpec as P

BS = 64
LANES = 128
MAIN = 24
EXTRA = 8
META = 16
PACKED = META + 6 * LANES
BF = jnp.bfloat16
F32 = jnp.float32


def lane_half():
    return lax.broadcasted_iota(jnp.int32, (BS, LANES), 1) // BS


def pair_mask(low, high):
    return jnp.where(lane_half() == 0, low.astype(F32), high.astype(F32))


def prepare_kernel(left_flags, left, flags, x, left_out, out, holes):
    for i in range(8):
        for c in range(2):
            mask = pair_mask(left_flags[2 * c, i], left_flags[2 * c + 1, i])
            at = (pl.ds(i * BS, BS), pl.ds(c * LANES, LANES))
            left_out[at] = left[at] * mask
    for c in range(6):
        out[pl.ds(META + c * LANES, LANES), :] = x[:, pl.ds(c * LANES, LANES)]
    count = jnp.int32(0)
    for s in range(MAIN):
        holes[count] = s
        count = count + jnp.where(flags[(s >> 1) & 1, 2 * (s >> 2) + (s & 1)] == 0, 1, 0)
    used = jnp.int32(0)
    half = lane_half()
    lane = lax.broadcasted_iota(jnp.int32, (1, LANES), 1)
    row = jnp.zeros((1, LANES), F32)
    for e in range(EXTRA):
        kept = flags[e >> 2, 12 + (e & 3)] != 0
        slot = holes[jnp.minimum(used, EXTRA)]
        row = jnp.where(lane == e, jnp.where(kept, slot, -1).astype(F32), row)
        used = used + jnp.where(kept, 1, 0)

        @pl.when(kept)
        def _():
            at = pl.ds(pl.multiple_of(META + (slot >> 1) * BS, 16), BS)
            block = x[pl.ds((e >> 2) * BS, BS), pl.ds((6 + ((e >> 1) & 1)) * LANES, LANES)]
            side = slot & 1
            block = jnp.where(side == (e & 1), block, pltpu.roll(block, BS, 1))
            out[at, :] = jnp.where(half == side, block, out[at, :])

    out[pl.ds(0, 1), :] = row
    for c in range(6):
        for b in range(2):
            mask = jnp.where(lane < BS, flags[b, 2 * c].astype(F32), flags[b, 2 * c + 1].astype(F32))
            out[pl.ds(1 + c * 2 + b, 1), :] = mask
    out[pl.ds(13, 3), :] = jnp.zeros((3, LANES), F32)


def prepare(left, left_flags, right, right_flags):
    smem = pl.BlockSpec(memory_space=pltpu.SMEM)
    vmem = pl.BlockSpec(memory_space=pltpu.VMEM)
    return pl.pallas_call(
        prepare_kernel,
        out_shape=(jax.ShapeDtypeStruct(left.shape, F32), jax.ShapeDtypeStruct((PACKED, LANES), F32)),
        in_specs=[smem, vmem, smem, vmem],
        out_specs=(vmem, vmem),
        scratch_shapes=[pltpu.SMEM((MAIN + 1,), jnp.int32)],
    )(left_flags, left, right_flags, right)


def split(x):
    high = x.astype(BF)
    return high, (x - high.astype(F32)).astype(BF)


def product_kernel(place, *refs):
    items, lefts_in = refs[:10], refs[10:18]
    out, tiles, lefts, rights, homes, tile_sems, home_sems, left_sems = refs[18:]
    z, core = place[8], place[9]
    other = 1 - core
    toward = 2 * core - 1

    def tile_copy(source, chip, parity):
        return pltpu.make_async_copy(source, tiles.at[chip, parity], tile_sems.at[chip, parity])

    def home_copy(source, chip, parity):
        return pltpu.make_async_copy(source, homes.at[chip, parity], home_sems.at[chip, parity])

    def left_copy(n):
        return pltpu.make_async_copy(lefts_in[n], lefts.at[n], left_sems.at[n])

    own, swapped, rings, trades = items[0], items[1], items[2:6], items[6:10]
    sources = [(own, 0, core), (swapped, 0, other)]
    for s in range(3):
        sources += [(rings[s].at[0], (s + 1) * toward, core), (rings[s].at[1], (s + 1) * toward, other)]
        sources += [(trades[s].at[0], -(s + 1) * toward, other), (trades[s].at[1], -(s + 1) * toward, core)]
    sources += [(rings[3], 4, core), (trades[3], 4, other)]
    for ref, by, parity in sources:
        chip = (z + by + 8) & 7
        home_copy(ref.at[pl.ds(0, 1)], chip, parity).start()
        tile_copy(ref, chip, parity).start()
    for n in range(8):
        left_copy(n).start()
    half = lane_half()

    def unpack(n, slot):
        chip = place[n]
        for parity in range(2):
            tile_copy(own, chip, parity).wait()
            home_copy(own.at[pl.ds(0, 1)], chip, parity).wait()
        for parity in range(2):
            for b in range(2):
                for pair in range(8):
                    if pair < 6:
                        mask = tiles[chip, parity, pl.ds(1 + pair * 2 + b, 1), :]
                        value = tiles[chip, parity, pl.ds(META + pair * LANES + b * BS, BS), :] * mask
                    else:
                        halves = []
                        for h in range(2):
                            home = homes[chip, parity, 0, b * 4 + 2 * (pair - 6) + h].astype(jnp.int32)
                            kept = home >= 0
                            home = jnp.maximum(home, 0)
                            block = tiles[chip, parity, pl.ds(pl.multiple_of(META + (home >> 1) * BS, 16), BS), :]
                            block = jnp.where((home & 1) == h, block, pltpu.roll(block, BS, 1))
                            halves.append(jnp.where(kept, block, 0.0))
                        value = jnp.where(half == 0, halves[0], halves[1])
                    high, low = split(value)
                    row, columns = parity * LANES + b * BS, pl.ds(pair * LANES, LANES)
                    rights[slot, pl.ds(row, BS), columns] = high
                    rights[slot, pl.ds(256 + row, BS), columns] = high
                    rights[slot, pl.ds(512 + row, BS), columns] = low

    def multiply(n, slot):
        high, low = split(lefts[n])
        left = jnp.concatenate([low, high, high], 1)
        out[...] += jnp.dot(left, rights[slot], preferred_element_type=F32)

    out[...] = jnp.zeros_like(out)
    unpack(0, 0)

    @pl.loop(0, 3)
    def _(i):
        n = 2 * i
        pltpu.make_async_copy(lefts_in[0], lefts.at[n], left_sems.at[n]).wait()
        unpack(n + 1, 1)
        multiply(n, 0)
        pltpu.make_async_copy(lefts_in[0], lefts.at[n + 1], left_sems.at[n + 1]).wait()
        unpack(n + 2, 0)
        multiply(n + 1, 1)

    left_copy(6).wait()
    unpack(7, 1)
    multiply(6, 0)
    left_copy(7).wait()
    multiply(7, 1)


def product(place, items, parts):
    smem = pl.BlockSpec(memory_space=pltpu.SMEM)
    hbm = pl.BlockSpec(memory_space=pltpu.HBM)
    return pl.pallas_call(
        product_kernel,
        out_shape=jax.ShapeDtypeStruct((512, 1024), F32),
        in_specs=[smem] + [hbm] * 18,
        out_specs=pl.BlockSpec(memory_space=pltpu.VMEM),
        scratch_shapes=[
            pltpu.VMEM((8, 2, PACKED, LANES), F32),
            pltpu.VMEM((8, 512, 256), F32),
            pltpu.VMEM((2, 768, 1024), BF),
            pltpu.SMEM((8, 2, 1, LANES), F32),
            pltpu.SemaphoreType.DMA((8, 2)),
            pltpu.SemaphoreType.DMA((8, 2)),
            pltpu.SemaphoreType.DMA((8,)),
        ],
        cost_estimate=pl.CostEstimate(flops=6 * 512 * 1024 * 2048, bytes_accessed=13 << 20, transcendentals=0),
        compiler_params=pltpu.CompilerParams(vmem_limit_bytes=56 << 20),
    )(place, *items, *parts)


def finish_kernel(place, flags, terms, square, out):
    for b in range(2):
        for c in range(8):
            at = (pl.ds(b * BS, BS), pl.ds(c * LANES, LANES))
            total = (terms[(0,) + at] + terms[(1,) + at]) + (terms[(2,) + at] + terms[(3,) + at])
            line = place[10] * 2 + b
            mask = pair_mask(flags[line, 2 * c], flags[line, 2 * c + 1])
            out[at] = mask * (3.0 * square[at] - 2.0 * total)


def finish(place, terms, square, flags):
    smem = pl.BlockSpec(memory_space=pltpu.SMEM)
    vmem = pl.BlockSpec(memory_space=pltpu.VMEM)
    return pl.pallas_call(
        finish_kernel,
        out_shape=jax.ShapeDtypeStruct(square.shape, F32),
        in_specs=[smem, smem, vmem, vmem],
        out_specs=vmem,
        cost_estimate=pl.CostEstimate(flops=1 << 20, bytes_accessed=3 << 20, transcendentals=0),
        compiler_params=pltpu.CompilerParams(vmem_limit_bytes=56 << 20),
    )(place, flags, terms, square)


def shift(n, by):
    return [(i, (i + by) % n) for i in range(n)]


def gather(left, right):
    def send(x, by):
        return lax.ppermute(x, "col", shift(8, by))

    def tie(x, *others):
        return lax.optimization_barrier((x,) + others)[0]

    ring = [(2 * z + c, 2 * ((z + 1 - 2 * c) % 8) + c) for z in range(8) for c in range(2)]
    trade = [(i, i ^ 1) for i in range(16)]
    up = down = left
    parts, rings, trades = [left], [], []
    swapped = lax.ppermute(right, "row", trade)
    pair = jnp.stack([right, swapped])
    for step in range(4):
        up = send(up, 1)
        parts.append(up)
        if step:
            pair = tie(pair, parts[2 * step - 1], down)
        pair = lax.ppermute(pair if step < 3 else pair[0], "row", ring)
        rings.append(pair)
        if step < 3:
            down = send(down, -1)
            parts.append(down)
        trades.append(lax.ppermute(tie(pair, up), "row", trade))
    return [right, swapped] + rings + trades, parts


def local(left_slab, right_window, left_pattern, right_pattern, square_blocks, result_pattern):
    left, packed = prepare(left_slab[0], left_pattern[0].T, right_window[0], right_pattern[0])
    items, parts = gather(left, packed)
    row, col, layer = (lax.axis_index(name) for name in ("row", "col", "layer"))
    arrivals = lax.rem(col + jnp.array([8, 7, 9, 6, 10, 5, 11, 4], jnp.int32), 8)
    place = jnp.concatenate([arrivals, jnp.stack([row >> 1, row & 1, layer])])
    cube = product(place, items, parts)
    terms = lax.all_to_all(cube.reshape(4, 128, 1024), "layer", 0, 0)
    return finish(place, terms, square_blocks, result_pattern)


def solution(mesh):
    in_specs = (
        P("layer", "row", "col"),
        P("layer", "row", "col"),
        P("layer", "row", "col"),
        P("layer", "row", "col"),
        P(("row", "layer"), "col"),
        P("row", "col"),
    )
    out_specs = P(("row", "layer"), "col")
    return jax.shard_map(local, mesh=mesh, in_specs=in_specs, out_specs=out_specs, check_vma=False)
```

time: 124 us -> 147 us (1.19)
  blocking collectives: 0 us -> 30.6 us
  starting transfers between devices: 33.3 us -> 56.5 us
  between operations: 13.6 us -> 0.25 us
  waiting for transfers between devices: 48.4 us -> 37.5 us
  Pallas kernels: 25.2 us -> 19 us
    ppermute x0 -> x9, starting transfers between devices: none -> 35.7 us  [the longest x4 17.5 us: gather(): pair = lax.ppermute(pair if step < 3 else pair[0], 'row', ring)]
    all_to_all x0 -> x1, blocking collectives: none -> 30.6 us  [local(): terms = lax.all_to_all(cube.reshape(4, 128, 1024), 'layer', 0, 0)]
    all_to_all x1 -> x0, waiting for transfers between devices: 15.7 us -> none  [local(): terms = lax.all_to_all(cube.reshape(4, 128, 512), 'layer', 0, 0)]
    ppermute x8 -> x7, waiting for transfers between devices: 19.4 us -> 35 us  [send(): return lax.ppermute(x, 'col', shift(8, by))]
    reduce_scatter x1 -> x0, waiting for transfers between devices: 8.64 us -> none  [local(): summed = lax.psum_scatter(cube, 'layer', scatter_dimension=0, tiled=True)]
    ppermute x8 -> x7, starting transfers between devices: 29.3 us -> 20.8 us  [send(): return lax.ppermute(x, 'col', shift(8, by))]
    pallas_call x3 -> x1, Pallas kernels: 20.1 us -> 13.7 us  [product(): pl.pallas_call(product_kernel, out_shape=jax.ShapeDtypeStruct((512, 1024)...]
    all_gather x1 -> x0, waiting for transfers between devices: 4.6 us -> none  [local(): packed = lax.all_gather(packed, 'row', axis=0, tiled=False)]
  transfers between devices with their start and end apart: 11 -> 16, of which waited for: 6 -> 8; matrix products, arithmetic and copies ran while one was open for 2% -> 0% of each run, Pallas kernels for 13% -> 0%
where the time goes in v5:
time: 147 us
  starting transfers between devices  56.5 us (38%)
  waiting for transfers between devices  37.5 us (26%)
  blocking collectives  30.6 us (21%)
  Pallas kernels  19 us (13%)
  other arithmetic  1.86 us (1%)
    ppermute x7, waiting for transfers between devices, send(): return lax.ppermute(x, 'col', shift(8, by))  35 us
    all_to_all x1, blocking collectives, local(): terms = lax.all_to_all(cube.reshape(4, 128, 1024), 'layer', 0, 0)  30.6 us
    ppermute x7, starting transfers between devices, send(): return lax.ppermute(x, 'col', shift(8, by))  20.8 us
    ppermute x4, starting transfers between devices, gather(): pair = lax.ppermute(pair if step < 3 else pair[0], 'row', ring)  17.5 us
    pallas_call x1, Pallas kernels, product(): pl.pallas_call(product_kernel, out_shape=jax.ShapeDtypeStruct((512, 1024)...  13.7 us
    ppermute x4, starting transfers between devices, gather(): trades.append(lax.ppermute(tie(pair, up), 'row', trade))  9.27 us
    ppermute x1, starting transfers between devices, gather(): swapped = lax.ppermute(right, 'row', trade)  8.92 us
  transfers between devices with their start and end apart: 16, of which 8 were waited for; matrix products, arithmetic and copies ran while one was open for 0% of the time, Pallas kernels for 0%

profile of v5, /device:TPU:1, one launch (start us, length us, event | category | flops | bytes accessed | tf_op | source)
XLA Modules:
  0.0 146.5 jit_solution(15008855122061300750)
XLA Ops:
  0.0 2.6 %shard_map.73 = (f32[512,256]{1,0:T(8,128)}, f32[784,128]{1,0:T(8,128)}) custom-call(s32[4,8]{1,0:T(4,128)} %bitcast.19, f32[512,256]{1,0:T(8,128)} %bitcast.15, s32[2,16]{1,0:T(2,128)} %bitcast.20, f32[128,1024]{1,0:T(8,128)} %bitcast.16), custom_call_target="tpu_custom_call" | custom-call | tf_op jit(solution)/shard_map/pallas_call | solution.py:69
  2.6 8.9 %collective-permute-start = (f32[784,128]{1,0:T(8,128)}, f32[784,128]{1,0:T(8,128)S(1)}, u32[]{:S(2)}, u32[]{:S(2)}) collective-permute-start(f32[784,128]{1,0:T(8,128)} %get-tuple-element.14.refs_0_), channel_id=1, source_target_pairs={{0,32},{32,0},{64,96},{96,64},{128,160},{160,128},{192,224},{224,1... | collective-permute-start | bytes 1204232 | tf_op jit(solution)/shard_map/ppermute | solution.py:225
  11.6 1.5 %collective-permute-done.refs_1_ = f32[784,128]{1,0:T(8,128)S(1)} collective-permute-done((f32[784,128]{1,0:T(8,128)}, f32[784,128]{1,0:T(8,128)S(1)}, u32[]{:S(2)}, u32[]{:S(2)}) %collective-permute-start) | collective-permute-done | bytes 401440 | tf_op jit(solution)/shard_map/ppermute | solution.py:225
  13.1 1.2 pad_maximum_fusion
  14.3 5.2 %collective-permute-start.1 = (f32[2,784,128]{2,1,0:T(8,128)S(1)}, f32[2,784,128]{2,1,0:T(8,128)S(1)}, u32[]{:S(2)}, u32[]{:S(2)}) collective-permute-start(f32[2,784,128]{2,1,0:T(8,128)S(1)} %pad_maximum_fusion), channel_id=1, source_target_pairs={{0,64},{32,480},{64,128},{96,32},{128,192},{160,96},{192,256},{224... | collective-permute-start | bytes 2408456 | tf_op jit(solution)/shard_map/ppermute | solution.py:232
  19.5 5.2 %collective-permute-start.3 = (f32[512,256]{1,0:T(8,128)}, f32[512,256]{1,0:T(8,128)S(1)}, u32[]{:S(2)}, u32[]{:S(2)}) collective-permute-start(f32[512,256]{1,0:T(8,128)} %get-tuple-element.15.refs_10_), channel_id=1, source_target_pairs={{0,28},{4,0},{8,4},{12,8},{16,12},{20,16},{24,20},{28,24},{1,29},{... | collective-permute-start | bytes 1572872 | tf_op jit(solution)/shard_map/ppermute | solution.py:216
  24.7 1.9 %collective-permute-start.2 = (f32[512,256]{1,0:T(8,128)}, f32[512,256]{1,0:T(8,128)S(1)}, u32[]{:S(2)}, u32[]{:S(2)}) collective-permute-start(f32[512,256]{1,0:T(8,128)} %get-tuple-element.15.refs_10_), channel_id=1, source_target_pairs={{0,4},{4,8},{8,12},{12,16},{16,20},{20,24},{24,28},{28,0},{1,5},{5... | collective-permute-start | bytes 1572872 | tf_op jit(solution)/shard_map/ppermute | solution.py:216
  26.6 6.2 %collective-permute-done.3.refs_12_ = f32[512,256]{1,0:T(8,128)S(1)} collective-permute-done((f32[512,256]{1,0:T(8,128)}, f32[512,256]{1,0:T(8,128)S(1)}, u32[]{:S(2)}, u32[]{:S(2)}) %collective-permute-start.3) | collective-permute-done | bytes 524320 | tf_op jit(solution)/shard_map/ppermute | solution.py:216
  32.8 3.5 %collective-permute-done.2.refs_11_ = f32[512,256]{1,0:T(8,128)S(1)} collective-permute-done((f32[512,256]{1,0:T(8,128)}, f32[512,256]{1,0:T(8,128)S(1)}, u32[]{:S(2)}, u32[]{:S(2)}) %collective-permute-start.2) | collective-permute-done | bytes 524320 | tf_op jit(solution)/shard_map/ppermute | solution.py:216
  36.4 0.0 collective-permute-done.1.refs_2_
  36.4 6.9 %collective-permute-start.4 = (f32[2,784,128]{2,1,0:T(8,128)S(1)}, f32[2,784,128]{2,1,0:T(8,128)S(1)}, u32[]{:S(2)}, u32[]{:S(2)}) collective-permute-start(f32[2,784,128]{2,1,0:T(8,128)S(1)} %collective-permute-done.1.refs_2_), channel_id=1, source_target_pairs={{0,64},{32,480},{64,128},{96,32},{128,192},{160,96},{192,256},{224... | collective-permute-start | bytes 2408456 | tf_op jit(solution)/shard_map/ppermute | solution.py:232
  43.2 2.0 %collective-permute-start.6 = (f32[512,256]{1,0:T(8,128)S(1)}, f32[512,256]{1,0:T(8,128)S(1)}, u32[]{:S(2)}, u32[]{:S(2)}) collective-permute-start(f32[512,256]{1,0:T(8,128)S(1)} %collective-permute-done.3.refs_12_), channel_id=1, source_target_pairs={{0,28},{4,0},{8,4},{12,8},{16,12},{20,16},{24,20},{28,24},{1,29},{... | collective-permute-start | bytes 1572872 | tf_op jit(solution)/shard_map/ppermute | solution.py:216
  45.2 3.3 %collective-permute-start.5 = (f32[512,256]{1,0:T(8,128)S(1)}, f32[512,256]{1,0:T(8,128)S(1)}, u32[]{:S(2)}, u32[]{:S(2)}) collective-permute-start(f32[512,256]{1,0:T(8,128)S(1)} %collective-permute-done.2.refs_11_), channel_id=1, source_target_pairs={{0,4},{4,8},{8,12},{12,16},{16,20},{20,24},{24,28},{28,0},{1,5},{5... | collective-permute-start | bytes 1572872 | tf_op jit(solution)/shard_map/ppermute | solution.py:216
  48.5 7.0 %collective-permute-done.6.refs_14_ = f32[512,256]{1,0:T(8,128)S(1)} collective-permute-done((f32[512,256]{1,0:T(8,128)S(1)}, f32[512,256]{1,0:T(8,128)S(1)}, u32[]{:S(2)}, u32[]{:S(2)}) %collective-permute-start.6) | collective-permute-done | bytes 524320 | tf_op jit(solution)/shard_map/ppermute | solution.py:216
  55.5 3.1 %collective-permute-done.5.refs_13_ = f32[512,256]{1,0:T(8,128)S(1)} collective-permute-done((f32[512,256]{1,0:T(8,128)S(1)}, f32[512,256]{1,0:T(8,128)S(1)}, u32[]{:S(2)}, u32[]{:S(2)}) %collective-permute-start.5) | collective-permute-done | bytes 524320 | tf_op jit(solution)/shard_map/ppermute | solution.py:216
  58.7 3.6 %collective-permute-start.7 = (f32[2,784,128]{2,1,0:T(8,128)S(1)}, f32[2,784,128]{2,1,0:T(8,128)S(1)}, u32[]{:S(2)}, u32[]{:S(2)}) collective-permute-start(f32[2,784,128]{2,1,0:T(8,128)S(1)} %collective-permute-done.4.refs_3_), channel_id=1, source_target_pairs={{0,64},{32,480},{64,128},{96,32},{128,192},{160,96},{192,256},{224... | collective-permute-start | bytes 2408456 | tf_op jit(solution)/shard_map/ppermute | solution.py:232
  62.3 2.0 %collective-permute-start.8 = (f32[512,256]{1,0:T(8,128)S(1)}, f32[512,256]{1,0:T(8,128)S(1)}, u32[]{:S(2)}, u32[]{:S(2)}) collective-permute-start(f32[512,256]{1,0:T(8,128)S(1)} %collective-permute-done.5.refs_13_), channel_id=1, source_target_pairs={{0,4},{4,8},{8,12},{12,16},{16,20},{20,24},{24,28},{28,0},{1,5},{5... | collective-permute-start | bytes 1572872 | tf_op jit(solution)/shard_map/ppermute | solution.py:216
  64.3 4.5 %collective-permute-start.9 = (f32[512,256]{1,0:T(8,128)S(1)}, f32[512,256]{1,0:T(8,128)S(1)}, u32[]{:S(2)}, u32[]{:S(2)}) collective-permute-start(f32[512,256]{1,0:T(8,128)S(1)} %collective-permute-done.6.refs_14_), channel_id=1, source_target_pairs={{0,28},{4,0},{8,4},{12,8},{16,12},{20,16},{24,20},{28,24},{1,29},{... | collective-permute-start | bytes 1572872 | tf_op jit(solution)/shard_map/ppermute | solution.py:216
  68.8 1.9 %collective-permute-start.11 = (f32[2,784,128]{2,1,0:T(8,128)S(1)}, f32[2,784,128]{2,1,0:T(8,128)}, u32[]{:S(2)}, u32[]{:S(2)}) collective-permute-start(f32[2,784,128]{2,1,0:T(8,128)S(1)} %collective-permute-done.1.refs_2_), channel_id=1, source_target_pairs={{0,32},{32,0},{64,96},{96,64},{128,160},{160,128},{192,224},{224,1... | collective-permute-start | bytes 2408456 | tf_op jit(solution)/shard_map/ppermute | solution.py:237
  70.7 7.8 %collective-permute-done.8.refs_15_ = f32[512,256]{1,0:T(8,128)S(1)} collective-permute-done((f32[512,256]{1,0:T(8,128)S(1)}, f32[512,256]{1,0:T(8,128)S(1)}, u32[]{:S(2)}, u32[]{:S(2)}) %collective-permute-start.8) | collective-permute-done | bytes 524320 | tf_op jit(solution)/shard_map/ppermute | solution.py:216
  78.6 1.9 %collective-permute-start.14 = (f32[512,256]{1,0:T(8,128)S(1)}, f32[512,256]{1,0:T(8,128)S(1)}, u32[]{:S(2)}, u32[]{:S(2)}) collective-permute-start(f32[512,256]{1,0:T(8,128)S(1)} %collective-permute-done.8.refs_15_), channel_id=1, source_target_pairs={{0,4},{4,8},{8,12},{12,16},{16,20},{20,24},{24,28},{28,0},{1,5},{5... | collective-permute-start | bytes 1572872 | tf_op jit(solution)/shard_map/ppermute | solution.py:216
  80.5 0.8 copy-done.9
  81.3 1.9 %collective-permute-start.10 = (f32[784,128]{1,0:T(8,128)S(1)}, f32[784,128]{1,0:T(8,128)}, u32[]{:S(2)}, u32[]{:S(2)}) collective-permute-start(f32[784,128]{1,0:T(8,128)S(1)} %slice_bitcast_fusion), channel_id=1, source_target_pairs={{0,64},{32,480},{64,128},{96,32},{128,192},{160,96},{192,256},{224... | collective-permute-start | bytes 1204232 | tf_op jit(solution)/shard_map/ppermute | solution.py:232
  83.2 2.2 %collective-permute-start.12 = (f32[2,784,128]{2,1,0:T(8,128)S(1)}, f32[2,784,128]{2,1,0:T(8,128)}, u32[]{:S(2)}, u32[]{:S(2)}) collective-permute-start(f32[2,784,128]{2,1,0:T(8,128)S(1)} %collective-permute-done.4.refs_3_), channel_id=1, source_target_pairs={{0,32},{32,0},{64,96},{96,64},{128,160},{160,128},{192,224},{224,1... | collective-permute-start | bytes 2408456 | tf_op jit(solution)/shard_map/ppermute | solution.py:237
  85.5 2.1 %collective-permute-start.13 = (f32[2,784,128]{2,1,0:T(8,128)S(1)}, f32[2,784,128]{2,1,0:T(8,128)}, u32[]{:S(2)}, u32[]{:S(2)}) collective-permute-start(f32[2,784,128]{2,1,0:T(8,128)S(1)} %collective-permute-done.7.refs_4_), channel_id=1, source_target_pairs={{0,32},{32,0},{64,96},{96,64},{128,160},{160,128},{192,224},{224,1... | collective-permute-start | bytes 2408456 | tf_op jit(solution)/shard_map/ppermute | solution.py:237
  87.6 7.3 %collective-permute-done.14.refs_17_ = f32[512,256]{1,0:T(8,128)S(1)} collective-permute-done((f32[512,256]{1,0:T(8,128)S(1)}, f32[512,256]{1,0:T(8,128)S(1)}, u32[]{:S(2)}, u32[]{:S(2)}) %collective-permute-start.14) | collective-permute-done | bytes 524320 | tf_op jit(solution)/shard_map/ppermute | solution.py:216
  94.9 3.0 %collective-permute-start.15 = (f32[784,128]{1,0:T(8,128)}, f32[784,128]{1,0:T(8,128)}, u32[]{:S(2)}, u32[]{:S(2)}) collective-permute-start(f32[784,128]{1,0:T(8,128)} %collective-permute-done.10.refs_5_), channel_id=1, source_target_pairs={{0,32},{32,0},{64,96},{96,64},{128,160},{160,128},{192,224},{224,1... | collective-permute-start | bytes 1204232 | tf_op jit(solution)/shard_map/ppermute | solution.py:237
  98.0 0.7 pad_add_fusion.place
  98.6 1.0 collective-permute-done.15.refs_9_
  99.6 13.7 %shard_map.74 = f32[512,1024]{1,0:T(8,128)} custom-call(s32[11]{0:T(128)} %pad_add_fusion.place, f32[784,128]{1,0:T(8,128)} %get-tuple-element.14.refs_0_, f32[784,128]{1,0:T(8,128)} %copy-done, f32[2,784,128]{2,1,0:T(8,128)} %copy-done.2, f32[2,784,128]{2,1,0:T(8,128)} %copy-done.3, f32[2,784,128]{2,1,0:T(8,128)} %copy-done.1, ...), custom_call_target="tpu_custom_call" | custom-call | flops 6442450944 | bytes 13631488 | tf_op jit(solution)/shard_map/pallas_call | solution.py:168
  113.3 30.6 %all_to_all.5.terms = f32[4,128,1024]{2,1,0:T(8,128)} all-to-all(f32[4,128,1024]{2,1,0:T(8,128)} %bitcast.14), channel_id=1, replica_groups=mesh['row'=16,'col'=8,'layer'=4] {'layer'}, dimensions={0} | all-to-all | bytes 4194304 | tf_op jit(solution)/shard_map/all_to_all | solution.py:248
  143.9 2.6 %shard_map.75 = f32[128,1024]{1,0:T(8,128)} custom-call(s32[11]{0:T(128)} %pad_add_fusion.place, s32[8,16]{1,0:T(8,128)} %flags.1, f32[4,128,1024]{2,1,0:T(8,128)} %all_to_all.5.terms, f32[128,1024]{1,0:T(8,128)} %square.1), custom_call_target="tpu_custom_call" | custom-call | flops 1048576 | bytes 3145728 | tf_op jit(solution)/shard_map/pallas_call | solution.py:200
  (32 shorter events, 0.1 us)
Async XLA Ops:
  0.0 97.9 %copy-start.11 = (s32[8]{0:T(128)S(1)}, s32[8]{0:T(128)}, u32[]{:S(2)}) copy-start(s32[8]{0:T(128)} %constant.24.clone) | copy-start | bytes 100
  2.6 10.5 %collective-permute-start = (f32[784,128]{1,0:T(8,128)}, f32[784,128]{1,0:T(8,128)S(1)}, u32[]{:S(2)}, u32[]{:S(2)}) collective-permute-start(f32[784,128]{1,0:T(8,128)} %get-tuple-element.14.refs_0_), channel_id=1, source_target_pairs={{0,32},{32,0},{64,96},{96,64},{128,160},{160,128},{192,224},{224,1... | collective-permute-start | bytes 1204232 | tf_op jit(solution)/shard_map/ppermute | solution.py:225
  13.1 86.5 %copy-start = (f32[784,128]{1,0:T(8,128)}, f32[784,128]{1,0:T(8,128)S(1)}, u32[]{:S(2)}) copy-start(f32[784,128]{1,0:T(8,128)S(1)} %collective-permute-done.refs_1_) | copy-start | bytes 1204228
  14.3 22.0 %collective-permute-start.1 = (f32[2,784,128]{2,1,0:T(8,128)S(1)}, f32[2,784,128]{2,1,0:T(8,128)S(1)}, u32[]{:S(2)}, u32[]{:S(2)}) collective-permute-start(f32[2,784,128]{2,1,0:T(8,128)S(1)} %pad_maximum_fusion), channel_id=1, source_target_pairs={{0,64},{32,480},{64,128},{96,32},{128,192},{160,96},{192,256},{224... | collective-permute-start | bytes 2408456 | tf_op jit(solution)/shard_map/ppermute | solution.py:232
  19.5 13.3 %collective-permute-start.3 = (f32[512,256]{1,0:T(8,128)}, f32[512,256]{1,0:T(8,128)S(1)}, u32[]{:S(2)}, u32[]{:S(2)}) collective-permute-start(f32[512,256]{1,0:T(8,128)} %get-tuple-element.15.refs_10_), channel_id=1, source_target_pairs={{0,28},{4,0},{8,4},{12,8},{16,12},{20,16},{24,20},{28,24},{1,29},{... | collective-permute-start | bytes 1572872 | tf_op jit(solution)/shard_map/ppermute | solution.py:216
  24.7 11.7 %collective-permute-start.2 = (f32[512,256]{1,0:T(8,128)}, f32[512,256]{1,0:T(8,128)S(1)}, u32[]{:S(2)}, u32[]{:S(2)}) collective-permute-start(f32[512,256]{1,0:T(8,128)} %get-tuple-element.15.refs_10_), channel_id=1, source_target_pairs={{0,4},{4,8},{8,12},{12,16},{16,20},{20,24},{24,28},{28,0},{1,5},{5... | collective-permute-start | bytes 1572872 | tf_op jit(solution)/shard_map/ppermute | solution.py:216
  32.8 66.8 %copy-start.4 = (f32[512,256]{1,0:T(8,128)}, f32[512,256]{1,0:T(8,128)S(1)}, u32[]{:S(2)}) copy-start(f32[512,256]{1,0:T(8,128)S(1)} %collective-permute-done.3.refs_12_) | copy-start | bytes 1572868
  36.4 22.3 %copy-start.5 = (f32[512,256]{1,0:T(8,128)}, f32[512,256]{1,0:T(8,128)S(1)}, u32[]{:S(2)}) copy-start(f32[512,256]{1,0:T(8,128)S(1)} %collective-permute-done.2.refs_11_) | copy-start | bytes 1572868
  36.4 63.2 %copy-start.2 = (f32[2,784,128]{2,1,0:T(8,128)}, f32[2,784,128]{2,1,0:T(8,128)S(1)}, u32[]{:S(2)}) copy-start(f32[2,784,128]{2,1,0:T(8,128)S(1)} %collective-permute-done.1.refs_2_) | copy-start | bytes 2408452
  36.4 22.3 %collective-permute-start.4 = (f32[2,784,128]{2,1,0:T(8,128)S(1)}, f32[2,784,128]{2,1,0:T(8,128)S(1)}, u32[]{:S(2)}, u32[]{:S(2)}) collective-permute-start(f32[2,784,128]{2,1,0:T(8,128)S(1)} %collective-permute-done.1.refs_2_), channel_id=1, source_target_pairs={{0,64},{32,480},{64,128},{96,32},{128,192},{160,96},{192,256},{224... | collective-permute-start | bytes 2408456 | tf_op jit(solution)/shard_map/ppermute | solution.py:232
  43.2 12.3 %collective-permute-start.6 = (f32[512,256]{1,0:T(8,128)S(1)}, f32[512,256]{1,0:T(8,128)S(1)}, u32[]{:S(2)}, u32[]{:S(2)}) collective-permute-start(f32[512,256]{1,0:T(8,128)S(1)} %collective-permute-done.3.refs_12_), channel_id=1, source_target_pairs={{0,28},{4,0},{8,4},{12,8},{16,12},{20,16},{24,20},{28,24},{1,29},{... | collective-permute-start | bytes 1572872 | tf_op jit(solution)/shard_map/ppermute | solution.py:216
  45.2 13.4 %collective-permute-start.5 = (f32[512,256]{1,0:T(8,128)S(1)}, f32[512,256]{1,0:T(8,128)S(1)}, u32[]{:S(2)}, u32[]{:S(2)}) collective-permute-start(f32[512,256]{1,0:T(8,128)S(1)} %collective-permute-done.2.refs_11_), channel_id=1, source_target_pairs={{0,4},{4,8},{8,12},{12,16},{16,20},{20,24},{24,28},{28,0},{1,5},{5... | collective-permute-start | bytes 1572872 | tf_op jit(solution)/shard_map/ppermute | solution.py:216
  55.5 25.0 %copy-start.6 = (f32[512,256]{1,0:T(8,128)}, f32[512,256]{1,0:T(8,128)S(1)}, u32[]{:S(2)}) copy-start(f32[512,256]{1,0:T(8,128)S(1)} %collective-permute-done.6.refs_14_) | copy-start | bytes 1572868
  58.6 21.9 %copy-start.7 = (f32[512,256]{1,0:T(8,128)}, f32[512,256]{1,0:T(8,128)S(1)}, u32[]{:S(2)}) copy-start(f32[512,256]{1,0:T(8,128)S(1)} %collective-permute-done.5.refs_13_) | copy-start | bytes 1572868
  58.6 41.0 %copy-start.3 = (f32[2,784,128]{2,1,0:T(8,128)}, f32[2,784,128]{2,1,0:T(8,128)S(1)}, u32[]{:S(2)}) copy-start(f32[2,784,128]{2,1,0:T(8,128)S(1)} %collective-permute-done.4.refs_3_) | copy-start | bytes 2408452
  58.7 22.6 %collective-permute-start.7 = (f32[2,784,128]{2,1,0:T(8,128)S(1)}, f32[2,784,128]{2,1,0:T(8,128)S(1)}, u32[]{:S(2)}, u32[]{:S(2)}) collective-permute-start(f32[2,784,128]{2,1,0:T(8,128)S(1)} %collective-permute-done.4.refs_3_), channel_id=1, source_target_pairs={{0,64},{32,480},{64,128},{96,32},{128,192},{160,96},{192,256},{224... | collective-permute-start | bytes 2408456 | tf_op jit(solution)/shard_map/ppermute | solution.py:232
  62.3 16.3 %collective-permute-start.8 = (f32[512,256]{1,0:T(8,128)S(1)}, f32[512,256]{1,0:T(8,128)S(1)}, u32[]{:S(2)}, u32[]{:S(2)}) collective-permute-start(f32[512,256]{1,0:T(8,128)S(1)} %collective-permute-done.5.refs_13_), channel_id=1, source_target_pairs={{0,4},{4,8},{8,12},{12,16},{16,20},{20,24},{24,28},{28,0},{1,5},{5... | collective-permute-start | bytes 1572872 | tf_op jit(solution)/shard_map/ppermute | solution.py:216
  64.3 16.2 %collective-permute-start.9 = (f32[512,256]{1,0:T(8,128)S(1)}, f32[512,256]{1,0:T(8,128)S(1)}, u32[]{:S(2)}, u32[]{:S(2)}) collective-permute-start(f32[512,256]{1,0:T(8,128)S(1)} %collective-permute-done.6.refs_14_), channel_id=1, source_target_pairs={{0,28},{4,0},{8,4},{12,8},{16,12},{20,16},{24,20},{28,24},{1,29},{... | collective-permute-start | bytes 1572872 | tf_op jit(solution)/shard_map/ppermute | solution.py:216
  68.8 29.8 %collective-permute-start.11 = (f32[2,784,128]{2,1,0:T(8,128)S(1)}, f32[2,784,128]{2,1,0:T(8,128)}, u32[]{:S(2)}, u32[]{:S(2)}) collective-permute-start(f32[2,784,128]{2,1,0:T(8,128)S(1)} %collective-permute-done.1.refs_2_), channel_id=1, source_target_pairs={{0,32},{32,0},{64,96},{96,64},{128,160},{160,128},{192,224},{224,1... | collective-permute-start | bytes 2408456 | tf_op jit(solution)/shard_map/ppermute | solution.py:237
  78.5 16.3 %copy-start.8 = (f32[512,256]{1,0:T(8,128)}, f32[512,256]{1,0:T(8,128)S(1)}, u32[]{:S(2)}) copy-start(f32[512,256]{1,0:T(8,128)S(1)} %collective-permute-done.8.refs_15_) | copy-start | bytes 1572868
  78.6 16.3 %collective-permute-start.14 = (f32[512,256]{1,0:T(8,128)S(1)}, f32[512,256]{1,0:T(8,128)S(1)}, u32[]{:S(2)}, u32[]{:S(2)}) collective-permute-start(f32[512,256]{1,0:T(8,128)S(1)} %collective-permute-done.8.refs_15_), channel_id=1, source_target_pairs={{0,4},{4,8},{8,12},{12,16},{16,20},{20,24},{24,28},{28,0},{1,5},{5... | collective-permute-start | bytes 1572872 | tf_op jit(solution)/shard_map/ppermute | solution.py:216
  80.5 0.8 copy-start.9
  81.3 18.3 %copy-start.1 = (f32[2,784,128]{2,1,0:T(8,128)}, f32[2,784,128]{2,1,0:T(8,128)S(1)}, u32[]{:S(2)}) copy-start(f32[2,784,128]{2,1,0:T(8,128)S(1)} %collective-permute-done.7.refs_4_) | copy-start | bytes 2408452
  81.3 13.6 %collective-permute-start.10 = (f32[784,128]{1,0:T(8,128)S(1)}, f32[784,128]{1,0:T(8,128)}, u32[]{:S(2)}, u32[]{:S(2)}) collective-permute-start(f32[784,128]{1,0:T(8,128)S(1)} %slice_bitcast_fusion), channel_id=1, source_target_pairs={{0,64},{32,480},{64,128},{96,32},{128,192},{160,96},{192,256},{224... | collective-permute-start | bytes 1204232 | tf_op jit(solution)/shard_map/ppermute | solution.py:232
  83.2 15.4 %collective-permute-start.12 = (f32[2,784,128]{2,1,0:T(8,128)S(1)}, f32[2,784,128]{2,1,0:T(8,128)}, u32[]{:S(2)}, u32[]{:S(2)}) collective-permute-start(f32[2,784,128]{2,1,0:T(8,128)S(1)} %collective-permute-done.4.refs_3_), channel_id=1, source_target_pairs={{0,32},{32,0},{64,96},{96,64},{128,160},{160,128},{192,224},{224,1... | collective-permute-start | bytes 2408456 | tf_op jit(solution)/shard_map/ppermute | solution.py:237
  85.5 14.1 %collective-permute-start.13 = (f32[2,784,128]{2,1,0:T(8,128)S(1)}, f32[2,784,128]{2,1,0:T(8,128)}, u32[]{:S(2)}, u32[]{:S(2)}) collective-permute-start(f32[2,784,128]{2,1,0:T(8,128)S(1)} %collective-permute-done.7.refs_4_), channel_id=1, source_target_pairs={{0,32},{32,0},{64,96},{96,64},{128,160},{160,128},{192,224},{224,1... | collective-permute-start | bytes 2408456 | tf_op jit(solution)/shard_map/ppermute | solution.py:237
  94.9 3.0 %copy-start.10 = (f32[512,256]{1,0:T(8,128)}, f32[512,256]{1,0:T(8,128)S(1)}, u32[]{:S(2)}) copy-start(f32[512,256]{1,0:T(8,128)S(1)} %collective-permute-done.14.refs_17_) | copy-start | bytes 1572868
  94.9 4.7 %collective-permute-start.15 = (f32[784,128]{1,0:T(8,128)}, f32[784,128]{1,0:T(8,128)}, u32[]{:S(2)}, u32[]{:S(2)}) collective-permute-start(f32[784,128]{1,0:T(8,128)} %collective-permute-done.10.refs_5_), channel_id=1, source_target_pairs={{0,32},{32,0},{64,96},{96,64},{128,160},{160,128},{192,224},{224,1... | collective-permute-start | bytes 1204232 | tf_op jit(solution)/shard_map/ppermute | solution.py:237

commit v6 on v5

v6 whole, which is shorter than its diff:
```python
import functools

import jax
import jax.numpy as jnp
from jax import lax
from jax.experimental import pallas as pl
from jax.experimental.pallas import tpu as pltpu
from jax.sharding import PartitionSpec as P

BS = 64
LANES = 128
MAIN = 24
EXTRA = 8
META = 16
PACKED = META + 6 * LANES
BF = jnp.bfloat16
F32 = jnp.float32


def lane_half():
    return lax.broadcasted_iota(jnp.int32, (BS, LANES), 1) // BS


def pair_mask(low, high):
    return jnp.where(lane_half() == 0, low.astype(F32), high.astype(F32))


def prepare_kernel(left_flags, left, flags, x, left_out, out, holes):
    for i in range(8):
        for c in range(2):
            mask = pair_mask(left_flags[2 * c, i], left_flags[2 * c + 1, i])
            at = (pl.ds(i * BS, BS), pl.ds(c * LANES, LANES))
            left_out[at] = left[at] * mask
    for c in range(6):
        out[pl.ds(META + c * LANES, LANES), :] = x[:, pl.ds(c * LANES, LANES)]
    count = jnp.int32(0)
    for s in range(MAIN):
        holes[count] = s
        count = count + jnp.where(flags[(s >> 1) & 1, 2 * (s >> 2) + (s & 1)] == 0, 1, 0)
    used = jnp.int32(0)
    half = lane_half()
    lane = lax.broadcasted_iota(jnp.int32, (1, LANES), 1)
    row = jnp.zeros((1, LANES), F32)
    for e in range(EXTRA):
        kept = flags[e >> 2, 12 + (e & 3)] != 0
        slot = holes[jnp.minimum(used, EXTRA)]
        row = jnp.where(lane == e, jnp.where(kept, slot, -1).astype(F32), row)
        used = used + jnp.where(kept, 1, 0)

        @pl.when(kept)
        def _():
            at = pl.ds(pl.multiple_of(META + (slot >> 1) * BS, 16), BS)
            block = x[pl.ds((e >> 2) * BS, BS), pl.ds((6 + ((e >> 1) & 1)) * LANES, LANES)]
            side = slot & 1
            block = jnp.where(side == (e & 1), block, pltpu.roll(block, BS, 1))
            out[at, :] = jnp.where(half == side, block, out[at, :])

    out[pl.ds(0, 1), :] = row
    for c in range(6):
        for b in range(2):
            mask = jnp.where(lane < BS, flags[b, 2 * c].astype(F32), flags[b, 2 * c + 1].astype(F32))
            out[pl.ds(1 + c * 2 + b, 1), :] = mask
    out[pl.ds(13, 3), :] = jnp.zeros((3, LANES), F32)


def prepare(left, left_flags, right, right_flags):
    smem = pl.BlockSpec(memory_space=pltpu.SMEM)
    vmem = pl.BlockSpec(memory_space=pltpu.VMEM)
    return pl.pallas_call(
        prepare_kernel,
        out_shape=(jax.ShapeDtypeStruct(left.shape, F32), jax.ShapeDtypeStruct((PACKED, LANES), F32)),
        in_specs=[smem, vmem, smem, vmem],
        out_specs=(vmem, vmem),
        scratch_shapes=[pltpu.SMEM((MAIN + 1,), jnp.int32)],
    )(left_flags, left, right_flags, right)


def split(x):
    high = x.astype(BF)
    return high, (x - high.astype(F32)).astype(BF)


def product_kernel(side, place, left, *refs):
    items = refs[:10]
    out, tiles, lefts, rights, homes, tile_sems, home_sems, left_sems = refs[10:]
    need = tiles.shape[2]
    z, core = place[0], place[1]
    other = 1 - core
    toward = 2 * core - 1

    def tile_copy(source, n, parity):
        return pltpu.make_async_copy(source.at[pl.ds(0, need)], tiles.at[n, parity], tile_sems.at[n, parity])

    def home_copy(source, n, parity):
        return pltpu.make_async_copy(source.at[pl.ds(0, 1)], homes.at[n, parity], home_sems.at[n, parity])

    def left_copy(n, chip):
        return pltpu.make_async_copy(left.at[chip], lefts.at[n], left_sems.at[n])

    own, swapped, rings, trades = items[0], items[1], items[2:6], items[6:10]
    chunks = [(0, (own, core), (swapped, other))]
    for s in range(3):
        chunks.append(((s + 1) * toward, (rings[s].at[0], core), (rings[s].at[1], other)))
        chunks.append((-(s + 1) * toward, (trades[s].at[0], other), (trades[s].at[1], core)))
    chunks.append((4, (rings[3], core), (trades[3], other)))
    for n, (by, *pieces) in enumerate(chunks):
        for ref, parity in pieces:
            if side:
                home_copy(ref, n, parity).start()
            tile_copy(ref, n, parity).start()
        left_copy(n, (z + by + 8) & 7).start()
    half = lane_half()

    def unpack(n, slot):
        for parity in range(2):
            tile_copy(own, n, parity).wait()
            if side:
                home_copy(own, n, parity).wait()
        for parity in range(2):
            for b in range(2):
                for c in range(4):
                    pair = 4 * side + c
                    if pair < 6:
                        mask = tiles[n, parity, pl.ds(1 + pair * 2 + b, 1), :]
                        value = tiles[n, parity, pl.ds(META + pair * LANES + b * BS, BS), :] * mask
                    else:
                        halves = []
                        for h in range(2):
                            home = homes[n, parity, 0, b * 4 + 2 * (pair - 6) + h].astype(jnp.int32)
                            kept = home >= 0
                            home = jnp.maximum(home, 0)
                            block = tiles[n, parity, pl.ds(pl.multiple_of(META + (home >> 1) * BS, 16), BS), :]
                            block = jnp.where((home & 1) == h, block, pltpu.roll(block, BS, 1))
                            halves.append(jnp.where(kept, block, 0.0))
                        value = jnp.where(half == 0, halves[0], halves[1])
                    high, low = split(value)
                    row, columns = parity * LANES + b * BS, pl.ds(c * LANES, LANES)
                    rights[slot, pl.ds(row, BS), columns] = high
                    rights[slot, pl.ds(256 + row, BS), columns] = high
                    rights[slot, pl.ds(512 + row, BS), columns] = low

    def multiply(n, slot):
        high, low = split(lefts[n])
        return jnp.dot(jnp.concatenate([low, high, high], 1), rights[slot], preferred_element_type=F32)

    unpack(0, 0)
    for n in range(8):
        left_copy(n, 0).wait()
        if n < 7:
            unpack(n + 1, (n + 1) % 2)
        total = multiply(n, n % 2)
        out[...] = total + out[...] if n else total


def product(side, place, left, items):
    smem = pl.BlockSpec(memory_space=pltpu.SMEM)
    hbm = pl.BlockSpec(memory_space=pltpu.HBM)
    need = PACKED if side else META + 4 * LANES
    return pl.pallas_call(
        functools.partial(product_kernel, side),
        out_shape=jax.ShapeDtypeStruct((512, 512), F32),
        in_specs=[smem] + [hbm] * 11,
        out_specs=pl.BlockSpec(memory_space=pltpu.VMEM),
        scratch_shapes=[
            pltpu.VMEM((8, 2, need, LANES), F32),
            pltpu.VMEM((8, 512, 256), F32),
            pltpu.VMEM((2, 768, 512), BF),
            pltpu.SMEM((8, 2, 1, LANES), F32),
            pltpu.SemaphoreType.DMA((8, 2)),
            pltpu.SemaphoreType.DMA((8, 2)),
            pltpu.SemaphoreType.DMA((8,)),
        ],
        cost_estimate=pl.CostEstimate(flops=6 * 512 * 512 * 2048, bytes_accessed=10 << 20, transcendentals=0),
        compiler_params=pltpu.CompilerParams(vmem_limit_bytes=56 << 20),
    )(place, left, *items)


def finish_kernel(side, place, flags, terms, square, *refs):
    out = refs[-1]
    for b in range(2):
        for c in range(4):
            at = (pl.ds(b * BS, BS), pl.ds(c * LANES, LANES))
            total = (terms[(0,) + at] + terms[(1,) + at]) + (terms[(2,) + at] + terms[(3,) + at])
            line, column = place[2] * 2 + b, 8 * side + 2 * c
            mask = pair_mask(flags[line, column], flags[line, column + 1])
            out[at] = mask * (3.0 * square[at] - 2.0 * total)


def finish(side, terms, square, flags, place, *before):
    smem = pl.BlockSpec(memory_space=pltpu.SMEM)
    half = pl.BlockSpec((128, 512), lambda i: (0, side))
    return pl.pallas_call(
        functools.partial(finish_kernel, side),
        out_shape=jax.ShapeDtypeStruct(square.shape, F32),
        grid=(1,),
        in_specs=[smem, smem, pl.BlockSpec((4, 128, 512), lambda i: (0, 0, 0)), half]
        + [pl.BlockSpec(memory_space=pltpu.HBM)] * len(before),
        out_specs=half,
        input_output_aliases={4: 0} if before else {},
        cost_estimate=pl.CostEstimate(flops=1 << 20, bytes_accessed=2 << 20, transcendentals=0),
        compiler_params=pltpu.CompilerParams(vmem_limit_bytes=56 << 20),
    )(place, flags, terms, square, *before)


def gather_right(own):
    ring = [(2 * z + c, 2 * ((z + 1 - 2 * c) % 8) + c) for z in range(8) for c in range(2)]
    trade = [(i, i ^ 1) for i in range(16)]
    swapped = lax.ppermute(own, "row", trade)
    rings, pair = [], jnp.stack([own, swapped])
    for step in range(4):
        pair = lax.ppermute(pair if step < 3 else pair[0], "row", ring)
        rings.append(pair)
    return [own, swapped] + rings + [lax.ppermute(pair, "row", trade) for pair in rings]


def local(left_slab, right_window, left_pattern, right_pattern, square_blocks, result_pattern):
    left, packed = prepare(left_slab[0], left_pattern[0].T, right_window[0], right_pattern[0])
    left = lax.all_gather(left, "col", axis=0, tiled=False)
    items = gather_right(packed)
    row, layer = lax.axis_index("row"), lax.axis_index("layer")
    place = jnp.stack([row >> 1, row & 1, layer])
    out = ()
    for side in range(2):
        cube = product(side, place, left, items)
        terms = lax.all_to_all(cube.reshape(4, 128, 512), "layer", 0, 0)
        out = (finish(side, terms, square_blocks, result_pattern, place, *out),)
    return out[0]


def solution(mesh):
    in_specs = (
        P("layer", "row", "col"),
        P("layer", "row", "col"),
        P("layer", "row", "col"),
        P("layer", "row", "col"),
        P(("row", "layer"), "col"),
        P("row", "col"),
    )
    out_specs = P(("row", "layer"), "col")
    return jax.shard_map(local, mesh=mesh, in_specs=in_specs, out_specs=out_specs, check_vma=False)
```

time: 147 us -> 137 us (0.932)
  the two profiles are of different devices: /device:TPU:1 before, /device:TPU:48 now
where the time goes in v6:
time: 137 us
  waiting for transfers between devices  68.4 us (50%)
  starting transfers between devices  28.5 us (21%)
  Pallas kernels  23.3 us (17%)
  between operations  13.6 us (10%)
  other arithmetic  1.79 us (1%)
    ppermute x4, waiting for transfers between devices, gather_right(): pair = lax.ppermute(pair if step < 3 else pair[0], 'row', ring)  45.6 us
    all_to_all x2, waiting for transfers between devices, local(): terms = lax.all_to_all(cube.reshape(4, 128, 512), 'layer', 0, 0)  19.6 us
    pallas_call x2, Pallas kernels, product(): pl.pallas_call(functools.partial(product_kernel, side), out_shape=jax.Sha...  16.4 us
    ppermute x4, starting transfers between devices, gather_right(): pair = lax.ppermute(pair if step < 3 else pair[0], 'row', ring)  9.88 us
    ppermute x4, starting transfers between devices, gather_right(): lax.ppermute(pair, 'row', trade)  8.92 us
    all_to_all x2, starting transfers between devices, local(): terms = lax.all_to_all(cube.reshape(4, 128, 512), 'layer', 0, 0)  7.81 us
    pallas_call x2, Pallas kernels, finish(): pl.pallas_call(functools.partial(finish_kernel, side), out_shape=jax.Shap...  4.14 us
    pallas_call x1, Pallas kernels, prepare(): pl.pallas_call(prepare_kernel, out_shape=(jax.ShapeDtypeStruct(left.shape...  2.78 us
  transfers between devices with their start and end apart: 12, of which 8 were waited for; matrix products, arithmetic and copies ran while one was open for 1% of the time, Pallas kernels for 8%

profile of v6, /device:TPU:48, one launch (start us, length us, event | category | flops | bytes accessed | tf_op | source)
XLA Modules:
  0.0 136.6 jit_solution(3157549149214396162)
XLA Ops:
  6.5 2.8 %shard_map.64 = (f32[512,256]{1,0:T(8,128)}, f32[784,128]{1,0:T(8,128)}) custom-call(s32[4,8]{1,0:T(4,128)} %bitcast.22, f32[512,256]{1,0:T(8,128)} %bitcast.18, s32[2,16]{1,0:T(2,128)} %bitcast.23, f32[128,1024]{1,0:T(8,128)} %bitcast.19), custom_call_target="tpu_custom_call" | custom-call | tf_op jit(solution)/shard_map/pallas_call | solution.py:69
  9.3 0.0 all-gather.3.cloned.1.call-update
  9.3 1.9 %collective-permute-start = (f32[784,128]{1,0:T(8,128)}, f32[784,128]{1,0:T(8,128)S(1)}, u32[]{:S(2)}, u32[]{:S(2)}) collective-permute-start(f32[784,128]{1,0:T(8,128)} %get-tuple-element.8.refs_0_), channel_id=1, source_target_pairs={{0,32},{32,0},{64,96},{96,64},{128,160},{160,128},{192,224},{224,1... | collective-permute-start | bytes 1204232 | tf_op jit(solution)/shard_map/ppermute | solution.py:208
  11.3 1.9 %collective-permute-done.refs_1_ = f32[784,128]{1,0:T(8,128)S(1)} collective-permute-done((f32[784,128]{1,0:T(8,128)}, f32[784,128]{1,0:T(8,128)S(1)}, u32[]{:S(2)}, u32[]{:S(2)}) %collective-permute-start) | collective-permute-done | bytes 401440 | tf_op jit(solution)/shard_map/ppermute | solution.py:208
  13.2 1.2 pad_maximum_fusion
  14.4 4.1 %collective-permute-start.1 = (f32[2,784,128]{2,1,0:T(8,128)S(1)}, f32[2,784,128]{2,1,0:T(8,128)S(1)}, u32[]{:S(2)}, u32[]{:S(2)}) collective-permute-start(f32[2,784,128]{2,1,0:T(8,128)S(1)} %pad_maximum_fusion), channel_id=1, source_target_pairs={{0,64},{32,480},{64,128},{96,32},{128,192},{160,96},{192,256},{224... | collective-permute-start | bytes 2408456 | tf_op jit(solution)/shard_map/ppermute | solution.py:211
  18.5 16.9 %collective-permute-done.1.refs_2_ = f32[2,784,128]{2,1,0:T(8,128)S(1)} collective-permute-done((f32[2,784,128]{2,1,0:T(8,128)S(1)}, f32[2,784,128]{2,1,0:T(8,128)S(1)}, u32[]{:S(2)}, u32[]{:S(2)}) %collective-permute-start.1) | collective-permute-done | bytes 802848 | tf_op jit(solution)/shard_map/ppermute | solution.py:211
  35.5 1.9 %collective-permute-start.2 = (f32[2,784,128]{2,1,0:T(8,128)S(1)}, f32[2,784,128]{2,1,0:T(8,128)S(1)}, u32[]{:S(2)}, u32[]{:S(2)}) collective-permute-start(f32[2,784,128]{2,1,0:T(8,128)S(1)} %collective-permute-done.1.refs_2_), channel_id=1, source_target_pairs={{0,64},{32,480},{64,128},{96,32},{128,192},{160,96},{192,256},{224... | collective-permute-start | bytes 2408456 | tf_op jit(solution)/shard_map/ppermute | solution.py:211
  37.4 13.3 %collective-permute-done.2.refs_3_ = f32[2,784,128]{2,1,0:T(8,128)S(1)} collective-permute-done((f32[2,784,128]{2,1,0:T(8,128)S(1)}, f32[2,784,128]{2,1,0:T(8,128)S(1)}, u32[]{:S(2)}, u32[]{:S(2)}) %collective-permute-start.2) | collective-permute-done | bytes 802848 | tf_op jit(solution)/shard_map/ppermute | solution.py:211
  50.7 1.9 %collective-permute-start.3 = (f32[2,784,128]{2,1,0:T(8,128)S(1)}, f32[2,784,128]{2,1,0:T(8,128)S(1)}, u32[]{:S(2)}, u32[]{:S(2)}) collective-permute-start(f32[2,784,128]{2,1,0:T(8,128)S(1)} %collective-permute-done.2.refs_3_), channel_id=1, source_target_pairs={{0,64},{32,480},{64,128},{96,32},{128,192},{160,96},{192,256},{224... | collective-permute-start | bytes 2408456 | tf_op jit(solution)/shard_map/ppermute | solution.py:211
  52.7 2.7 %collective-permute-start.5 = (f32[2,784,128]{2,1,0:T(8,128)S(1)}, f32[2,784,128]{2,1,0:T(8,128)}, u32[]{:S(2)}, u32[]{:S(2)}) collective-permute-start(f32[2,784,128]{2,1,0:T(8,128)S(1)} %collective-permute-done.1.refs_2_), channel_id=1, source_target_pairs={{0,32},{32,0},{64,96},{96,64},{128,160},{160,128},{192,224},{224,1... | collective-permute-start | bytes 2408456 | tf_op jit(solution)/shard_map/ppermute | solution.py:213
  55.3 10.7 %collective-permute-done.3.refs_4_ = f32[2,784,128]{2,1,0:T(8,128)S(1)} collective-permute-done((f32[2,784,128]{2,1,0:T(8,128)S(1)}, f32[2,784,128]{2,1,0:T(8,128)S(1)}, u32[]{:S(2)}, u32[]{:S(2)}) %collective-permute-start.3) | collective-permute-done | bytes 802848 | tf_op jit(solution)/shard_map/ppermute | solution.py:211
  66.0 1.9 %collective-permute-start.4 = (f32[784,128]{1,0:T(8,128)S(1)}, f32[784,128]{1,0:T(8,128)S(1)}, u32[]{:S(2)}, u32[]{:S(2)}) collective-permute-start(f32[784,128]{1,0:T(8,128)S(1)} %slice_bitcast_fusion), channel_id=1, source_target_pairs={{0,64},{32,480},{64,128},{96,32},{128,192},{160,96},{192,256},{224... | collective-permute-start | bytes 1204232 | tf_op jit(solution)/shard_map/ppermute | solution.py:211
  68.0 1.9 %collective-permute-start.6 = (f32[2,784,128]{2,1,0:T(8,128)S(1)}, f32[2,784,128]{2,1,0:T(8,128)}, u32[]{:S(2)}, u32[]{:S(2)}) collective-permute-start(f32[2,784,128]{2,1,0:T(8,128)S(1)} %collective-permute-done.2.refs_3_), channel_id=1, source_target_pairs={{0,32},{32,0},{64,96},{96,64},{128,160},{160,128},{192,224},{224,1... | collective-permute-start | bytes 2408456 | tf_op jit(solution)/shard_map/ppermute | solution.py:213
  69.9 2.4 %collective-permute-start.7 = (f32[2,784,128]{2,1,0:T(8,128)S(1)}, f32[2,784,128]{2,1,0:T(8,128)}, u32[]{:S(2)}, u32[]{:S(2)}) collective-permute-start(f32[2,784,128]{2,1,0:T(8,128)S(1)} %collective-permute-done.3.refs_4_), channel_id=1, source_target_pairs={{0,32},{32,0},{64,96},{96,64},{128,160},{160,128},{192,224},{224,1... | collective-permute-start | bytes 2408456 | tf_op jit(solution)/shard_map/ppermute | solution.py:213
  72.3 4.7 %collective-permute-done.4.refs_5_ = f32[784,128]{1,0:T(8,128)S(1)} collective-permute-done((f32[784,128]{1,0:T(8,128)S(1)}, f32[784,128]{1,0:T(8,128)S(1)}, u32[]{:S(2)}, u32[]{:S(2)}) %collective-permute-start.4) | collective-permute-done | bytes 401440 | tf_op jit(solution)/shard_map/ppermute | solution.py:211
  77.0 1.9 %collective-permute-start.8 = (f32[784,128]{1,0:T(8,128)S(1)}, f32[784,128]{1,0:T(8,128)}, u32[]{:S(2)}, u32[]{:S(2)}) collective-permute-start(f32[784,128]{1,0:T(8,128)S(1)} %collective-permute-done.4.refs_5_), channel_id=1, source_target_pairs={{0,32},{32,0},{64,96},{96,64},{128,160},{160,128},{192,224},{224,1... | collective-permute-start | bytes 1204232 | tf_op jit(solution)/shard_map/ppermute | solution.py:213
  78.9 0.6 pad_add_fusion.place
  79.5 0.0 collective-permute-done.5.refs_6_
  79.5 0.0 collective-permute-done.6.refs_7_
  79.5 1.2 collective-permute-done.8.refs_9_
  80.8 0.0 collective-permute-done.7.refs_8_
  80.8 0.0 copy-done.2
  80.8 8.2 %shard_map.66 = f32[512,512]{1,0:T(8,128)} custom-call(s32[3]{0:T(128)} %pad_add_fusion.place, f32[8,512,256]{2,1,0:T(8,128)} %bitcast.24, f32[784,128]{1,0:T(8,128)} %get-tuple-element.8.refs_0_, f32[784,128]{1,0:T(8,128)} %copy-done.2, f32[2,784,128]{2,1,0:T(8,128)} %copy-done.4, f32[2,784,128]{2,1,0:T(8,128)} %copy-done.5, f32[2,784,128]{2,1,0:T(8,128)} %copy-done.3, ...), custom_call_target="tpu_custom_call" | custom-call | flops 3221225472 | bytes 10485760 | tf_op jit(solution)/shard_map/pallas_call | solution.py:159
  89.0 4.3 %all-to-all-start.1 = ((f32[4,128,512]{2,1,0:T(8,128)}), f32[4,128,512]{2,1,0:T(8,128)S(1)}, u32[]{:S(2)}, u32[]{:S(2)}) async-start(f32[4,128,512]{2,1,0:T(8,128)} %bitcast.17), calls=%async_computation.1 | async-start | bytes 2097152 | tf_op jit(solution)/shard_map/all_to_all | solution.py:225
  93.3 8.2 %shard_map.65 = f32[512,512]{1,0:T(8,128)} custom-call(s32[3]{0:T(128)} %pad_add_fusion.place, f32[8,512,256]{2,1,0:T(8,128)} %bitcast.25, f32[784,128]{1,0:T(8,128)} %get-tuple-element.8.refs_0_, f32[784,128]{1,0:T(8,128)} %copy-done.2, f32[2,784,128]{2,1,0:T(8,128)} %copy-done.4, f32[2,784,128]{2,1,0:T(8,128)} %copy-done.5, f32[2,784,128]{2,1,0:T(8,128)} %copy-done.3, ...), custom_call_target="tpu_custom_call" | custom-call | flops 3221225472 | bytes 10485760 | tf_op jit(solution)/shard_map/pallas_call | solution.py:159
  101.5 7.2 %all-to-all-done.1.terms = f32[4,128,512]{2,1,0:T(8,128)S(1)} async-done(((f32[4,128,512]{2,1,0:T(8,128)}), f32[4,128,512]{2,1,0:T(8,128)S(1)}, u32[]{:S(2)}, u32[]{:S(2)}) %all-to-all-start.1) | async-done | bytes 1048608 | tf_op jit(solution)/shard_map/all_to_all | solution.py:225
  108.7 3.5 %all-to-all-start = ((f32[4,128,512]{2,1,0:T(8,128)}), f32[4,128,512]{2,1,0:T(8,128)S(1)}, u32[]{:S(2)}, u32[]{:S(2)}) async-start(f32[4,128,512]{2,1,0:T(8,128)} %bitcast.16), calls=%async_computation | async-start | bytes 2097152 | tf_op jit(solution)/shard_map/all_to_all | solution.py:225
  112.2 2.1 %shard_map.67.refs_0_ = f32[128,1024]{1,0:T(8,128)} custom-call(s32[3]{0:T(128)} %pad_add_fusion.place, s32[8,16]{1,0:T(8,128)} %flags.3, f32[4,128,512]{2,1,0:T(8,128)} %copy-done, f32[128,1024]{1,0:T(8,128)} %square.3), custom_call_target="tpu_custom_call" | custom-call | flops 1048576 | bytes 2097152 | tf_op jit(solution)/shard_map/pallas_call | solution.py:192
  114.3 12.4 %all-to-all-done.terms = f32[4,128,512]{2,1,0:T(8,128)S(1)} async-done(((f32[4,128,512]{2,1,0:T(8,128)}), f32[4,128,512]{2,1,0:T(8,128)S(1)}, u32[]{:S(2)}, u32[]{:S(2)}) %all-to-all-start) | async-done | bytes 1048608 | tf_op jit(solution)/shard_map/all_to_all | solution.py:225
  126.7 1.0 copy-done.1
  127.7 2.1 %shard_map.68 = f32[128,1024]{1,0:T(8,128)} custom-call(s32[3]{0:T(128)} %pad_add_fusion.place, s32[8,16]{1,0:T(8,128)} %flags.3, f32[4,128,512]{2,1,0:T(8,128)} %copy-done.1, f32[128,1024]{1,0:T(8,128)} %square.3, f32[128,1024]{1,0:T(8,128)} %shard_map.67.refs_0_), custom_call_target="tpu_custom_call", output_to_operand_aliasing={{}: (4, {})} | custom-call | flops 1048576 | bytes 2097152 | tf_op jit(solution)/shard_map/pallas_call | solution.py:192
  (15 shorter events, 0.1 us)
Async XLA Ops:
  6.5 74.2 %all-gather.3.cloned.1.call-start = ((), (), s32[]{:S(2)}) async-start(), calls=%async_computation.2 | async-start | bytes 4718592 | tf_op jit(solution)/shard_map/all_gather | solution.py:218
  9.3 3.8 %collective-permute-start = (f32[784,128]{1,0:T(8,128)}, f32[784,128]{1,0:T(8,128)S(1)}, u32[]{:S(2)}, u32[]{:S(2)}) collective-permute-start(f32[784,128]{1,0:T(8,128)} %get-tuple-element.8.refs_0_), channel_id=1, source_target_pairs={{0,32},{32,0},{64,96},{96,64},{128,160},{160,128},{192,224},{224,1... | collective-permute-start | bytes 1204232 | tf_op jit(solution)/shard_map/ppermute | solution.py:208
  13.2 67.6 %copy-start.2 = (f32[784,128]{1,0:T(8,128)}, f32[784,128]{1,0:T(8,128)S(1)}, u32[]{:S(2)}) copy-start(f32[784,128]{1,0:T(8,128)S(1)} %collective-permute-done.refs_1_) | copy-start | bytes 1204228
  14.4 21.1 %collective-permute-start.1 = (f32[2,784,128]{2,1,0:T(8,128)S(1)}, f32[2,784,128]{2,1,0:T(8,128)S(1)}, u32[]{:S(2)}, u32[]{:S(2)}) collective-permute-start(f32[2,784,128]{2,1,0:T(8,128)S(1)} %pad_maximum_fusion), channel_id=1, source_target_pairs={{0,64},{32,480},{64,128},{96,32},{128,192},{160,96},{192,256},{224... | collective-permute-start | bytes 2408456 | tf_op jit(solution)/shard_map/ppermute | solution.py:211
  35.5 45.3 %copy-start.4 = (f32[2,784,128]{2,1,0:T(8,128)}, f32[2,784,128]{2,1,0:T(8,128)S(1)}, u32[]{:S(2)}) copy-start(f32[2,784,128]{2,1,0:T(8,128)S(1)} %collective-permute-done.1.refs_2_) | copy-start | bytes 2408452
  35.5 15.3 %collective-permute-start.2 = (f32[2,784,128]{2,1,0:T(8,128)S(1)}, f32[2,784,128]{2,1,0:T(8,128)S(1)}, u32[]{:S(2)}, u32[]{:S(2)}) collective-permute-start(f32[2,784,128]{2,1,0:T(8,128)S(1)} %collective-permute-done.1.refs_2_), channel_id=1, source_target_pairs={{0,64},{32,480},{64,128},{96,32},{128,192},{160,96},{192,256},{224... | collective-permute-start | bytes 2408456 | tf_op jit(solution)/shard_map/ppermute | solution.py:211
  50.7 30.0 %copy-start.5 = (f32[2,784,128]{2,1,0:T(8,128)}, f32[2,784,128]{2,1,0:T(8,128)S(1)}, u32[]{:S(2)}) copy-start(f32[2,784,128]{2,1,0:T(8,128)S(1)} %collective-permute-done.2.refs_3_) | copy-start | bytes 2408452
  50.7 15.3 %collective-permute-start.3 = (f32[2,784,128]{2,1,0:T(8,128)S(1)}, f32[2,784,128]{2,1,0:T(8,128)S(1)}, u32[]{:S(2)}, u32[]{:S(2)}) collective-permute-start(f32[2,784,128]{2,1,0:T(8,128)S(1)} %collective-permute-done.2.refs_3_), channel_id=1, source_target_pairs={{0,64},{32,480},{64,128},{96,32},{128,192},{160,96},{192,256},{224... | collective-permute-start | bytes 2408456 | tf_op jit(solution)/shard_map/ppermute | solution.py:211
  52.7 26.9 %collective-permute-start.5 = (f32[2,784,128]{2,1,0:T(8,128)S(1)}, f32[2,784,128]{2,1,0:T(8,128)}, u32[]{:S(2)}, u32[]{:S(2)}) collective-permute-start(f32[2,784,128]{2,1,0:T(8,128)S(1)} %collective-permute-done.1.refs_2_), channel_id=1, source_target_pairs={{0,32},{32,0},{64,96},{96,64},{128,160},{160,128},{192,224},{224,1... | collective-permute-start | bytes 2408456 | tf_op jit(solution)/shard_map/ppermute | solution.py:213
  66.0 14.8 %copy-start.3 = (f32[2,784,128]{2,1,0:T(8,128)}, f32[2,784,128]{2,1,0:T(8,128)S(1)}, u32[]{:S(2)}) copy-start(f32[2,784,128]{2,1,0:T(8,128)S(1)} %collective-permute-done.3.refs_4_) | copy-start | bytes 2408452
  66.0 11.0 %collective-permute-start.4 = (f32[784,128]{1,0:T(8,128)S(1)}, f32[784,128]{1,0:T(8,128)S(1)}, u32[]{:S(2)}, u32[]{:S(2)}) collective-permute-start(f32[784,128]{1,0:T(8,128)S(1)} %slice_bitcast_fusion), channel_id=1, source_target_pairs={{0,64},{32,480},{64,128},{96,32},{128,192},{160,96},{192,256},{224... | collective-permute-start | bytes 1204232 | tf_op jit(solution)/shard_map/ppermute | solution.py:211
  68.0 11.6 %collective-permute-start.6 = (f32[2,784,128]{2,1,0:T(8,128)S(1)}, f32[2,784,128]{2,1,0:T(8,128)}, u32[]{:S(2)}, u32[]{:S(2)}) collective-permute-start(f32[2,784,128]{2,1,0:T(8,128)S(1)} %collective-permute-done.2.refs_3_), channel_id=1, source_target_pairs={{0,32},{32,0},{64,96},{96,64},{128,160},{160,128},{192,224},{224,1... | collective-permute-start | bytes 2408456 | tf_op jit(solution)/shard_map/ppermute | solution.py:213
  69.9 10.9 %collective-permute-start.7 = (f32[2,784,128]{2,1,0:T(8,128)S(1)}, f32[2,784,128]{2,1,0:T(8,128)}, u32[]{:S(2)}, u32[]{:S(2)}) collective-permute-start(f32[2,784,128]{2,1,0:T(8,128)S(1)} %collective-permute-done.3.refs_4_), channel_id=1, source_target_pairs={{0,32},{32,0},{64,96},{96,64},{128,160},{160,128},{192,224},{224,1... | collective-permute-start | bytes 2408456 | tf_op jit(solution)/shard_map/ppermute | solution.py:213
  77.0 3.8 %copy-start.6 = (f32[784,128]{1,0:T(8,128)}, f32[784,128]{1,0:T(8,128)S(1)}, u32[]{:S(2)}) copy-start(f32[784,128]{1,0:T(8,128)S(1)} %collective-permute-done.4.refs_5_) | copy-start | bytes 1204228
  77.0 3.7 %collective-permute-start.8 = (f32[784,128]{1,0:T(8,128)S(1)}, f32[784,128]{1,0:T(8,128)}, u32[]{:S(2)}, u32[]{:S(2)}) collective-permute-start(f32[784,128]{1,0:T(8,128)S(1)} %collective-permute-done.4.refs_5_), channel_id=1, source_target_pairs={{0,32},{32,0},{64,96},{96,64},{128,160},{160,128},{192,224},{224,1... | collective-permute-start | bytes 1204232 | tf_op jit(solution)/shard_map/ppermute | solution.py:213
  89.0 19.7 %all-to-all-start.1 = ((f32[4,128,512]{2,1,0:T(8,128)}), f32[4,128,512]{2,1,0:T(8,128)S(1)}, u32[]{:S(2)}, u32[]{:S(2)}) async-start(f32[4,128,512]{2,1,0:T(8,128)} %bitcast.17), calls=%async_computation.1 | async-start | bytes 2097152 | tf_op jit(solution)/shard_map/all_to_all | solution.py:225
  108.7 3.5 %copy-start = (f32[4,128,512]{2,1,0:T(8,128)}, f32[4,128,512]{2,1,0:T(8,128)S(1)}, u32[]{:S(2)}) copy-start(f32[4,128,512]{2,1,0:T(8,128)S(1)} %all-to-all-done.1.terms) | copy-start | bytes 3145732
  108.7 18.0 %all-to-all-start = ((f32[4,128,512]{2,1,0:T(8,128)}), f32[4,128,512]{2,1,0:T(8,128)S(1)}, u32[]{:S(2)}, u32[]{:S(2)}) async-start(f32[4,128,512]{2,1,0:T(8,128)} %bitcast.16), calls=%async_computation | async-start | bytes 2097152 | tf_op jit(solution)/shard_map/all_to_all | solution.py:225
  126.7 1.0 copy-start.1
Sparse Core Ops, SparseCore 0:
  9.5 59.9 all-gather.2

commit v7 on v6

--- a/solution.py
+++ b/solution.py
@@ -81,12 +81,11 @@
 
 
 def product_kernel(side, place, left, *refs):
-    items = refs[:10]
-    out, tiles, lefts, rights, homes, tile_sems, home_sems, left_sems = refs[10:]
+    items = refs[:16]
+    out, tiles, lefts, rights, homes, tile_sems, home_sems, left_sems = refs[16:]
     need = tiles.shape[2]
     z, core = place[0], place[1]
     other = 1 - core
-    toward = 2 * core - 1
 
     def tile_copy(source, n, parity):
         return pltpu.make_async_copy(source.at[pl.ds(0, need)], tiles.at[n, parity], tile_sems.at[n, parity])
@@ -97,12 +96,7 @@
     def left_copy(n, chip):
         return pltpu.make_async_copy(left.at[chip], lefts.at[n], left_sems.at[n])
 
-    own, swapped, rings, trades = items[0], items[1], items[2:6], items[6:10]
-    chunks = [(0, (own, core), (swapped, other))]
-    for s in range(3):
-        chunks.append(((s + 1) * toward, (rings[s].at[0], core), (rings[s].at[1], other)))
-        chunks.append((-(s + 1) * toward, (trades[s].at[0], other), (trades[s].at[1], core)))
-    chunks.append((4, (rings[3], core), (trades[3], other)))
+    chunks = [(by, (items[2 * n], core), (items[2 * n + 1], other)) for n, by in enumerate((0, -1, 1, -2, 2, -3, 3, 4))]
     for n, (by, *pieces) in enumerate(chunks):
         for ref, parity in pieces:
             if side:
@@ -113,9 +107,9 @@
 
     def unpack(n, slot):
         for parity in range(2):
-            tile_copy(own, n, parity).wait()
+            tile_copy(items[0], n, parity).wait()
             if side:
-                home_copy(own, n, parity).wait()
+                home_copy(items[0], n, parity).wait()
         for parity in range(2):
             for b in range(2):
                 for c in range(4):
@@ -159,7 +153,7 @@
     return pl.pallas_call(
         functools.partial(product_kernel, side),
         out_shape=jax.ShapeDtypeStruct((512, 512), F32),
-        in_specs=[smem] + [hbm] * 11,
+        in_specs=[smem] + [hbm] * 17,
         out_specs=pl.BlockSpec(memory_space=pltpu.VMEM),
         scratch_shapes=[
             pltpu.VMEM((8, 2, need, LANES), F32),
@@ -175,8 +169,13 @@
     )(place, left, *items)
 
 
-def finish_kernel(side, place, flags, terms, square, *refs):
-    out = refs[-1]
+def finish_kernel(side, place, flags, terms_in, square, *refs):
+    out, terms, sems = refs[-3:]
+    copies = [pltpu.make_async_copy(terms_in.at[n], terms.at[n], sems.at[n]) for n in range(4)]
+    for copy in copies:
+        copy.start()
+    for copy in copies:
+        copy.wait()
     for b in range(2):
         for c in range(4):
             at = (pl.ds(b * BS, BS), pl.ds(c * LANES, LANES))
@@ -188,29 +187,43 @@
 
 def finish(side, terms, square, flags, place, *before):
     smem = pl.BlockSpec(memory_space=pltpu.SMEM)
+    hbm = pl.BlockSpec(memory_space=pltpu.HBM)
     half = pl.BlockSpec((128, 512), lambda i: (0, side))
     return pl.pallas_call(
         functools.partial(finish_kernel, side),
         out_shape=jax.ShapeDtypeStruct(square.shape, F32),
         grid=(1,),
-        in_specs=[smem, smem, pl.BlockSpec((4, 128, 512), lambda i: (0, 0, 0)), half]
-        + [pl.BlockSpec(memory_space=pltpu.HBM)] * len(before),
+        in_specs=[smem, smem, hbm, half] + [hbm] * len(before),
         out_specs=half,
+        scratch_shapes=[pltpu.VMEM((4, 128, 512), F32), pltpu.SemaphoreType.DMA((4,))],
         input_output_aliases={4: 0} if before else {},
         cost_estimate=pl.CostEstimate(flops=1 << 20, bytes_accessed=2 << 20, transcendentals=0),
         compiler_params=pltpu.CompilerParams(vmem_limit_bytes=56 << 20),
     )(place, flags, terms, square, *before)
 
 
+def shift(n, by):
+    return [(i, (i + by) % n) for i in range(n)]
+
+
 def gather_right(own):
-    ring = [(2 * z + c, 2 * ((z + 1 - 2 * c) % 8) + c) for z in range(8) for c in range(2)]
     trade = [(i, i ^ 1) for i in range(16)]
-    swapped = lax.ppermute(own, "row", trade)
-    rings, pair = [], jnp.stack([own, swapped])
+
+    def send(x, by, after):
+        x = lax.optimization_barrier((x, *after))[0]
+        return lax.ppermute(x, "row", shift(16, 2 * by))
+
+    up = down = own
+    arrivals, traded = [own], [lax.ppermute(own, "row", trade)]
     for step in range(4):
-        pair = lax.ppermute(pair if step < 3 else pair[0], "row", ring)
-        rings.append(pair)
-    return [own, swapped] + rings + [lax.ppermute(pair, "row", trade) for pair in rings]
+        after = traded[:1] if step == 1 else traded[2 * step - 3 : 2 * step - 1] if step else []
+        up = send(up, 1, after)
+        arrivals.append(up)
+        if step < 3:
+            down = send(down, -1, after)
+            arrivals.append(down)
+        traded += [lax.ppermute(x, "row", trade) for x in arrivals[len(traded) :]]
+    return [x for both in zip(arrivals, traded) for x in both]
 
 
 def local(left_slab, right_window, left_pattern, right_pattern, square_blocks, result_pattern):

time: 137 us -> 141 us (1.029)
  the two profiles are of different devices: /device:TPU:48 before, /device:TPU:24 now
where the time goes in v7:
time: 141 us; the launch traced here: 140 us
  starting transfers between devices  52.9 us (38%)
  waiting for transfers between devices  46.4 us (33%)
  Pallas kernels  25 us (18%)
  between operations  13.7 us (10%)
    ppermute x7, starting transfers between devices, send(): return lax.ppermute(x, 'row', shift(16, 2 * by))  29.4 us
    ppermute x7, waiting for transfers between devices, send(): return lax.ppermute(x, 'row', shift(16, 2 * by))  26.3 us
    all_to_all x2, waiting for transfers between devices, local(): terms = lax.all_to_all(cube.reshape(4, 128, 512), 'layer', 0, 0)  18.6 us
    pallas_call x2, Pallas kernels, product(): pl.pallas_call(functools.partial(product_kernel, side), out_shape=jax.Sha...  16.4 us
    ppermute x7, starting transfers between devices, gather_right(): traded += [lax.ppermute(x, 'row', trade) for x in arrivals[len(traded):]]  13.9 us
    all_to_all x2, starting transfers between devices, local(): terms = lax.all_to_all(cube.reshape(4, 128, 512), 'layer', 0, 0)  7.74 us
    pallas_call x2, Pallas kernels, finish(): pl.pallas_call(functools.partial(finish_kernel, side), out_shape=jax.Shap...  5.95 us
  transfers between devices with their start and end apart: 18, of which 9 were waited for; matrix products, arithmetic and copies ran while one was open for 0% of the time, Pallas kernels for 8%

profile of v7, /device:TPU:24, one launch (start us, length us, event | category | flops | bytes accessed | tf_op | source)
XLA Modules:
  0.0 139.8 jit_solution(12518707614325684895)
XLA Ops:
  6.5 2.7 %shard_map.64 = (f32[512,256]{1,0:T(8,128)}, f32[784,128]{1,0:T(8,128)}) custom-call(s32[4,8]{1,0:T(4,128)} %bitcast.16, f32[512,256]{1,0:T(8,128)} %bitcast.14, s32[2,16]{1,0:T(2,128)} %bitcast.17, f32[128,1024]{1,0:T(8,128)} %bitcast.15), custom_call_target="tpu_custom_call" | custom-call | tf_op jit(solution)/shard_map/pallas_call | solution.py:69
  9.2 4.3 %collective-permute-start.1 = (f32[784,128]{1,0:T(8,128)}, f32[784,128]{1,0:T(8,128)S(1)}, u32[]{:S(2)}, u32[]{:S(2)}) collective-permute-start(f32[784,128]{1,0:T(8,128)} %get-tuple-element.13.refs_0_), channel_id=1, source_target_pairs={{0,64},{32,96},{64,128},{96,160},{128,192},{160,224},{192,256},{22... | collective-permute-start | bytes 1204232 | tf_op jit(solution)/shard_map/ppermute | solution.py:214
  13.6 1.9 %collective-permute-start = (f32[784,128]{1,0:T(8,128)}, f32[784,128]{1,0:T(8,128)S(1)}, u32[]{:S(2)}, u32[]{:S(2)}) collective-permute-start(f32[784,128]{1,0:T(8,128)} %get-tuple-element.13.refs_0_), channel_id=1, source_target_pairs={{0,32},{32,0},{64,96},{96,64},{128,160},{160,128},{192,224},{224,1... | collective-permute-start | bytes 1204232 | tf_op jit(solution)/shard_map/ppermute | solution.py:217
  15.5 8.7 %collective-permute-start.3 = (f32[784,128]{1,0:T(8,128)}, f32[784,128]{1,0:T(8,128)S(1)}, u32[]{:S(2)}, u32[]{:S(2)}) collective-permute-start(f32[784,128]{1,0:T(8,128)} %get-tuple-element.13.refs_0_), channel_id=1, source_target_pairs={{0,448},{32,480},{64,0},{96,32},{128,64},{160,96},{192,128},{224,1... | collective-permute-start | bytes 1204232 | tf_op jit(solution)/shard_map/ppermute | solution.py:214
  24.2 5.6 %collective-permute-done.1.refs_2_ = f32[784,128]{1,0:T(8,128)S(1)} collective-permute-done((f32[784,128]{1,0:T(8,128)}, f32[784,128]{1,0:T(8,128)S(1)}, u32[]{:S(2)}, u32[]{:S(2)}) %collective-permute-start.1) | collective-permute-done | bytes 401440 | tf_op jit(solution)/shard_map/ppermute | solution.py:214
  29.7 1.9 %collective-permute-start.2 = (f32[784,128]{1,0:T(8,128)S(1)}, f32[784,128]{1,0:T(8,128)S(1)}, u32[]{:S(2)}, u32[]{:S(2)}) collective-permute-start(f32[784,128]{1,0:T(8,128)S(1)} %collective-permute-done.1.refs_2_), channel_id=1, source_target_pairs={{0,32},{32,0},{64,96},{96,64},{128,160},{160,128},{192,224},{224,1... | collective-permute-start | bytes 1204232 | tf_op jit(solution)/shard_map/ppermute | solution.py:225
  31.7 2.0 %collective-permute-done.3.refs_4_ = f32[784,128]{1,0:T(8,128)S(1)} collective-permute-done((f32[784,128]{1,0:T(8,128)}, f32[784,128]{1,0:T(8,128)S(1)}, u32[]{:S(2)}, u32[]{:S(2)}) %collective-permute-start.3) | collective-permute-done | bytes 401440 | tf_op jit(solution)/shard_map/ppermute | solution.py:214
  33.7 1.9 %collective-permute-start.4 = (f32[784,128]{1,0:T(8,128)S(1)}, f32[784,128]{1,0:T(8,128)S(1)}, u32[]{:S(2)}, u32[]{:S(2)}) collective-permute-start(f32[784,128]{1,0:T(8,128)S(1)} %collective-permute-done.3.refs_4_), channel_id=1, source_target_pairs={{0,32},{32,0},{64,96},{96,64},{128,160},{160,128},{192,224},{224,1... | collective-permute-start | bytes 1204232 | tf_op jit(solution)/shard_map/ppermute | solution.py:225
  35.6 1.9 %collective-permute-start.5 = (f32[784,128]{1,0:T(8,128)S(1)}, f32[784,128]{1,0:T(8,128)S(1)}, u32[]{:S(2)}, u32[]{:S(2)}) collective-permute-start(f32[784,128]{1,0:T(8,128)S(1)} %collective-permute-done.1.refs_2_), channel_id=1, source_target_pairs={{0,64},{32,96},{64,128},{96,160},{128,192},{160,224},{192,256},{22... | collective-permute-start | bytes 1204232 | tf_op jit(solution)/shard_map/ppermute | solution.py:214
  37.5 5.5 %collective-permute-start.7 = (f32[784,128]{1,0:T(8,128)S(1)}, f32[784,128]{1,0:T(8,128)S(1)}, u32[]{:S(2)}, u32[]{:S(2)}) collective-permute-start(f32[784,128]{1,0:T(8,128)S(1)} %collective-permute-done.3.refs_4_), channel_id=1, source_target_pairs={{0,448},{32,480},{64,0},{96,32},{128,64},{160,96},{192,128},{224,1... | collective-permute-start | bytes 1204232 | tf_op jit(solution)/shard_map/ppermute | solution.py:214
  43.1 8.0 %collective-permute-done.5.refs_6_ = f32[784,128]{1,0:T(8,128)S(1)} collective-permute-done((f32[784,128]{1,0:T(8,128)S(1)}, f32[784,128]{1,0:T(8,128)S(1)}, u32[]{:S(2)}, u32[]{:S(2)}) %collective-permute-start.5) | collective-permute-done | bytes 401440 | tf_op jit(solution)/shard_map/ppermute | solution.py:214
  51.0 1.9 %collective-permute-start.9 = (f32[784,128]{1,0:T(8,128)S(1)}, f32[784,128]{1,0:T(8,128)S(1)}, u32[]{:S(2)}, u32[]{:S(2)}) collective-permute-start(f32[784,128]{1,0:T(8,128)S(1)} %collective-permute-done.5.refs_6_), channel_id=1, source_target_pairs={{0,64},{32,96},{64,128},{96,160},{128,192},{160,224},{192,256},{22... | collective-permute-start | bytes 1204232 | tf_op jit(solution)/shard_map/ppermute | solution.py:214
  52.9 1.9 %collective-permute-start.6 = (f32[784,128]{1,0:T(8,128)S(1)}, f32[784,128]{1,0:T(8,128)S(1)}, u32[]{:S(2)}, u32[]{:S(2)}) collective-permute-start(f32[784,128]{1,0:T(8,128)S(1)} %collective-permute-done.5.refs_6_), channel_id=1, source_target_pairs={{0,32},{32,0},{64,96},{96,64},{128,160},{160,128},{192,224},{224,1... | collective-permute-start | bytes 1204232 | tf_op jit(solution)/shard_map/ppermute | solution.py:225
  54.9 2.4 %collective-permute-start.8 = (f32[784,128]{1,0:T(8,128)S(1)}, f32[784,128]{1,0:T(8,128)S(1)}, u32[]{:S(2)}, u32[]{:S(2)}) collective-permute-start(f32[784,128]{1,0:T(8,128)S(1)} %collective-permute-done.7.refs_8_), channel_id=1, source_target_pairs={{0,32},{32,0},{64,96},{96,64},{128,160},{160,128},{192,224},{224,1... | collective-permute-start | bytes 1204232 | tf_op jit(solution)/shard_map/ppermute | solution.py:225
  57.3 5.1 %collective-permute-start.11 = (f32[784,128]{1,0:T(8,128)S(1)}, f32[784,128]{1,0:T(8,128)}, u32[]{:S(2)}, u32[]{:S(2)}) collective-permute-start(f32[784,128]{1,0:T(8,128)S(1)} %collective-permute-done.7.refs_8_), channel_id=1, source_target_pairs={{0,448},{32,480},{64,0},{96,32},{128,64},{160,96},{192,128},{224,1... | collective-permute-start | bytes 1204232 | tf_op jit(solution)/shard_map/ppermute | solution.py:214
  62.5 2.9 %collective-permute-done.9.refs_10_ = f32[784,128]{1,0:T(8,128)S(1)} collective-permute-done((f32[784,128]{1,0:T(8,128)S(1)}, f32[784,128]{1,0:T(8,128)S(1)}, u32[]{:S(2)}, u32[]{:S(2)}) %collective-permute-start.9) | collective-permute-done | bytes 401440 | tf_op jit(solution)/shard_map/ppermute | solution.py:214
  65.4 1.9 %collective-permute-start.13 = (f32[784,128]{1,0:T(8,128)S(1)}, f32[784,128]{1,0:T(8,128)}, u32[]{:S(2)}, u32[]{:S(2)}) collective-permute-start(f32[784,128]{1,0:T(8,128)S(1)} %collective-permute-done.9.refs_10_), channel_id=1, source_target_pairs={{0,64},{32,96},{64,128},{96,160},{128,192},{160,224},{192,256},{22... | collective-permute-start | bytes 1204232 | tf_op jit(solution)/shard_map/ppermute | solution.py:214
  67.3 1.9 %collective-permute-start.10 = (f32[784,128]{1,0:T(8,128)S(1)}, f32[784,128]{1,0:T(8,128)}, u32[]{:S(2)}, u32[]{:S(2)}) collective-permute-start(f32[784,128]{1,0:T(8,128)S(1)} %collective-permute-done.9.refs_10_), channel_id=1, source_target_pairs={{0,32},{32,0},{64,96},{96,64},{128,160},{160,128},{192,224},{224,1... | collective-permute-start | bytes 1204232 | tf_op jit(solution)/shard_map/ppermute | solution.py:225
  69.2 1.9 %collective-permute-done.11.refs_12_ = f32[784,128]{1,0:T(8,128)} collective-permute-done((f32[784,128]{1,0:T(8,128)S(1)}, f32[784,128]{1,0:T(8,128)}, u32[]{:S(2)}, u32[]{:S(2)}) %collective-permute-start.11) | collective-permute-done | bytes 401440 | tf_op jit(solution)/shard_map/ppermute | solution.py:214
  71.2 1.9 %collective-permute-start.12 = (f32[784,128]{1,0:T(8,128)}, f32[784,128]{1,0:T(8,128)}, u32[]{:S(2)}, u32[]{:S(2)}) collective-permute-start(f32[784,128]{1,0:T(8,128)} %collective-permute-done.11.refs_12_), channel_id=1, source_target_pairs={{0,32},{32,0},{64,96},{96,64},{128,160},{160,128},{192,224},{224,1... | collective-permute-start | bytes 1204232 | tf_op jit(solution)/shard_map/ppermute | solution.py:225
  73.1 6.0 %collective-permute-done.13.refs_14_ = f32[784,128]{1,0:T(8,128)} collective-permute-done((f32[784,128]{1,0:T(8,128)S(1)}, f32[784,128]{1,0:T(8,128)}, u32[]{:S(2)}, u32[]{:S(2)}) %collective-permute-start.13) | collective-permute-done | bytes 401440 | tf_op jit(solution)/shard_map/ppermute | solution.py:214
  79.1 1.9 %collective-permute-start.14 = (f32[784,128]{1,0:T(8,128)}, f32[784,128]{1,0:T(8,128)}, u32[]{:S(2)}, u32[]{:S(2)}) collective-permute-start(f32[784,128]{1,0:T(8,128)} %collective-permute-done.13.refs_14_), channel_id=1, source_target_pairs={{0,32},{32,0},{64,96},{96,64},{128,160},{160,128},{192,224},{224,1... | collective-permute-start | bytes 1204232 | tf_op jit(solution)/shard_map/ppermute | solution.py:225
  81.6 1.4 collective-permute-done.14.refs_15_
  83.1 8.2 %shard_map.66 = f32[512,512]{1,0:T(8,128)} custom-call(s32[3]{0:T(128)} %pad_add_fusion.place, f32[8,512,256]{2,1,0:T(8,128)} %bitcast.18, f32[784,128]{1,0:T(8,128)} %get-tuple-element.13.refs_0_, f32[784,128]{1,0:T(8,128)} %copy-done.3, f32[784,128]{1,0:T(8,128)} %copy-done.2, f32[784,128]{1,0:T(8,128)} %copy-done.5, f32[784,128]{1,0:T(8,128)} %copy-done.4, ...), custom_call_target="tpu_custom_call" | custom-call | flops 3221225472 | bytes 10485760 | tf_op jit(solution)/shard_map/pallas_call | solution.py:153
  91.3 4.2 %all-to-all-start.1 = ((f32[4,128,512]{2,1,0:T(8,128)}), f32[4,128,512]{2,1,0:T(8,128)S(1)}, u32[]{:S(2)}, u32[]{:S(2)}) async-start(f32[4,128,512]{2,1,0:T(8,128)} %bitcast.13), calls=%async_computation.1 | async-start | bytes 2097152 | tf_op jit(solution)/shard_map/all_to_all | solution.py:238
  95.5 8.2 %shard_map.65 = f32[512,512]{1,0:T(8,128)} custom-call(s32[3]{0:T(128)} %pad_add_fusion.place, f32[8,512,256]{2,1,0:T(8,128)} %bitcast.19, f32[784,128]{1,0:T(8,128)} %get-tuple-element.13.refs_0_, f32[784,128]{1,0:T(8,128)} %copy-done.3, f32[784,128]{1,0:T(8,128)} %copy-done.2, f32[784,128]{1,0:T(8,128)} %copy-done.5, f32[784,128]{1,0:T(8,128)} %copy-done.4, ...), custom_call_target="tpu_custom_call" | custom-call | flops 3221225472 | bytes 10485760 | tf_op jit(solution)/shard_map/pallas_call | solution.py:153
  103.8 7.1 %all-to-all-done.1.terms_in = f32[4,128,512]{2,1,0:T(8,128)S(1)} async-done(((f32[4,128,512]{2,1,0:T(8,128)}), f32[4,128,512]{2,1,0:T(8,128)S(1)}, u32[]{:S(2)}, u32[]{:S(2)}) %all-to-all-start.1) | async-done | bytes 1048608 | tf_op jit(solution)/shard_map/all_to_all | solution.py:238
  110.9 3.5 %all-to-all-start = ((f32[4,128,512]{2,1,0:T(8,128)}), f32[4,128,512]{2,1,0:T(8,128)S(1)}, u32[]{:S(2)}, u32[]{:S(2)}) async-start(f32[4,128,512]{2,1,0:T(8,128)} %bitcast.12), calls=%async_computation | async-start | bytes 2097152 | tf_op jit(solution)/shard_map/all_to_all | solution.py:238
  114.4 3.0 %shard_map.67.refs_0_ = f32[128,1024]{1,0:T(8,128)} custom-call(s32[3]{0:T(128)} %pad_add_fusion.place, s32[8,16]{1,0:T(8,128)} %flags.3, f32[4,128,512]{2,1,0:T(8,128)} %copy-done, f32[128,1024]{1,0:T(8,128)} %square.3), custom_call_target="tpu_custom_call" | custom-call | flops 1048576 | bytes 2097152 | tf_op jit(solution)/shard_map/pallas_call | solution.py:192
  117.4 11.5 %all-to-all-done.terms_in = f32[4,128,512]{2,1,0:T(8,128)S(1)} async-done(((f32[4,128,512]{2,1,0:T(8,128)}), f32[4,128,512]{2,1,0:T(8,128)S(1)}, u32[]{:S(2)}, u32[]{:S(2)}) %all-to-all-start) | async-done | bytes 1048608 | tf_op jit(solution)/shard_map/all_to_all | solution.py:238
  128.9 1.0 copy-done.1
  129.9 3.0 %shard_map.68 = f32[128,1024]{1,0:T(8,128)} custom-call(s32[3]{0:T(128)} %pad_add_fusion.place, s32[8,16]{1,0:T(8,128)} %flags.3, f32[4,128,512]{2,1,0:T(8,128)} %copy-done.1, f32[128,1024]{1,0:T(8,128)} %square.3, f32[128,1024]{1,0:T(8,128)} %shard_map.67.refs_0_), custom_call_target="tpu_custom_call", output_to_operand_aliasing={{}: (4, {})} | custom-call | flops 1048576 | bytes 2097152 | tf_op jit(solution)/shard_map/pallas_call | solution.py:192
  (35 shorter events, 0.7 us)
Async XLA Ops:
  6.5 76.5 %all-gather.3.cloned.1.call-start = ((), (), s32[]{:S(2)}) async-start(), calls=%async_computation.2 | async-start | bytes 4718592 | tf_op jit(solution)/shard_map/all_gather | solution.py:231
  9.2 20.5 %collective-permute-start.1 = (f32[784,128]{1,0:T(8,128)}, f32[784,128]{1,0:T(8,128)S(1)}, u32[]{:S(2)}, u32[]{:S(2)}) collective-permute-start(f32[784,128]{1,0:T(8,128)} %get-tuple-element.13.refs_0_), channel_id=1, source_target_pairs={{0,64},{32,96},{64,128},{96,160},{128,192},{160,224},{192,256},{22... | collective-permute-start | bytes 1204232 | tf_op jit(solution)/shard_map/ppermute | solution.py:214
  13.6 16.2 %collective-permute-start = (f32[784,128]{1,0:T(8,128)}, f32[784,128]{1,0:T(8,128)S(1)}, u32[]{:S(2)}, u32[]{:S(2)}) collective-permute-start(f32[784,128]{1,0:T(8,128)} %get-tuple-element.13.refs_0_), channel_id=1, source_target_pairs={{0,32},{32,0},{64,96},{96,64},{128,160},{160,128},{192,224},{224,1... | collective-permute-start | bytes 1204232 | tf_op jit(solution)/shard_map/ppermute | solution.py:217
  15.5 18.2 %collective-permute-start.3 = (f32[784,128]{1,0:T(8,128)}, f32[784,128]{1,0:T(8,128)S(1)}, u32[]{:S(2)}, u32[]{:S(2)}) collective-permute-start(f32[784,128]{1,0:T(8,128)} %get-tuple-element.13.refs_0_), channel_id=1, source_target_pairs={{0,448},{32,480},{64,0},{96,32},{128,64},{160,96},{192,128},{224,1... | collective-permute-start | bytes 1204232 | tf_op jit(solution)/shard_map/ppermute | solution.py:214
  29.7 53.3 %copy-start.2 = (f32[784,128]{1,0:T(8,128)}, f32[784,128]{1,0:T(8,128)S(1)}, u32[]{:S(2)}) copy-start(f32[784,128]{1,0:T(8,128)S(1)} %collective-permute-done.1.refs_2_) | copy-start | bytes 1204228
  29.7 53.3 %copy-start.3 = (f32[784,128]{1,0:T(8,128)}, f32[784,128]{1,0:T(8,128)S(1)}, u32[]{:S(2)}) copy-start(f32[784,128]{1,0:T(8,128)S(1)} %collective-permute-done.refs_1_) | copy-start | bytes 1204228
  29.7 13.3 %collective-permute-start.2 = (f32[784,128]{1,0:T(8,128)S(1)}, f32[784,128]{1,0:T(8,128)S(1)}, u32[]{:S(2)}, u32[]{:S(2)}) collective-permute-start(f32[784,128]{1,0:T(8,128)S(1)} %collective-permute-done.1.refs_2_), channel_id=1, source_target_pairs={{0,32},{32,0},{64,96},{96,64},{128,160},{160,128},{192,224},{224,1... | collective-permute-start | bytes 1204232 | tf_op jit(solution)/shard_map/ppermute | solution.py:225
  33.7 49.4 %copy-start.4 = (f32[784,128]{1,0:T(8,128)}, f32[784,128]{1,0:T(8,128)S(1)}, u32[]{:S(2)}) copy-start(f32[784,128]{1,0:T(8,128)S(1)} %collective-permute-done.3.refs_4_) | copy-start | bytes 1204228
  33.7 9.4 %collective-permute-start.4 = (f32[784,128]{1,0:T(8,128)S(1)}, f32[784,128]{1,0:T(8,128)S(1)}, u32[]{:S(2)}, u32[]{:S(2)}) collective-permute-start(f32[784,128]{1,0:T(8,128)S(1)} %collective-permute-done.3.refs_4_), channel_id=1, source_target_pairs={{0,32},{32,0},{64,96},{96,64},{128,160},{160,128},{192,224},{224,1... | collective-permute-start | bytes 1204232 | tf_op jit(solution)/shard_map/ppermute | solution.py:225
  35.6 15.4 %collective-permute-start.5 = (f32[784,128]{1,0:T(8,128)S(1)}, f32[784,128]{1,0:T(8,128)S(1)}, u32[]{:S(2)}, u32[]{:S(2)}) collective-permute-start(f32[784,128]{1,0:T(8,128)S(1)} %collective-permute-done.1.refs_2_), channel_id=1, source_target_pairs={{0,64},{32,96},{64,128},{96,160},{128,192},{160,224},{192,256},{22... | collective-permute-start | bytes 1204232 | tf_op jit(solution)/shard_map/ppermute | solution.py:214
  37.5 17.4 %collective-permute-start.7 = (f32[784,128]{1,0:T(8,128)S(1)}, f32[784,128]{1,0:T(8,128)S(1)}, u32[]{:S(2)}, u32[]{:S(2)}) collective-permute-start(f32[784,128]{1,0:T(8,128)S(1)} %collective-permute-done.3.refs_4_), channel_id=1, source_target_pairs={{0,448},{32,480},{64,0},{96,32},{128,64},{160,96},{192,128},{224,1... | collective-permute-start | bytes 1204232 | tf_op jit(solution)/shard_map/ppermute | solution.py:214
  43.0 40.0 %copy-start.6 = (f32[784,128]{1,0:T(8,128)}, f32[784,128]{1,0:T(8,128)S(1)}, u32[]{:S(2)}) copy-start(f32[784,128]{1,0:T(8,128)S(1)} %collective-permute-done.4.refs_5_) | copy-start | bytes 1204228
  43.0 40.0 %copy-start.5 = (f32[784,128]{1,0:T(8,128)}, f32[784,128]{1,0:T(8,128)S(1)}, u32[]{:S(2)}) copy-start(f32[784,128]{1,0:T(8,128)S(1)} %collective-permute-done.2.refs_3_) | copy-start | bytes 1204228
  51.0 32.0 %copy-start.7 = (f32[784,128]{1,0:T(8,128)}, f32[784,128]{1,0:T(8,128)S(1)}, u32[]{:S(2)}) copy-start(f32[784,128]{1,0:T(8,128)S(1)} %collective-permute-done.5.refs_6_) | copy-start | bytes 1204228
  51.0 14.3 %collective-permute-start.9 = (f32[784,128]{1,0:T(8,128)S(1)}, f32[784,128]{1,0:T(8,128)S(1)}, u32[]{:S(2)}, u32[]{:S(2)}) collective-permute-start(f32[784,128]{1,0:T(8,128)S(1)} %collective-permute-done.5.refs_6_), channel_id=1, source_target_pairs={{0,64},{32,96},{64,128},{96,160},{128,192},{160,224},{192,256},{22... | collective-permute-start | bytes 1204232 | tf_op jit(solution)/shard_map/ppermute | solution.py:214
  52.9 12.4 %collective-permute-start.6 = (f32[784,128]{1,0:T(8,128)S(1)}, f32[784,128]{1,0:T(8,128)S(1)}, u32[]{:S(2)}, u32[]{:S(2)}) collective-permute-start(f32[784,128]{1,0:T(8,128)S(1)} %collective-permute-done.5.refs_6_), channel_id=1, source_target_pairs={{0,32},{32,0},{64,96},{96,64},{128,160},{160,128},{192,224},{224,1... | collective-permute-start | bytes 1204232 | tf_op jit(solution)/shard_map/ppermute | solution.py:225
  54.9 28.2 %copy-start.8 = (f32[784,128]{1,0:T(8,128)}, f32[784,128]{1,0:T(8,128)S(1)}, u32[]{:S(2)}) copy-start(f32[784,128]{1,0:T(8,128)S(1)} %collective-permute-done.7.refs_8_) | copy-start | bytes 1204228
  54.9 10.4 %collective-permute-start.8 = (f32[784,128]{1,0:T(8,128)S(1)}, f32[784,128]{1,0:T(8,128)S(1)}, u32[]{:S(2)}, u32[]{:S(2)}) collective-permute-start(f32[784,128]{1,0:T(8,128)S(1)} %collective-permute-done.7.refs_8_), channel_id=1, source_target_pairs={{0,32},{32,0},{64,96},{96,64},{128,160},{160,128},{192,224},{224,1... | collective-permute-start | bytes 1204232 | tf_op jit(solution)/shard_map/ppermute | solution.py:225
  57.3 13.8 %collective-permute-start.11 = (f32[784,128]{1,0:T(8,128)S(1)}, f32[784,128]{1,0:T(8,128)}, u32[]{:S(2)}, u32[]{:S(2)}) collective-permute-start(f32[784,128]{1,0:T(8,128)S(1)} %collective-permute-done.7.refs_8_), channel_id=1, source_target_pairs={{0,448},{32,480},{64,0},{96,32},{128,64},{160,96},{192,128},{224,1... | collective-permute-start | bytes 1204232 | tf_op jit(solution)/shard_map/ppermute | solution.py:214
  65.3 17.7 %copy-start.9 = (f32[784,128]{1,0:T(8,128)}, f32[784,128]{1,0:T(8,128)S(1)}, u32[]{:S(2)}) copy-start(f32[784,128]{1,0:T(8,128)S(1)} %collective-permute-done.9.refs_10_) | copy-start | bytes 1204228
  65.3 13.7 %copy-start.10 = (f32[784,128]{1,0:T(8,128)}, f32[784,128]{1,0:T(8,128)S(1)}, u32[]{:S(2)}) copy-start(f32[784,128]{1,0:T(8,128)S(1)} %collective-permute-done.6.refs_7_) | copy-start | bytes 1204228
  65.4 15.6 %copy-start.11 = (f32[784,128]{1,0:T(8,128)}, f32[784,128]{1,0:T(8,128)S(1)}, u32[]{:S(2)}) copy-start(f32[784,128]{1,0:T(8,128)S(1)} %collective-permute-done.8.refs_9_) | copy-start | bytes 1204228
  65.4 13.7 %collective-permute-start.13 = (f32[784,128]{1,0:T(8,128)S(1)}, f32[784,128]{1,0:T(8,128)}, u32[]{:S(2)}, u32[]{:S(2)}) collective-permute-start(f32[784,128]{1,0:T(8,128)S(1)} %collective-permute-done.9.refs_10_), channel_id=1, source_target_pairs={{0,64},{32,96},{64,128},{96,160},{128,192},{160,224},{192,256},{22... | collective-permute-start | bytes 1204232 | tf_op jit(solution)/shard_map/ppermute | solution.py:214
  67.3 14.3 %collective-permute-start.10 = (f32[784,128]{1,0:T(8,128)S(1)}, f32[784,128]{1,0:T(8,128)}, u32[]{:S(2)}, u32[]{:S(2)}) collective-permute-start(f32[784,128]{1,0:T(8,128)S(1)} %collective-permute-done.9.refs_10_), channel_id=1, source_target_pairs={{0,32},{32,0},{64,96},{96,64},{128,160},{160,128},{192,224},{224,1... | collective-permute-start | bytes 1204232 | tf_op jit(solution)/shard_map/ppermute | solution.py:225
  71.2 10.5 %collective-permute-start.12 = (f32[784,128]{1,0:T(8,128)}, f32[784,128]{1,0:T(8,128)}, u32[]{:S(2)}, u32[]{:S(2)}) collective-permute-start(f32[784,128]{1,0:T(8,128)} %collective-permute-done.11.refs_12_), channel_id=1, source_target_pairs={{0,32},{32,0},{64,96},{96,64},{128,160},{160,128},{192,224},{224,1... | collective-permute-start | bytes 1204232 | tf_op jit(solution)/shard_map/ppermute | solution.py:225
  79.1 4.0 %collective-permute-start.14 = (f32[784,128]{1,0:T(8,128)}, f32[784,128]{1,0:T(8,128)}, u32[]{:S(2)}, u32[]{:S(2)}) collective-permute-start(f32[784,128]{1,0:T(8,128)} %collective-permute-done.13.refs_14_), channel_id=1, source_target_pairs={{0,32},{32,0},{64,96},{96,64},{128,160},{160,128},{192,224},{224,1... | collective-permute-start | bytes 1204232 | tf_op jit(solution)/shard_map/ppermute | solution.py:225
  91.3 19.6 %all-to-all-start.1 = ((f32[4,128,512]{2,1,0:T(8,128)}), f32[4,128,512]{2,1,0:T(8,128)S(1)}, u32[]{:S(2)}, u32[]{:S(2)}) async-start(f32[4,128,512]{2,1,0:T(8,128)} %bitcast.13), calls=%async_computation.1 | async-start | bytes 2097152 | tf_op jit(solution)/shard_map/all_to_all | solution.py:238
  110.9 3.5 %copy-start = (f32[4,128,512]{2,1,0:T(8,128)}, f32[4,128,512]{2,1,0:T(8,128)S(1)}, u32[]{:S(2)}) copy-start(f32[4,128,512]{2,1,0:T(8,128)S(1)} %all-to-all-done.1.terms_in) | copy-start | bytes 3145732
  110.9 18.0 %all-to-all-start = ((f32[4,128,512]{2,1,0:T(8,128)}), f32[4,128,512]{2,1,0:T(8,128)S(1)}, u32[]{:S(2)}, u32[]{:S(2)}) async-start(f32[4,128,512]{2,1,0:T(8,128)} %bitcast.12), calls=%async_computation | async-start | bytes 2097152 | tf_op jit(solution)/shard_map/all_to_all | solution.py:238
  128.9 1.0 copy-start.1
Sparse Core Ops, SparseCore 0:
  9.4 61.3 all-gather.2

commit v8 on v3

--- a/solution.py
+++ b/solution.py
@@ -82,29 +82,25 @@
 
 def product_kernel(side, first, last, where, packed, *refs):
     steps = range(first, last)
-    count = sum(2 if k == 7 else 1 for k in steps)
-    parts, refs = refs[:count], refs[count:]
+    parts, refs = refs[: last - first], refs[last - first :]
     if first:
         before, refs = refs[0], refs[1:]
     out, tiles, lefts, high0, high1, low0, low1, homes, tile_sems, left_sems, home_sem = refs
     need = tiles.shape[2]
     copies = {}
+    if first:
+        sum_copy = pltpu.make_async_copy(before, out, home_sem)
+        sum_copy.start()
     if side:
-        home_copy = pltpu.make_async_copy(packed.at[:, pl.ds(0, 8), :], homes, home_sem)
+        home_copy = pltpu.make_async_copy(packed.at[:, pl.ds(0, 1), :], homes, home_sem)
         home_copy.start()
     for k in steps:
         n = k - first
         tile = pltpu.make_async_copy(packed.at[pl.ds(where[k] * 2, 2), pl.ds(0, need), :], tiles.at[n], tile_sems.at[n])
         tile.start()
-        if k < 7:
-            pieces = [pltpu.make_async_copy(parts[n], lefts.at[n], left_sems.at[n])]
-        else:
-            pieces = [
-                pltpu.make_async_copy(parts[n + h], lefts.at[n, pl.ds(h * 256, 256)], left_sems.at[n + h]) for h in range(2)
-            ]
-        for piece in pieces:
-            piece.start()
-        copies[k] = [tile] + pieces
+        part = pltpu.make_async_copy(parts[n], lefts.at[n], left_sems.at[n])
+        part.start()
+        copies[k] = [tile, part]
     half = lane_half()
     if side:
         home_copy.wait()
@@ -141,10 +137,10 @@
         total = jnp.dot(left_low, high[...], preferred_element_type=F32)
         total += jnp.dot(left_high, low[...], preferred_element_type=F32)
         total += jnp.dot(left_high, high[...], preferred_element_type=F32)
-        if k > first:
+        if k == first and first:
+            sum_copy.wait()
+        if k:
             total += out[...]
-        elif first:
-            total += before[...]
         out[...] = total
 
 
@@ -158,7 +154,7 @@
     return pl.pallas_call(
         functools.partial(product_kernel, side, first, last),
         out_shape=jax.ShapeDtypeStruct((512, 512), F32),
-        in_specs=[smem] + [hbm] * (1 + len(parts)) + [vmem] * len(before),
+        in_specs=[smem] + [hbm] * (1 + len(parts)) + [hbm] * len(before),
         out_specs=vmem,
         scratch_shapes=[
             pltpu.VMEM((steps, 2, need, LANES), F32),
@@ -167,9 +163,9 @@
             half,
             half,
             half,
-            pltpu.SMEM((16, 8, LANES), F32),
+            pltpu.SMEM((16, 1, LANES), F32),
             pltpu.SemaphoreType.DMA((steps,)),
-            pltpu.SemaphoreType.DMA((steps + 1,)),
+            pltpu.SemaphoreType.DMA((steps,)),
             pltpu.SemaphoreType.DMA,
         ],
         cost_estimate=pl.CostEstimate(flops=6 * 512 * 512 * 256 * steps, bytes_accessed=steps << 20, transcendentals=0),
@@ -214,8 +210,7 @@
     up1, down1 = send(own, 1), send(own, -1)
     up2, down2 = send(up1, 1), send(down1, -1)
     up3, down3 = send(up2, 1), send(down2, -1)
-    far_a, far_b = send(up3[:256], 1), send(down3[256:], -1)
-    return [own, up1, down1, up2, down2, up3, down3, far_a, far_b]
+    return [own, up1, down1, up2, down2, up3, down3, send(up3, 1)]
 
 
 def local(left_slab, right_window, left_pattern, right_pattern, square_blocks, result_pattern):

time: 125 us -> 124 us (level)
  waiting for transfers between devices: 42.9 us -> 46.2 us
  local copies, waits for them, and re-layouts: 3.26 us -> 1.03 us
  starting transfers between devices: 35.7 us -> 34.3 us
    all_gather x1, waiting for transfers between devices: 1.02 us -> 5.53 us  [local(): packed = lax.all_gather(packed, 'row', axis=0, tiled=False)]
    ppermute x8 -> x7, waiting for transfers between devices: 23.2 us -> 21.4 us  [send(): return lax.ppermute(x, 'col', shift(8, by))]
    slice x2 -> x0, local copies, waits for them, and re-layouts: 1.55 us -> none  [gather_left(): far_a, far_b = (send(up3[:256], 1), send(down3[256:], -1))]
    ppermute x8 -> x7, starting transfers between devices: 27.9 us -> 26.5 us  [send(): return lax.ppermute(x, 'col', shift(8, by))]
  transfers between devices with their start and end apart: 11 -> 10, of which waited for: 8 -> 8; matrix products, arithmetic and copies ran while one was open for 2% -> 1% of each run, Pallas kernels for 15% -> 15%
where the time goes in v8:
time: 124 us; the launch traced here: 123 us
  waiting for transfers between devices  46.2 us (37%)
  starting transfers between devices  34.3 us (28%)
  Pallas kernels  26.9 us (22%)
  between operations  13.5 us (11%)
  other arithmetic  1.24 us (1%)
    ppermute x7, starting transfers between devices, send(): return lax.ppermute(x, 'col', shift(8, by))  26.5 us
    ppermute x7, waiting for transfers between devices, send(): return lax.ppermute(x, 'col', shift(8, by))  21.4 us
    pallas_call x3, Pallas kernels, product(): pl.pallas_call(functools.partial(product_kernel, side, first, last), out_...  20 us
    all_to_all x2, waiting for transfers between devices, local(): terms = lax.all_to_all(cube.reshape(4, 128, 512), 'layer', 0, 0)  19.2 us
    all_to_all x2, starting transfers between devices, local(): terms = lax.all_to_all(cube.reshape(4, 128, 512), 'layer', 0, 0)  7.77 us
    all_gather x1, waiting for transfers between devices, local(): packed = lax.all_gather(packed, 'row', axis=0, tiled=False)  5.53 us
    pallas_call x2, Pallas kernels, finish(): pl.pallas_call(functools.partial(finish_kernel, side), out_shape=jax.Shap...  4.13 us
    pallas_call x1, Pallas kernels, prepare(): pl.pallas_call(prepare_kernel, out_shape=(jax.ShapeDtypeStruct(left.shape...  2.84 us
  transfers between devices with their start and end apart: 10, of which 8 were waited for; matrix products, arithmetic and copies ran while one was open for 1% of the time, Pallas kernels for 15%

profile of v8, /device:TPU:8, one launch (start us, length us, event | category | flops | bytes accessed | tf_op | source)
XLA Modules:
  0.0 123.2 jit_solution(6841943665164034454)
XLA Ops:
  6.5 0.0 all-gather.3.cloned.1.call-start
  6.5 2.8 %shard_map.73 = (f32[512,256]{1,0:T(8,128)}, f32[784,128]{1,0:T(8,128)}) custom-call(s32[4,8]{1,0:T(4,128)} %bitcast.17, f32[512,256]{1,0:T(8,128)} %bitcast.15, s32[2,16]{1,0:T(2,128)} %bitcast.18, f32[128,1024]{1,0:T(8,128)} %bitcast.16), custom_call_target="tpu_custom_call" | custom-call | tf_op jit(solution)/shard_map/pallas_call | solution.py:69
  9.4 0.0 all-gather.3.cloned.1.call-update
  9.4 3.3 %collective-permute-start = (f32[512,256]{1,0:T(8,128)}, f32[512,256]{1,0:T(8,128)S(1)}, u32[]{:S(2)}, u32[]{:S(2)}) collective-permute-start(f32[512,256]{1,0:T(8,128)} %get-tuple-element.8.refs_0_), channel_id=1, source_target_pairs={{0,4},{4,8},{8,12},{12,16},{16,20},{20,24},{24,28},{28,0},{1,5},{5... | collective-permute-start | bytes 1572872 | tf_op jit(solution)/shard_map/ppermute | solution.py:208
  12.7 6.1 %collective-permute-start.1 = (f32[512,256]{1,0:T(8,128)}, f32[512,256]{1,0:T(8,128)S(1)}, u32[]{:S(2)}, u32[]{:S(2)}) collective-permute-start(f32[512,256]{1,0:T(8,128)} %get-tuple-element.8.refs_0_), channel_id=1, source_target_pairs={{0,28},{4,0},{8,4},{12,8},{16,12},{20,16},{24,20},{28,24},{1,29},{... | collective-permute-start | bytes 1572872 | tf_op jit(solution)/shard_map/ppermute | solution.py:208
  18.8 6.2 %collective-permute-done.refs_1_ = f32[512,256]{1,0:T(8,128)S(1)} collective-permute-done((f32[512,256]{1,0:T(8,128)}, f32[512,256]{1,0:T(8,128)S(1)}, u32[]{:S(2)}, u32[]{:S(2)}) %collective-permute-start) | collective-permute-done | bytes 524320 | tf_op jit(solution)/shard_map/ppermute | solution.py:208
  25.0 3.5 %collective-permute-start.2 = (f32[512,256]{1,0:T(8,128)S(1)}, f32[512,256]{1,0:T(8,128)S(1)}, u32[]{:S(2)}, u32[]{:S(2)}) collective-permute-start(f32[512,256]{1,0:T(8,128)S(1)} %collective-permute-done.refs_1_), channel_id=1, source_target_pairs={{0,4},{4,8},{8,12},{12,16},{16,20},{20,24},{24,28},{28,0},{1,5},{5... | collective-permute-start | bytes 1572872 | tf_op jit(solution)/shard_map/ppermute | solution.py:208
  28.5 0.0 collective-permute-done.1.refs_2_
  28.5 0.0 copy-start.3
  28.5 2.8 %collective-permute-start.3 = (f32[512,256]{1,0:T(8,128)S(1)}, f32[512,256]{1,0:T(8,128)S(1)}, u32[]{:S(2)}, u32[]{:S(2)}) collective-permute-start(f32[512,256]{1,0:T(8,128)S(1)} %collective-permute-done.1.refs_2_), channel_id=1, source_target_pairs={{0,28},{4,0},{8,4},{12,8},{16,12},{20,16},{24,20},{28,24},{1,29},{... | collective-permute-start | bytes 1572872 | tf_op jit(solution)/shard_map/ppermute | solution.py:208
  31.3 7.7 %collective-permute-done.2.refs_3_ = f32[512,256]{1,0:T(8,128)S(1)} collective-permute-done((f32[512,256]{1,0:T(8,128)S(1)}, f32[512,256]{1,0:T(8,128)S(1)}, u32[]{:S(2)}, u32[]{:S(2)}) %collective-permute-start.2) | collective-permute-done | bytes 524320 | tf_op jit(solution)/shard_map/ppermute | solution.py:208
  39.0 4.3 %collective-permute-start.4 = (f32[512,256]{1,0:T(8,128)S(1)}, f32[512,256]{1,0:T(8,128)S(1)}, u32[]{:S(2)}, u32[]{:S(2)}) collective-permute-start(f32[512,256]{1,0:T(8,128)S(1)} %collective-permute-done.2.refs_3_), channel_id=1, source_target_pairs={{0,4},{4,8},{8,12},{12,16},{16,20},{20,24},{24,28},{28,0},{1,5},{5... | collective-permute-start | bytes 1572872 | tf_op jit(solution)/shard_map/ppermute | solution.py:208
  43.2 0.4 collective-permute-done.3.refs_4_
  43.6 2.1 %collective-permute-start.5 = (f32[512,256]{1,0:T(8,128)S(1)}, f32[512,256]{1,0:T(8,128)S(1)}, u32[]{:S(2)}, u32[]{:S(2)}) collective-permute-start(f32[512,256]{1,0:T(8,128)S(1)} %collective-permute-done.3.refs_4_), channel_id=1, source_target_pairs={{0,28},{4,0},{8,4},{12,8},{16,12},{20,16},{24,20},{28,24},{1,29},{... | collective-permute-start | bytes 1572872 | tf_op jit(solution)/shard_map/ppermute | solution.py:208
  45.8 7.0 %collective-permute-done.4.refs_5_ = f32[512,256]{1,0:T(8,128)S(1)} collective-permute-done((f32[512,256]{1,0:T(8,128)S(1)}, f32[512,256]{1,0:T(8,128)S(1)}, u32[]{:S(2)}, u32[]{:S(2)}) %collective-permute-start.4) | collective-permute-done | bytes 524320 | tf_op jit(solution)/shard_map/ppermute | solution.py:208
  52.8 4.5 %collective-permute-start.6 = (f32[512,256]{1,0:T(8,128)S(1)}, f32[512,256]{1,0:T(8,128)}, u32[]{:S(2)}, u32[]{:S(2)}) collective-permute-start(f32[512,256]{1,0:T(8,128)S(1)} %collective-permute-done.4.refs_5_), channel_id=1, source_target_pairs={{0,4},{4,8},{8,12},{12,16},{16,20},{20,24},{24,28},{28,0},{1,5},{5... | collective-permute-start | bytes 1572872 | tf_op jit(solution)/shard_map/ppermute | solution.py:208
  57.3 1.2 %compare_select_fusion.where = s32[8]{0:T(128)} fusion(s32[8]{0:T(128)} %constant.16.clone, s32[]{:T(128)S(6)} %axis_index.25), kind=kLoop, calls=%fused_computation | loop fusion | flops 56 | bytes 68 | tf_op jit(solution)/shard_map/rem | solution.py:221
  58.5 0.1 collective-permute-done.5.refs_6_
  58.6 5.5 %all-gather.3.cloned.1.call-done = f32[12544,128]{1,0:T(8,128)} async-done(((f32[784,128]{1,0:T(8,128)}), f32[12544,128]{1,0:T(8,128)}) %all-gather.3.cloned.1.call-update) | async-done | bytes 6422544 | tf_op jit(solution)/shard_map/all_gather | solution.py:218
  64.2 0.0 copy-done.2
  64.2 7.0 %shard_map.75.refs_1_ = f32[512,512]{1,0:T(8,128)} custom-call(s32[8]{0:T(128)} %compare_select_fusion.where, f32[16,784,128]{2,1,0:T(8,128)} %bitcast.10, f32[512,256]{1,0:T(8,128)} %get-tuple-element.8.refs_0_, f32[512,256]{1,0:T(8,128)} %copy-done.2, f32[512,256]{1,0:T(8,128)} %copy-done.3, f32[512,256]{1,0:T(8,128)} %copy-done.4, f32[512,256]{1,0:T(8,128)} %copy-done.5, ...), custom_call_target="tpu_custom_call" | custom-call | flops 2818572288 | bytes 7340032 | tf_op jit(solution)/shard_map/pallas_call | solution.py:154
  71.3 0.0 collective-permute-done.6.refs_7_.refs_0_
  71.3 4.1 %shard_map.76 = f32[512,512]{1,0:T(8,128)} custom-call(s32[8]{0:T(128)} %compare_select_fusion.where, f32[16,784,128]{2,1,0:T(8,128)} %bitcast.11, f32[512,256]{1,0:T(8,128)} %collective-permute-done.6.refs_7_.refs_0_, f32[512,512]{1,0:T(8,128)} %shard_map.75.refs_1_), custom_call_target="tpu_custom_call" | custom-call | flops 402653184 | bytes 1048576 | tf_op jit(solution)/shard_map/pallas_call | solution.py:154
  75.3 4.3 %all-to-all-start.1 = ((f32[4,128,512]{2,1,0:T(8,128)}), f32[4,128,512]{2,1,0:T(8,128)S(1)}, u32[]{:S(2)}, u32[]{:S(2)}) async-start(f32[4,128,512]{2,1,0:T(8,128)} %bitcast.13), calls=%async_computation.1 | async-start | bytes 2097152 | tf_op jit(solution)/shard_map/all_to_all | solution.py:230
  79.6 8.9 %shard_map.74 = f32[512,512]{1,0:T(8,128)} custom-call(s32[8]{0:T(128)} %compare_select_fusion.where, f32[16,784,128]{2,1,0:T(8,128)} %bitcast.12, f32[512,256]{1,0:T(8,128)} %get-tuple-element.8.refs_0_, f32[512,256]{1,0:T(8,128)} %copy-done.2, f32[512,256]{1,0:T(8,128)} %copy-done.3, f32[512,256]{1,0:T(8,128)} %copy-done.4, f32[512,256]{1,0:T(8,128)} %copy-done.5, ...), custom_call_target="tpu_custom_call" | custom-call | flops 3221225472 | bytes 8388608 | tf_op jit(solution)/shard_map/pallas_call | solution.py:154
  88.5 6.6 %all-to-all-done.1.terms = f32[4,128,512]{2,1,0:T(8,128)S(1)} async-done(((f32[4,128,512]{2,1,0:T(8,128)}), f32[4,128,512]{2,1,0:T(8,128)S(1)}, u32[]{:S(2)}, u32[]{:S(2)}) %all-to-all-start.1) | async-done | bytes 1048608 | tf_op jit(solution)/shard_map/all_to_all | solution.py:230
  95.1 3.5 %all-to-all-start = ((f32[4,128,512]{2,1,0:T(8,128)}), f32[4,128,512]{2,1,0:T(8,128)S(1)}, u32[]{:S(2)}, u32[]{:S(2)}) async-start(f32[4,128,512]{2,1,0:T(8,128)} %bitcast.14), calls=%async_computation | async-start | bytes 2097152 | tf_op jit(solution)/shard_map/all_to_all | solution.py:230
  98.6 0.0 copy-done
  98.6 2.1 %shard_map.77.refs_0_ = f32[128,1024]{1,0:T(8,128)} custom-call(s32[1]{0:T(128)} %bitcast.where, s32[8,16]{1,0:T(8,128)} %flags.3, f32[4,128,512]{2,1,0:T(8,128)} %copy-done, f32[128,1024]{1,0:T(8,128)} %square.3), custom_call_target="tpu_custom_call" | custom-call | flops 1048576 | bytes 2097152 | tf_op jit(solution)/shard_map/pallas_call | solution.py:190
  100.7 12.6 %all-to-all-done.terms = f32[4,128,512]{2,1,0:T(8,128)S(1)} async-done(((f32[4,128,512]{2,1,0:T(8,128)}), f32[4,128,512]{2,1,0:T(8,128)S(1)}, u32[]{:S(2)}, u32[]{:S(2)}) %all-to-all-start) | async-done | bytes 1048608 | tf_op jit(solution)/shard_map/all_to_all | solution.py:230
  113.3 1.0 copy-done.1
  114.3 2.1 %shard_map.78 = f32[128,1024]{1,0:T(8,128)} custom-call(s32[1]{0:T(128)} %bitcast.where, s32[8,16]{1,0:T(8,128)} %flags.3, f32[4,128,512]{2,1,0:T(8,128)} %copy-done.1, f32[128,1024]{1,0:T(8,128)} %square.3, f32[128,1024]{1,0:T(8,128)} %shard_map.77.refs_0_), custom_call_target="tpu_custom_call", output_to_operand_aliasing={{}: (4, {})} | custom-call | flops 1048576 | bytes 2097152 | tf_op jit(solution)/shard_map/pallas_call | solution.py:190
  (12 shorter events, 0.0 us)
Async XLA Ops:
  6.5 57.6 %all-gather.3.cloned.1.call-start = ((), (), s32[]{:S(2)}) async-start(), calls=%async_computation.2 | async-start | bytes 6823936 | tf_op jit(solution)/shard_map/all_gather | solution.py:218
  9.4 15.6 %collective-permute-start = (f32[512,256]{1,0:T(8,128)}, f32[512,256]{1,0:T(8,128)S(1)}, u32[]{:S(2)}, u32[]{:S(2)}) collective-permute-start(f32[512,256]{1,0:T(8,128)} %get-tuple-element.8.refs_0_), channel_id=1, source_target_pairs={{0,4},{4,8},{8,12},{12,16},{16,20},{20,24},{24,28},{28,0},{1,5},{5... | collective-permute-start | bytes 1572872 | tf_op jit(solution)/shard_map/ppermute | solution.py:208
  12.7 15.8 %collective-permute-start.1 = (f32[512,256]{1,0:T(8,128)}, f32[512,256]{1,0:T(8,128)S(1)}, u32[]{:S(2)}, u32[]{:S(2)}) collective-permute-start(f32[512,256]{1,0:T(8,128)} %get-tuple-element.8.refs_0_), channel_id=1, source_target_pairs={{0,28},{4,0},{8,4},{12,8},{16,12},{20,16},{24,20},{28,24},{1,29},{... | collective-permute-start | bytes 1572872 | tf_op jit(solution)/shard_map/ppermute | solution.py:208
  25.0 39.1 %copy-start.2 = (f32[512,256]{1,0:T(8,128)}, f32[512,256]{1,0:T(8,128)S(1)}, u32[]{:S(2)}) copy-start(f32[512,256]{1,0:T(8,128)S(1)} %collective-permute-done.refs_1_) | copy-start | bytes 1572868
  25.0 13.9 %collective-permute-start.2 = (f32[512,256]{1,0:T(8,128)S(1)}, f32[512,256]{1,0:T(8,128)S(1)}, u32[]{:S(2)}, u32[]{:S(2)}) collective-permute-start(f32[512,256]{1,0:T(8,128)S(1)} %collective-permute-done.refs_1_), channel_id=1, source_target_pairs={{0,4},{4,8},{8,12},{12,16},{16,20},{20,24},{24,28},{28,0},{1,5},{5... | collective-permute-start | bytes 1572872 | tf_op jit(solution)/shard_map/ppermute | solution.py:208
  28.5 35.7 %copy-start.3 = (f32[512,256]{1,0:T(8,128)}, f32[512,256]{1,0:T(8,128)S(1)}, u32[]{:S(2)}) copy-start(f32[512,256]{1,0:T(8,128)S(1)} %collective-permute-done.1.refs_2_) | copy-start | bytes 1572868
  28.5 15.1 %collective-permute-start.3 = (f32[512,256]{1,0:T(8,128)S(1)}, f32[512,256]{1,0:T(8,128)S(1)}, u32[]{:S(2)}, u32[]{:S(2)}) collective-permute-start(f32[512,256]{1,0:T(8,128)S(1)} %collective-permute-done.1.refs_2_), channel_id=1, source_target_pairs={{0,28},{4,0},{8,4},{12,8},{16,12},{20,16},{24,20},{28,24},{1,29},{... | collective-permute-start | bytes 1572872 | tf_op jit(solution)/shard_map/ppermute | solution.py:208
  39.0 25.2 %copy-start.4 = (f32[512,256]{1,0:T(8,128)}, f32[512,256]{1,0:T(8,128)S(1)}, u32[]{:S(2)}) copy-start(f32[512,256]{1,0:T(8,128)S(1)} %collective-permute-done.2.refs_3_) | copy-start | bytes 1572868
  39.0 13.8 %collective-permute-start.4 = (f32[512,256]{1,0:T(8,128)S(1)}, f32[512,256]{1,0:T(8,128)S(1)}, u32[]{:S(2)}, u32[]{:S(2)}) collective-permute-start(f32[512,256]{1,0:T(8,128)S(1)} %collective-permute-done.2.refs_3_), channel_id=1, source_target_pairs={{0,4},{4,8},{8,12},{12,16},{16,20},{20,24},{24,28},{28,0},{1,5},{5... | collective-permute-start | bytes 1572872 | tf_op jit(solution)/shard_map/ppermute | solution.py:208
  43.6 20.5 %copy-start.5 = (f32[512,256]{1,0:T(8,128)}, f32[512,256]{1,0:T(8,128)S(1)}, u32[]{:S(2)}) copy-start(f32[512,256]{1,0:T(8,128)S(1)} %collective-permute-done.3.refs_4_) | copy-start | bytes 1572868
  43.6 15.0 %collective-permute-start.5 = (f32[512,256]{1,0:T(8,128)S(1)}, f32[512,256]{1,0:T(8,128)S(1)}, u32[]{:S(2)}, u32[]{:S(2)}) collective-permute-start(f32[512,256]{1,0:T(8,128)S(1)} %collective-permute-done.3.refs_4_), channel_id=1, source_target_pairs={{0,28},{4,0},{8,4},{12,8},{16,12},{20,16},{24,20},{28,24},{1,29},{... | collective-permute-start | bytes 1572872 | tf_op jit(solution)/shard_map/ppermute | solution.py:208
  52.8 11.4 %copy-start.6 = (f32[512,256]{1,0:T(8,128)}, f32[512,256]{1,0:T(8,128)S(1)}, u32[]{:S(2)}) copy-start(f32[512,256]{1,0:T(8,128)S(1)} %collective-permute-done.4.refs_5_) | copy-start | bytes 1572868
  52.8 18.5 %collective-permute-start.6 = (f32[512,256]{1,0:T(8,128)S(1)}, f32[512,256]{1,0:T(8,128)}, u32[]{:S(2)}, u32[]{:S(2)}) collective-permute-start(f32[512,256]{1,0:T(8,128)S(1)} %collective-permute-done.4.refs_5_), channel_id=1, source_target_pairs={{0,4},{4,8},{8,12},{12,16},{16,20},{20,24},{24,28},{28,0},{1,5},{5... | collective-permute-start | bytes 1572872 | tf_op jit(solution)/shard_map/ppermute | solution.py:208
  58.6 5.6 %copy-start.7 = (f32[512,256]{1,0:T(8,128)}, f32[512,256]{1,0:T(8,128)S(1)}, u32[]{:S(2)}) copy-start(f32[512,256]{1,0:T(8,128)S(1)} %collective-permute-done.5.refs_6_) | copy-start | bytes 1572868
  75.3 19.8 %all-to-all-start.1 = ((f32[4,128,512]{2,1,0:T(8,128)}), f32[4,128,512]{2,1,0:T(8,128)S(1)}, u32[]{:S(2)}, u32[]{:S(2)}) async-start(f32[4,128,512]{2,1,0:T(8,128)} %bitcast.13), calls=%async_computation.1 | async-start | bytes 2097152 | tf_op jit(solution)/shard_map/all_to_all | solution.py:230
  95.1 3.5 %copy-start = (f32[4,128,512]{2,1,0:T(8,128)}, f32[4,128,512]{2,1,0:T(8,128)S(1)}, u32[]{:S(2)}) copy-start(f32[4,128,512]{2,1,0:T(8,128)S(1)} %all-to-all-done.1.terms) | copy-start | bytes 3145732
  95.1 18.2 %all-to-all-start = ((f32[4,128,512]{2,1,0:T(8,128)}), f32[4,128,512]{2,1,0:T(8,128)S(1)}, u32[]{:S(2)}, u32[]{:S(2)}) async-start(f32[4,128,512]{2,1,0:T(8,128)} %bitcast.14), calls=%async_computation | async-start | bytes 2097152 | tf_op jit(solution)/shard_map/all_to_all | solution.py:230
  113.3 1.0 copy-start.1
Sparse Core Ops, SparseCore 0:
  9.5 54.6 all-gather.2

commit v9 on v8

--- a/solution.py
+++ b/solution.py
@@ -208,9 +208,11 @@
         return lax.ppermute(x, "col", shift(8, by))
 
     up1, down1 = send(own, 1), send(own, -1)
+    far = send(own, 4)
     up2, down2 = send(up1, 1), send(down1, -1)
+    up2, down2, far = lax.optimization_barrier((up2, down2, far))
     up3, down3 = send(up2, 1), send(down2, -1)
-    return [own, up1, down1, up2, down2, up3, down3, send(up3, 1)]
+    return [own, up1, down1, up2, down2, far, up3, down3]
 
 
 def local(left_slab, right_window, left_pattern, right_pattern, square_blocks, result_pattern):
@@ -218,7 +220,7 @@
     packed = lax.all_gather(packed, "row", axis=0, tiled=False)
     parts = gather_left(left)
     me = lax.axis_index("col")
-    where = lax.rem(me + jnp.array([8, 7, 9, 6, 10, 5, 11, 12], jnp.int32), 8)
+    where = lax.rem(me + jnp.array([8, 7, 9, 6, 10, 12, 5, 11], jnp.int32), 8)
     layer = lax.axis_index("layer").reshape((1,))
     out = ()
     for side in range(2):

time: 124 us -> 138 us (1.11)
  the two profiles are of different devices: /device:TPU:8 before, /device:TPU:384 now
where the time goes in v9:
time: 138 us; the launch traced here: 137 us
  waiting for transfers between devices  58.7 us (43%)
  starting transfers between devices  35.5 us (26%)
  Pallas kernels  26.7 us (19%)
  between operations  13.6 us (10%)
  local copies, waits for them, and re-layouts  1.78 us (1%)
    ppermute x7, waiting for transfers between devices, send(): return lax.ppermute(x, 'col', shift(8, by))  46.3 us
    ppermute x7, starting transfers between devices, send(): return lax.ppermute(x, 'col', shift(8, by))  28.1 us
    pallas_call x3, Pallas kernels, product(): pl.pallas_call(functools.partial(product_kernel, side, first, last), out_...  20 us
    all_to_all x2, waiting for transfers between devices, local(): terms = lax.all_to_all(cube.reshape(4, 128, 512), 'layer', 0, 0)  12.3 us
    all_to_all x2, starting transfers between devices, local(): terms = lax.all_to_all(cube.reshape(4, 128, 512), 'layer', 0, 0)  7.34 us
    pallas_call x2, Pallas kernels, finish(): pl.pallas_call(functools.partial(finish_kernel, side), out_shape=jax.Shap...  4.13 us
  transfers between devices with their start and end apart: 10, of which 7 were waited for; matrix products, arithmetic and copies ran while one was open for 1% of the time, Pallas kernels for 13%

profile of v9, /device:TPU:384, one launch (start us, length us, event | category | flops | bytes accessed | tf_op | source)
XLA Modules:
  0.0 137.4 jit_solution(16970864648339762166)
XLA Ops:
  6.5 2.6 %shard_map.73 = (f32[512,256]{1,0:T(8,128)}, f32[784,128]{1,0:T(8,128)}) custom-call(s32[4,8]{1,0:T(4,128)} %bitcast.17, f32[512,256]{1,0:T(8,128)} %bitcast.15, s32[2,16]{1,0:T(2,128)} %bitcast.18, f32[128,1024]{1,0:T(8,128)} %bitcast.16), custom_call_target="tpu_custom_call" | custom-call | tf_op jit(solution)/shard_map/pallas_call | solution.py:69
  9.2 0.0 all-gather.3.cloned.1.call-update
  9.2 5.3 %collective-permute-start.1 = (f32[512,256]{1,0:T(8,128)}, f32[512,256]{1,0:T(8,128)S(1)}, u32[]{:S(2)}, u32[]{:S(2)}) collective-permute-start(f32[512,256]{1,0:T(8,128)} %get-tuple-element.11.refs_0_), channel_id=1, source_target_pairs={{0,28},{4,0},{8,4},{12,8},{16,12},{20,16},{24,20},{28,24},{1,29},{... | collective-permute-start | bytes 1572872 | tf_op jit(solution)/shard_map/ppermute | solution.py:208
  14.5 1.9 %collective-permute-start = (f32[512,256]{1,0:T(8,128)}, f32[512,256]{1,0:T(8,128)S(1)}, u32[]{:S(2)}, u32[]{:S(2)}) collective-permute-start(f32[512,256]{1,0:T(8,128)} %get-tuple-element.11.refs_0_), channel_id=1, source_target_pairs={{0,4},{4,8},{8,12},{12,16},{16,20},{20,24},{24,28},{28,0},{1,5},{5... | collective-permute-start | bytes 1572872 | tf_op jit(solution)/shard_map/ppermute | solution.py:208
  16.4 6.5 %collective-permute-start.4 = (f32[512,256]{1,0:T(8,128)}, f32[512,256]{1,0:T(8,128)S(1)}, u32[]{:S(2)}, u32[]{:S(2)}) collective-permute-start(f32[512,256]{1,0:T(8,128)} %get-tuple-element.11.refs_0_), channel_id=1, source_target_pairs={{0,16},{4,20},{8,24},{12,28},{16,0},{20,4},{24,8},{28,12},{1,17},{... | collective-permute-start | bytes 1572872 | tf_op jit(solution)/shard_map/ppermute | solution.py:208
  22.9 25.8 %collective-permute-done.1.refs_2_ = f32[512,256]{1,0:T(8,128)S(1)} collective-permute-done((f32[512,256]{1,0:T(8,128)}, f32[512,256]{1,0:T(8,128)S(1)}, u32[]{:S(2)}, u32[]{:S(2)}) %collective-permute-start.1) | collective-permute-done | bytes 524320 | tf_op jit(solution)/shard_map/ppermute | solution.py:208
  48.7 5.5 %collective-permute-start.3 = (f32[512,256]{1,0:T(8,128)S(1)}, f32[512,256]{1,0:T(8,128)S(1)}, u32[]{:S(2)}, u32[]{:S(2)}) collective-permute-start(f32[512,256]{1,0:T(8,128)S(1)} %collective-permute-done.1.refs_2_), channel_id=1, source_target_pairs={{0,28},{4,0},{8,4},{12,8},{16,12},{20,16},{24,20},{28,24},{1,29},{... | collective-permute-start | bytes 1572872 | tf_op jit(solution)/shard_map/ppermute | solution.py:208
  54.2 0.0 collective-permute-done.refs_1_
  54.2 1.9 %collective-permute-start.2 = (f32[512,256]{1,0:T(8,128)S(1)}, f32[512,256]{1,0:T(8,128)S(1)}, u32[]{:S(2)}, u32[]{:S(2)}) collective-permute-start(f32[512,256]{1,0:T(8,128)S(1)} %collective-permute-done.refs_1_), channel_id=1, source_target_pairs={{0,4},{4,8},{8,12},{12,16},{16,20},{20,24},{24,28},{28,0},{1,5},{5... | collective-permute-start | bytes 1572872 | tf_op jit(solution)/shard_map/ppermute | solution.py:208
  56.1 0.4 collective-permute-done.4.refs_5_
  56.5 8.2 %collective-permute-done.3.refs_4_ = f32[512,256]{1,0:T(8,128)S(1)} collective-permute-done((f32[512,256]{1,0:T(8,128)S(1)}, f32[512,256]{1,0:T(8,128)S(1)}, u32[]{:S(2)}, u32[]{:S(2)}) %collective-permute-start.3) | collective-permute-done | bytes 524320 | tf_op jit(solution)/shard_map/ppermute | solution.py:208
  64.7 5.3 %collective-permute-done.2.refs_3_ = f32[512,256]{1,0:T(8,128)S(1)} collective-permute-done((f32[512,256]{1,0:T(8,128)S(1)}, f32[512,256]{1,0:T(8,128)S(1)}, u32[]{:S(2)}, u32[]{:S(2)}) %collective-permute-start.2) | collective-permute-done | bytes 524320 | tf_op jit(solution)/shard_map/ppermute | solution.py:208
  70.0 1.9 %collective-permute-start.5 = (f32[512,256]{1,0:T(8,128)S(1)}, f32[512,256]{1,0:T(8,128)S(1)}, u32[]{:S(2)}, u32[]{:S(2)}) collective-permute-start(f32[512,256]{1,0:T(8,128)S(1)} %collective-permute-done.2.refs_3_), channel_id=1, source_target_pairs={{0,4},{4,8},{8,12},{12,16},{16,20},{20,24},{24,28},{28,0},{1,5},{5... | collective-permute-start | bytes 1572872 | tf_op jit(solution)/shard_map/ppermute | solution.py:208
  71.9 5.1 %collective-permute-start.6 = (f32[512,256]{1,0:T(8,128)S(1)}, f32[512,256]{1,0:T(8,128)}, u32[]{:S(2)}, u32[]{:S(2)}) collective-permute-start(f32[512,256]{1,0:T(8,128)S(1)} %collective-permute-done.3.refs_4_), channel_id=1, source_target_pairs={{0,28},{4,0},{8,4},{12,8},{16,12},{20,16},{24,20},{28,24},{1,29},{... | collective-permute-start | bytes 1572872 | tf_op jit(solution)/shard_map/ppermute | solution.py:208
  77.1 1.2 compare_select_fusion.where
  78.3 6.6 %collective-permute-done.5.refs_6_ = f32[512,256]{1,0:T(8,128)S(1)} collective-permute-done((f32[512,256]{1,0:T(8,128)S(1)}, f32[512,256]{1,0:T(8,128)S(1)}, u32[]{:S(2)}, u32[]{:S(2)}) %collective-permute-start.5) | collective-permute-done | bytes 524320 | tf_op jit(solution)/shard_map/ppermute | solution.py:208
  84.9 0.0 copy-done.2
  84.9 0.0 copy-done.4
  85.0 0.0 copy-done.5
  85.0 0.0 copy-done.6
  85.0 0.8 copy-done.7
  85.7 7.0 %shard_map.75.refs_1_ = f32[512,512]{1,0:T(8,128)} custom-call(s32[8]{0:T(128)} %compare_select_fusion.where, f32[16,784,128]{2,1,0:T(8,128)} %bitcast.10, f32[512,256]{1,0:T(8,128)} %get-tuple-element.11.refs_0_, f32[512,256]{1,0:T(8,128)} %copy-done.3, f32[512,256]{1,0:T(8,128)} %copy-done.2, f32[512,256]{1,0:T(8,128)} %copy-done.6, f32[512,256]{1,0:T(8,128)} %copy-done.5, ...), custom_call_target="tpu_custom_call" | custom-call | flops 2818572288 | bytes 7340032 | tf_op jit(solution)/shard_map/pallas_call | solution.py:154
  92.8 0.0 collective-permute-done.6.refs_7_.refs_0_
  92.8 4.1 %shard_map.76 = f32[512,512]{1,0:T(8,128)} custom-call(s32[8]{0:T(128)} %compare_select_fusion.where, f32[16,784,128]{2,1,0:T(8,128)} %bitcast.11, f32[512,256]{1,0:T(8,128)} %collective-permute-done.6.refs_7_.refs_0_, f32[512,512]{1,0:T(8,128)} %shard_map.75.refs_1_), custom_call_target="tpu_custom_call" | custom-call | flops 402653184 | bytes 1048576 | tf_op jit(solution)/shard_map/pallas_call | solution.py:154
  96.9 3.8 %all-to-all-start.1 = ((f32[4,128,512]{2,1,0:T(8,128)}), f32[4,128,512]{2,1,0:T(8,128)S(1)}, u32[]{:S(2)}, u32[]{:S(2)}) async-start(f32[4,128,512]{2,1,0:T(8,128)} %bitcast.13), calls=%async_computation.1 | async-start | bytes 2097152 | tf_op jit(solution)/shard_map/all_to_all | solution.py:232
  100.7 8.9 %shard_map.74 = f32[512,512]{1,0:T(8,128)} custom-call(s32[8]{0:T(128)} %compare_select_fusion.where, f32[16,784,128]{2,1,0:T(8,128)} %bitcast.12, f32[512,256]{1,0:T(8,128)} %get-tuple-element.11.refs_0_, f32[512,256]{1,0:T(8,128)} %copy-done.3, f32[512,256]{1,0:T(8,128)} %copy-done.2, f32[512,256]{1,0:T(8,128)} %copy-done.6, f32[512,256]{1,0:T(8,128)} %copy-done.5, ...), custom_call_target="tpu_custom_call" | custom-call | flops 3221225472 | bytes 8388608 | tf_op jit(solution)/shard_map/pallas_call | solution.py:154
  109.6 3.4 %all-to-all-done.1.terms = f32[4,128,512]{2,1,0:T(8,128)S(1)} async-done(((f32[4,128,512]{2,1,0:T(8,128)}), f32[4,128,512]{2,1,0:T(8,128)S(1)}, u32[]{:S(2)}, u32[]{:S(2)}) %all-to-all-start.1) | async-done | bytes 1048608 | tf_op jit(solution)/shard_map/all_to_all | solution.py:232
  113.0 3.5 %all-to-all-start = ((f32[4,128,512]{2,1,0:T(8,128)}), f32[4,128,512]{2,1,0:T(8,128)S(1)}, u32[]{:S(2)}, u32[]{:S(2)}) async-start(f32[4,128,512]{2,1,0:T(8,128)} %bitcast.14), calls=%async_computation | async-start | bytes 2097152 | tf_op jit(solution)/shard_map/all_to_all | solution.py:232
  116.5 2.1 %shard_map.77.refs_0_ = f32[128,1024]{1,0:T(8,128)} custom-call(s32[1]{0:T(128)} %bitcast.where, s32[8,16]{1,0:T(8,128)} %flags.3, f32[4,128,512]{2,1,0:T(8,128)} %copy-done, f32[128,1024]{1,0:T(8,128)} %square.3), custom_call_target="tpu_custom_call" | custom-call | flops 1048576 | bytes 2097152 | tf_op jit(solution)/shard_map/pallas_call | solution.py:190
  118.6 8.9 %all-to-all-done.terms = f32[4,128,512]{2,1,0:T(8,128)S(1)} async-done(((f32[4,128,512]{2,1,0:T(8,128)}), f32[4,128,512]{2,1,0:T(8,128)S(1)}, u32[]{:S(2)}, u32[]{:S(2)}) %all-to-all-start) | async-done | bytes 1048608 | tf_op jit(solution)/shard_map/all_to_all | solution.py:232
  127.5 1.0 copy-done.1
  128.5 2.1 %shard_map.78 = f32[128,1024]{1,0:T(8,128)} custom-call(s32[1]{0:T(128)} %bitcast.where, s32[8,16]{1,0:T(8,128)} %flags.3, f32[4,128,512]{2,1,0:T(8,128)} %copy-done.1, f32[128,1024]{1,0:T(8,128)} %square.3, f32[128,1024]{1,0:T(8,128)} %shard_map.77.refs_0_), custom_call_target="tpu_custom_call", output_to_operand_aliasing={{}: (4, {})} | custom-call | flops 1048576 | bytes 2097152 | tf_op jit(solution)/shard_map/pallas_call | solution.py:190
  (12 shorter events, 0.0 us)
Async XLA Ops:
  6.5 78.4 %all-gather.3.cloned.1.call-start = ((), (), s32[]{:S(2)}) async-start(), calls=%async_computation.2 | async-start | bytes 6823936 | tf_op jit(solution)/shard_map/all_gather | solution.py:220
  9.2 39.5 %collective-permute-start.1 = (f32[512,256]{1,0:T(8,128)}, f32[512,256]{1,0:T(8,128)S(1)}, u32[]{:S(2)}, u32[]{:S(2)}) collective-permute-start(f32[512,256]{1,0:T(8,128)} %get-tuple-element.11.refs_0_), channel_id=1, source_target_pairs={{0,28},{4,0},{8,4},{12,8},{16,12},{20,16},{24,20},{28,24},{1,29},{... | collective-permute-start | bytes 1572872 | tf_op jit(solution)/shard_map/ppermute | solution.py:208
  14.5 39.6 %collective-permute-start = (f32[512,256]{1,0:T(8,128)}, f32[512,256]{1,0:T(8,128)S(1)}, u32[]{:S(2)}, u32[]{:S(2)}) collective-permute-start(f32[512,256]{1,0:T(8,128)} %get-tuple-element.11.refs_0_), channel_id=1, source_target_pairs={{0,4},{4,8},{8,12},{12,16},{16,20},{20,24},{24,28},{28,0},{1,5},{5... | collective-permute-start | bytes 1572872 | tf_op jit(solution)/shard_map/ppermute | solution.py:208
  16.4 40.0 %collective-permute-start.4 = (f32[512,256]{1,0:T(8,128)}, f32[512,256]{1,0:T(8,128)S(1)}, u32[]{:S(2)}, u32[]{:S(2)}) collective-permute-start(f32[512,256]{1,0:T(8,128)} %get-tuple-element.11.refs_0_), channel_id=1, source_target_pairs={{0,16},{4,20},{8,24},{12,28},{16,0},{20,4},{24,8},{28,12},{1,17},{... | collective-permute-start | bytes 1572872 | tf_op jit(solution)/shard_map/ppermute | solution.py:208
  48.7 36.3 %copy-start.2 = (f32[512,256]{1,0:T(8,128)}, f32[512,256]{1,0:T(8,128)S(1)}, u32[]{:S(2)}) copy-start(f32[512,256]{1,0:T(8,128)S(1)} %collective-permute-done.1.refs_2_) | copy-start | bytes 1572868
  48.7 16.0 %collective-permute-start.3 = (f32[512,256]{1,0:T(8,128)S(1)}, f32[512,256]{1,0:T(8,128)S(1)}, u32[]{:S(2)}, u32[]{:S(2)}) collective-permute-start(f32[512,256]{1,0:T(8,128)S(1)} %collective-permute-done.1.refs_2_), channel_id=1, source_target_pairs={{0,28},{4,0},{8,4},{12,8},{16,12},{20,16},{24,20},{28,24},{1,29},{... | collective-permute-start | bytes 1572872 | tf_op jit(solution)/shard_map/ppermute | solution.py:208
  54.2 30.8 %copy-start.3 = (f32[512,256]{1,0:T(8,128)}, f32[512,256]{1,0:T(8,128)S(1)}, u32[]{:S(2)}) copy-start(f32[512,256]{1,0:T(8,128)S(1)} %collective-permute-done.refs_1_) | copy-start | bytes 1572868
  54.2 15.8 %collective-permute-start.2 = (f32[512,256]{1,0:T(8,128)S(1)}, f32[512,256]{1,0:T(8,128)S(1)}, u32[]{:S(2)}, u32[]{:S(2)}) collective-permute-start(f32[512,256]{1,0:T(8,128)S(1)} %collective-permute-done.refs_1_), channel_id=1, source_target_pairs={{0,4},{4,8},{8,12},{12,16},{16,20},{20,24},{24,28},{28,0},{1,5},{5... | collective-permute-start | bytes 1572872 | tf_op jit(solution)/shard_map/ppermute | solution.py:208
  56.5 28.5 %copy-start.4 = (f32[512,256]{1,0:T(8,128)}, f32[512,256]{1,0:T(8,128)S(1)}, u32[]{:S(2)}) copy-start(f32[512,256]{1,0:T(8,128)S(1)} %collective-permute-done.4.refs_5_) | copy-start | bytes 1572868
  64.7 20.3 %copy-start.5 = (f32[512,256]{1,0:T(8,128)}, f32[512,256]{1,0:T(8,128)S(1)}, u32[]{:S(2)}) copy-start(f32[512,256]{1,0:T(8,128)S(1)} %collective-permute-done.3.refs_4_) | copy-start | bytes 1572868
  70.0 15.0 %copy-start.6 = (f32[512,256]{1,0:T(8,128)}, f32[512,256]{1,0:T(8,128)S(1)}, u32[]{:S(2)}) copy-start(f32[512,256]{1,0:T(8,128)S(1)} %collective-permute-done.2.refs_3_) | copy-start | bytes 1572868
  70.0 14.9 %collective-permute-start.5 = (f32[512,256]{1,0:T(8,128)S(1)}, f32[512,256]{1,0:T(8,128)S(1)}, u32[]{:S(2)}, u32[]{:S(2)}) collective-permute-start(f32[512,256]{1,0:T(8,128)S(1)} %collective-permute-done.2.refs_3_), channel_id=1, source_target_pairs={{0,4},{4,8},{8,12},{12,16},{16,20},{20,24},{24,28},{28,0},{1,5},{5... | collective-permute-start | bytes 1572872 | tf_op jit(solution)/shard_map/ppermute | solution.py:208
  71.9 20.9 %collective-permute-start.6 = (f32[512,256]{1,0:T(8,128)S(1)}, f32[512,256]{1,0:T(8,128)}, u32[]{:S(2)}, u32[]{:S(2)}) collective-permute-start(f32[512,256]{1,0:T(8,128)S(1)} %collective-permute-done.3.refs_4_), channel_id=1, source_target_pairs={{0,28},{4,0},{8,4},{12,8},{16,12},{20,16},{24,20},{28,24},{1,29},{... | collective-permute-start | bytes 1572872 | tf_op jit(solution)/shard_map/ppermute | solution.py:208
  84.9 0.8 copy-start.7
  96.9 16.1 %all-to-all-start.1 = ((f32[4,128,512]{2,1,0:T(8,128)}), f32[4,128,512]{2,1,0:T(8,128)S(1)}, u32[]{:S(2)}, u32[]{:S(2)}) async-start(f32[4,128,512]{2,1,0:T(8,128)} %bitcast.13), calls=%async_computation.1 | async-start | bytes 2097152 | tf_op jit(solution)/shard_map/all_to_all | solution.py:232
  113.0 3.5 %copy-start = (f32[4,128,512]{2,1,0:T(8,128)}, f32[4,128,512]{2,1,0:T(8,128)S(1)}, u32[]{:S(2)}) copy-start(f32[4,128,512]{2,1,0:T(8,128)S(1)} %all-to-all-done.1.terms) | copy-start | bytes 3145732
  113.0 14.5 %all-to-all-start = ((f32[4,128,512]{2,1,0:T(8,128)}), f32[4,128,512]{2,1,0:T(8,128)S(1)}, u32[]{:S(2)}, u32[]{:S(2)}) async-start(f32[4,128,512]{2,1,0:T(8,128)} %bitcast.14), calls=%async_computation | async-start | bytes 2097152 | tf_op jit(solution)/shard_map/all_to_all | solution.py:232
  127.5 1.0 copy-start.1
Sparse Core Ops, SparseCore 0:
  9.5 47.7 all-gather.2

commit v10 on v4

--- a/solution.py
+++ b/solution.py
@@ -82,16 +82,10 @@
 
 def product_kernel(side, first, last, where, packed, *refs):
     steps = range(first, last)
-    count = sum(2 if k == 7 else 1 for k in steps)
-    parts, refs = refs[:count], refs[count:]
-    if first:
-        before, refs = refs[0], refs[1:]
+    parts, refs = refs[: last - first], refs[last - first :]
     out, tiles, lefts, high0, high1, low0, low1, homes, tile_sems, left_sems, home_sem = refs
     need = tiles.shape[2]
     copies = {}
-    if first:
-        sum_copy = pltpu.make_async_copy(before, out, home_sem)
-        sum_copy.start()
     if side:
         home_copy = pltpu.make_async_copy(packed.at[:, pl.ds(0, 1), :], homes, home_sem)
         home_copy.start()
@@ -99,15 +93,9 @@
         n = k - first
         tile = pltpu.make_async_copy(packed.at[pl.ds(where[k] * 2, 2), pl.ds(0, need), :], tiles.at[n], tile_sems.at[n])
         tile.start()
-        if k < 7:
-            pieces = [pltpu.make_async_copy(parts[n], lefts.at[n], left_sems.at[n])]
-        else:
-            pieces = [
-                pltpu.make_async_copy(parts[n + h], lefts.at[n, pl.ds(h * 256, 256)], left_sems.at[n + h]) for h in range(2)
-            ]
-        for piece in pieces:
-            piece.start()
-        copies[k] = [tile] + pieces
+        part = pltpu.make_async_copy(parts[n], lefts.at[n], left_sems.at[n])
+        part.start()
+        copies[k] = [tile, part]
     half = lane_half()
     if side:
         home_copy.wait()
@@ -144,14 +132,12 @@
         total = jnp.dot(left_low, high[...], preferred_element_type=F32)
         total += jnp.dot(left_high, low[...], preferred_element_type=F32)
         total += jnp.dot(left_high, high[...], preferred_element_type=F32)
-        if k == first and first:
-            sum_copy.wait()
         if k:
             total += out[...]
         out[...] = total
 
 
-def product(side, first, last, parts, where, packed, *before):
+def product(side, first, last, parts, where, packed):
     smem = pl.BlockSpec(memory_space=pltpu.SMEM)
     hbm = pl.BlockSpec(memory_space=pltpu.HBM)
     vmem = pl.BlockSpec(memory_space=pltpu.VMEM)
@@ -161,7 +147,7 @@
     return pl.pallas_call(
         functools.partial(product_kernel, side, first, last),
         out_shape=jax.ShapeDtypeStruct((512, 512), F32),
-        in_specs=[smem] + [hbm] * (1 + len(parts)) + [hbm] * len(before),
+        in_specs=[smem] + [hbm] * (1 + len(parts)),
         out_specs=vmem,
         scratch_shapes=[
             pltpu.VMEM((steps, 2, need, LANES), F32),
@@ -172,29 +158,66 @@
             half,
             pltpu.SMEM((16, 1, LANES), F32),
             pltpu.SemaphoreType.DMA((steps,)),
-            pltpu.SemaphoreType.DMA((steps + 1,)),
+            pltpu.SemaphoreType.DMA((steps,)),
             pltpu.SemaphoreType.DMA,
         ],
         cost_estimate=pl.CostEstimate(flops=6 * 512 * 512 * 256 * steps, bytes_accessed=steps << 20, transcendentals=0),
         compiler_params=pltpu.CompilerParams(vmem_limit_bytes=56 << 20),
-    )(where, packed, *parts, *before)
-
-
-def finish_kernel(where, flags, summed, terms, square, out):
+    )(where, packed, *parts)
+
+
+def last_kernel(where, tiles, left, before, out, rights_high, rights_low):
+    @pl.when(pl.program_id(0) == 0)
+    def _():
+        for z in range(2):
+            for b in range(2):
+                for c in range(4):
+                    mask = tiles[z, pl.ds(1 + c * 2 + b, 1), :]
+                    value = tiles[z, pl.ds(META + c * LANES + b * BS, BS), :] * mask
+                    at = (pl.ds(z * LANES + b * BS, BS), pl.ds(c * LANES, LANES))
+                    rights_high[at], rights_low[at] = split(value)
+
+    left_high, left_low = split(left[...])
+    total = jnp.dot(left_low, rights_high[...], preferred_element_type=F32)
+    total += jnp.dot(left_high, rights_low[...], preferred_element_type=F32)
+    total += jnp.dot(left_high, rights_high[...], preferred_element_type=F32)
+    out[...] = before[...] + total
+
+
+def add_last(part, where, packed, before):
+    rows = pl.BlockSpec((256, 512), lambda i, where: (i, 0))
+    return pl.pallas_call(
+        last_kernel,
+        out_shape=jax.ShapeDtypeStruct((512, 512), F32),
+        grid_spec=pltpu.PrefetchScalarGridSpec(
+            num_scalar_prefetch=1,
+            grid=(2,),
+            in_specs=[
+                pl.BlockSpec((2, META + 4 * LANES, LANES), lambda i, where: (where[7], 0, 0)),
+                pl.BlockSpec((256, 256), lambda i, where: (i, 0)),
+                rows,
+            ],
+            out_specs=rows,
+            scratch_shapes=[pltpu.VMEM((256, 512), BF)] * 2,
+        ),
+        cost_estimate=pl.CostEstimate(flops=6 * 512 * 512 * 256, bytes_accessed=3 << 20, transcendentals=0),
+        compiler_params=pltpu.CompilerParams(vmem_limit_bytes=56 << 20),
+    )(where, packed, part, before)
+
+
+def finish_kernel(layer, flags, terms0, terms1, square, out):
     for b in range(2):
         for c in range(8):
+            terms = terms1 if c >= 4 else terms0
             at = (pl.ds(b * BS, BS), pl.ds(c * LANES, LANES))
             near = (pl.ds(b * BS, BS), pl.ds(c % 4 * LANES, LANES))
-            if c < 4:
-                total = summed[near]
-            else:
-                total = (terms[(0,) + near] + terms[(1,) + near]) + (terms[(2,) + near] + terms[(3,) + near])
-            line = where[0] * 2 + b
+            total = (terms[(0,) + near] + terms[(1,) + near]) + (terms[(2,) + near] + terms[(3,) + near])
+            line = layer[0] * 2 + b
             mask = pair_mask(flags[line, 2 * c], flags[line, 2 * c + 1])
             out[at] = mask * (3.0 * square[at] - 2.0 * total)
 
 
-def finish(summed, terms, square, flags, where):
+def finish(terms, square, flags, layer):
     smem = pl.BlockSpec(memory_space=pltpu.SMEM)
     vmem = pl.BlockSpec(memory_space=pltpu.VMEM)
     return pl.pallas_call(
@@ -202,9 +225,8 @@
         out_shape=jax.ShapeDtypeStruct(square.shape, F32),
         in_specs=[smem, smem, vmem, vmem, vmem],
         out_specs=vmem,
-        cost_estimate=pl.CostEstimate(flops=1 << 20, bytes_accessed=2 << 20, transcendentals=0),
-        compiler_params=pltpu.CompilerParams(vmem_limit_bytes=56 << 20),
-    )(where, flags, summed, terms, square)
+        cost_estimate=pl.CostEstimate(flops=1 << 20, bytes_accessed=3 << 20, transcendentals=0),
+    )(layer, flags, *terms, square)
 
 
 def shift(n, by):
@@ -218,8 +240,7 @@
     up1, down1 = send(own, 1), send(own, -1)
     up2, down2 = send(up1, 1), send(down1, -1)
     up3, down3 = send(up2, 1), send(down2, -1)
-    far_a, far_b = send(up3[:256], 1), send(down3[256:], -1)
-    return [own, up1, down1, up2, down2, up3, down3, far_a, far_b]
+    return [own, up1, down1, up2, down2, up3, down3, send(up3, 1)]
 
 
 def local(left_slab, right_window, left_pattern, right_pattern, square_blocks, result_pattern):
@@ -230,11 +251,11 @@
     where = lax.rem(me + jnp.array([8, 7, 9, 6, 10, 5, 11, 12], jnp.int32), 8)
     layer = lax.axis_index("layer").reshape((1,))
     cube = product(0, 0, 7, parts[:7], where, packed)
-    cube = product(0, 7, 8, parts[7:], where, packed, cube)
-    summed = lax.psum_scatter(cube, "layer", scatter_dimension=0, tiled=True)
+    cube = add_last(parts[7], where, packed, cube)
+    terms = [lax.all_to_all(cube.reshape(4, 128, 512), "layer", 0, 0)]
     cube = product(1, 0, 8, parts, where, packed)
-    terms = lax.all_to_all(cube.reshape(4, 128, 512), "layer", 0, 0)
-    return finish(summed, terms, square_blocks, result_pattern, layer)
+    terms.append(lax.all_to_all(cube.reshape(4, 128, 512), "layer", 0, 0))
+    return finish(terms, square_blocks, result_pattern, layer)
 
 
 def solution(mesh):

time: 124 us -> 125 us (level)
  the two profiles are of different devices: /device:TPU:1 before, /device:TPU:448 now
where the time goes in v10:
time: 125 us; the launch traced here: 124 us
  waiting for transfers between devices  51.9 us (42%)
  starting transfers between devices  31.4 us (25%)
  Pallas kernels  24.9 us (20%)
  between operations  13.5 us (11%)
    ppermute x7, waiting for transfers between devices, send(): return lax.ppermute(x, 'col', shift(8, by))  39.3 us
    ppermute x7, starting transfers between devices, send(): return lax.ppermute(x, 'col', shift(8, by))  23.4 us
    pallas_call x2, Pallas kernels, product(): pl.pallas_call(functools.partial(product_kernel, side, first, last), out_...  16 us
    all_to_all x1, waiting for transfers between devices, local(): terms = [lax.all_to_all(cube.reshape(4, 128, 512), 'layer', 0, 0)]  11.4 us
    all_to_all x1, starting transfers between devices, local(): terms.append(lax.all_to_all(cube.reshape(4, 128, 512), 'layer', 0, 0))  4.34 us
    all_to_all x1, starting transfers between devices, local(): terms = [lax.all_to_all(cube.reshape(4, 128, 512), 'layer', 0, 0)]  3.66 us
    pallas_call x1, Pallas kernels, add_last(): pl.pallas_call(last_kernel, out_shape=jax.ShapeDtypeStruct((512, 512), F3...  3.66 us
    pallas_call x1, Pallas kernels, finish(): pl.pallas_call(finish_kernel, out_shape=jax.ShapeDtypeStruct(square.shape...  2.63 us
  transfers between devices with their start and end apart: 10, of which 6 were waited for; matrix products, arithmetic and copies ran while one was open for 1% of the time, Pallas kernels for 9%

profile of v10, /device:TPU:448, one launch (start us, length us, event | category | flops | bytes accessed | tf_op | source)
XLA Modules:
  0.0 124.0 jit_solution(11167256273892643704)
XLA Ops:
  6.5 0.0 all-gather.3.cloned.1.call-start
  6.5 2.6 %shard_map.73 = (f32[512,256]{1,0:T(8,128)}, f32[784,128]{1,0:T(8,128)}) custom-call(s32[4,8]{1,0:T(4,128)} %bitcast.17, f32[512,256]{1,0:T(8,128)} %bitcast.15, s32[2,16]{1,0:T(2,128)} %bitcast.18, f32[128,1024]{1,0:T(8,128)} %bitcast.16), custom_call_target="tpu_custom_call" | custom-call | tf_op jit(solution)/shard_map/pallas_call | solution.py:69
  9.2 0.0 all-gather.3.cloned.1.call-update
  9.2 3.6 %collective-permute-start = (f32[512,256]{1,0:T(8,128)}, f32[512,256]{1,0:T(8,128)S(1)}, u32[]{:S(2)}, u32[]{:S(2)}) collective-permute-start(f32[512,256]{1,0:T(8,128)} %get-tuple-element.8.refs_0_), channel_id=1, source_target_pairs={{0,4},{4,8},{8,12},{12,16},{16,20},{20,24},{24,28},{28,0},{1,5},{5... | collective-permute-start | bytes 1572872 | tf_op jit(solution)/shard_map/ppermute | solution.py:238
  12.8 3.8 %collective-permute-start.4 = (f32[512,256]{1,0:T(8,128)}, f32[512,256]{1,0:T(8,128)S(1)}, u32[]{:S(2)}, u32[]{:S(2)}) collective-permute-start(f32[512,256]{1,0:T(8,128)} %get-tuple-element.8.refs_0_), channel_id=1, source_target_pairs={{0,28},{4,0},{8,4},{12,8},{16,12},{20,16},{24,20},{28,24},{1,29},{... | collective-permute-start | bytes 1572872 | tf_op jit(solution)/shard_map/ppermute | solution.py:238
  16.6 10.2 %collective-permute-done.refs_1_ = f32[512,256]{1,0:T(8,128)S(1)} collective-permute-done((f32[512,256]{1,0:T(8,128)}, f32[512,256]{1,0:T(8,128)S(1)}, u32[]{:S(2)}, u32[]{:S(2)}) %collective-permute-start) | collective-permute-done | bytes 524320 | tf_op jit(solution)/shard_map/ppermute | solution.py:238
  26.8 1.9 %collective-permute-start.1 = (f32[512,256]{1,0:T(8,128)S(1)}, f32[512,256]{1,0:T(8,128)S(1)}, u32[]{:S(2)}, u32[]{:S(2)}) collective-permute-start(f32[512,256]{1,0:T(8,128)S(1)} %collective-permute-done.refs_1_), channel_id=1, source_target_pairs={{0,4},{4,8},{8,12},{12,16},{16,20},{20,24},{24,28},{28,0},{1,5},{5... | collective-permute-start | bytes 1572872 | tf_op jit(solution)/shard_map/ppermute | solution.py:238
  28.7 0.0 collective-permute-done.4.refs_2_
  28.7 0.0 copy-start.3
  28.7 5.1 %collective-permute-start.5 = (f32[512,256]{1,0:T(8,128)S(1)}, f32[512,256]{1,0:T(8,128)S(1)}, u32[]{:S(2)}, u32[]{:S(2)}) collective-permute-start(f32[512,256]{1,0:T(8,128)S(1)} %collective-permute-done.4.refs_2_), channel_id=1, source_target_pairs={{0,28},{4,0},{8,4},{12,8},{16,12},{20,16},{24,20},{28,24},{1,29},{... | collective-permute-start | bytes 1572872 | tf_op jit(solution)/shard_map/ppermute | solution.py:238
  33.8 9.2 %collective-permute-done.1.refs_3_ = f32[512,256]{1,0:T(8,128)S(1)} collective-permute-done((f32[512,256]{1,0:T(8,128)S(1)}, f32[512,256]{1,0:T(8,128)S(1)}, u32[]{:S(2)}, u32[]{:S(2)}) %collective-permute-start.1) | collective-permute-done | bytes 524320 | tf_op jit(solution)/shard_map/ppermute | solution.py:238
  43.1 1.9 %collective-permute-start.2 = (f32[512,256]{1,0:T(8,128)S(1)}, f32[512,256]{1,0:T(8,128)S(1)}, u32[]{:S(2)}, u32[]{:S(2)}) collective-permute-start(f32[512,256]{1,0:T(8,128)S(1)} %collective-permute-done.1.refs_3_), channel_id=1, source_target_pairs={{0,4},{4,8},{8,12},{12,16},{16,20},{20,24},{24,28},{28,0},{1,5},{5... | collective-permute-start | bytes 1572872 | tf_op jit(solution)/shard_map/ppermute | solution.py:238
  45.0 0.0 collective-permute-done.5.refs_4_
  45.0 0.0 copy-start.5
  45.0 5.1 %collective-permute-start.6 = (f32[512,256]{1,0:T(8,128)S(1)}, f32[512,256]{1,0:T(8,128)S(1)}, u32[]{:S(2)}, u32[]{:S(2)}) collective-permute-start(f32[512,256]{1,0:T(8,128)S(1)} %collective-permute-done.5.refs_4_), channel_id=1, source_target_pairs={{0,28},{4,0},{8,4},{12,8},{16,12},{20,16},{24,20},{28,24},{1,29},{... | collective-permute-start | bytes 1572872 | tf_op jit(solution)/shard_map/ppermute | solution.py:238
  50.1 8.4 %collective-permute-done.2.refs_5_ = f32[512,256]{1,0:T(8,128)S(1)} collective-permute-done((f32[512,256]{1,0:T(8,128)S(1)}, f32[512,256]{1,0:T(8,128)S(1)}, u32[]{:S(2)}, u32[]{:S(2)}) %collective-permute-start.2) | collective-permute-done | bytes 524320 | tf_op jit(solution)/shard_map/ppermute | solution.py:238
  58.5 1.9 %collective-permute-start.3 = (f32[512,256]{1,0:T(8,128)S(1)}, f32[512,256]{1,0:T(8,128)}, u32[]{:S(2)}, u32[]{:S(2)}) collective-permute-start(f32[512,256]{1,0:T(8,128)S(1)} %collective-permute-done.2.refs_5_), channel_id=1, source_target_pairs={{0,4},{4,8},{8,12},{12,16},{16,20},{20,24},{24,28},{28,0},{1,5},{5... | collective-permute-start | bytes 1572872 | tf_op jit(solution)/shard_map/ppermute | solution.py:238
  60.5 1.2 %compare_select_fusion.where = s32[8]{0:T(128)} fusion(s32[8]{0:T(128)} %constant.16.clone, s32[]{:T(128)S(6)} %axis_index.25), kind=kLoop, calls=%fused_computation | loop fusion | flops 56 | bytes 68 | tf_op jit(solution)/shard_map/rem | solution.py:251
  61.7 0.0 collective-permute-done.6.refs_6_
  61.7 11.5 %collective-permute-done.3.left.refs_7_ = f32[512,256]{1,0:T(8,128)} collective-permute-done((f32[512,256]{1,0:T(8,128)S(1)}, f32[512,256]{1,0:T(8,128)}, u32[]{:S(2)}, u32[]{:S(2)}) %collective-permute-start.3) | collective-permute-done | bytes 524320 | tf_op jit(solution)/shard_map/ppermute | solution.py:238
  73.2 0.0 copy-done.2
  73.2 0.0 copy-done.3
  73.2 0.0 copy-done.4
  73.2 8.9 %shard_map.76 = f32[512,512]{1,0:T(8,128)} custom-call(s32[8]{0:T(128)} %compare_select_fusion.where, f32[16,784,128]{2,1,0:T(8,128)} %bitcast.10, f32[512,256]{1,0:T(8,128)} %get-tuple-element.8.refs_0_, f32[512,256]{1,0:T(8,128)} %copy-done.2, f32[512,256]{1,0:T(8,128)} %copy-done.3, f32[512,256]{1,0:T(8,128)} %copy-done.4, f32[512,256]{1,0:T(8,128)} %copy-done.5, ...), custom_call_target="tpu_custom_call" | custom-call | flops 3221225472 | bytes 8388608 | tf_op jit(solution)/shard_map/pallas_call | solution.py:147
  82.1 4.3 %all-to-all-start.1 = ((f32[4,128,512]{2,1,0:T(8,128)}), f32[4,128,512]{2,1,0:T(8,128)S(1)}, u32[]{:S(2)}, u32[]{:S(2)}) async-start(f32[4,128,512]{2,1,0:T(8,128)} %bitcast.14), calls=%async_computation.1 | async-start | bytes 2097152 | tf_op jit(solution)/shard_map/all_to_all | solution.py:257
  86.5 7.2 %shard_map.74.before = f32[512,512]{1,0:T(8,128)} custom-call(s32[8]{0:T(128)} %compare_select_fusion.where, f32[16,784,128]{2,1,0:T(8,128)} %bitcast.11, f32[512,256]{1,0:T(8,128)} %get-tuple-element.8.refs_0_, f32[512,256]{1,0:T(8,128)} %copy-done.2, f32[512,256]{1,0:T(8,128)} %copy-done.3, f32[512,256]{1,0:T(8,128)} %copy-done.4, f32[512,256]{1,0:T(8,128)} %copy-done.5, ...), custom_call_target="tpu_custom_call" | custom-call | flops 2818572288 | bytes 7340032 | tf_op jit(solution)/shard_map/pallas_call | solution.py:147
  93.6 3.7 %shard_map.75 = f32[512,512]{1,0:T(8,128)} custom-call(s32[8]{0:T(128)} %compare_select_fusion.where, f32[16,784,128]{2,1,0:T(8,128)} %bitcast.12, f32[512,256]{1,0:T(8,128)} %collective-permute-done.3.left.refs_7_, f32[512,512]{1,0:T(8,128)} %shard_map.74.before), custom_call_target="tpu_custom_call" | custom-call | flops 402653184 | bytes 3145728 | tf_op jit(solution)/shard_map/pallas_call | solution.py:189
  97.3 1.2 all-to-all-done.1.terms1
  98.4 3.7 %all-to-all-start = ((f32[4,128,512]{2,1,0:T(8,128)}), f32[4,128,512]{2,1,0:T(8,128)S(1)}, u32[]{:S(2)}, u32[]{:S(2)}) async-start(f32[4,128,512]{2,1,0:T(8,128)} %bitcast.13), calls=%async_computation | async-start | bytes 2097152 | tf_op jit(solution)/shard_map/all_to_all | solution.py:255
  102.1 11.4 %all-to-all-done.terms0 = f32[4,128,512]{2,1,0:T(8,128)S(1)} async-done(((f32[4,128,512]{2,1,0:T(8,128)}), f32[4,128,512]{2,1,0:T(8,128)S(1)}, u32[]{:S(2)}, u32[]{:S(2)}) %all-to-all-start) | async-done | bytes 1048608 | tf_op jit(solution)/shard_map/all_to_all | solution.py:255
  113.5 1.0 copy-done.1
  114.5 2.6 %shard_map.77 = f32[128,1024]{1,0:T(8,128)} custom-call(s32[1]{0:T(128)} %bitcast.layer, s32[8,16]{1,0:T(8,128)} %flags.1, f32[4,128,512]{2,1,0:T(8,128)} %copy-done.1, f32[4,128,512]{2,1,0:T(8,128)} %copy-done, f32[128,1024]{1,0:T(8,128)} %square.1), custom_call_target="tpu_custom_call" | custom-call | flops 1048576 | bytes 3145728 | tf_op jit(solution)/shard_map/pallas_call | solution.py:223
  (11 shorter events, 0.0 us)
Async XLA Ops:
  6.5 66.7 %all-gather.3.cloned.1.call-start = ((), (), s32[]{:S(2)}) async-start(), calls=%async_computation.2 | async-start | bytes 6823936 | tf_op jit(solution)/shard_map/all_gather | solution.py:248
  9.2 17.6 %collective-permute-start = (f32[512,256]{1,0:T(8,128)}, f32[512,256]{1,0:T(8,128)S(1)}, u32[]{:S(2)}, u32[]{:S(2)}) collective-permute-start(f32[512,256]{1,0:T(8,128)} %get-tuple-element.8.refs_0_), channel_id=1, source_target_pairs={{0,4},{4,8},{8,12},{12,16},{16,20},{20,24},{24,28},{28,0},{1,5},{5... | collective-permute-start | bytes 1572872 | tf_op jit(solution)/shard_map/ppermute | solution.py:238
  12.8 15.9 %collective-permute-start.4 = (f32[512,256]{1,0:T(8,128)}, f32[512,256]{1,0:T(8,128)S(1)}, u32[]{:S(2)}, u32[]{:S(2)}) collective-permute-start(f32[512,256]{1,0:T(8,128)} %get-tuple-element.8.refs_0_), channel_id=1, source_target_pairs={{0,28},{4,0},{8,4},{12,8},{16,12},{20,16},{24,20},{28,24},{1,29},{... | collective-permute-start | bytes 1572872 | tf_op jit(solution)/shard_map/ppermute | solution.py:238
  26.8 46.5 %copy-start.2 = (f32[512,256]{1,0:T(8,128)}, f32[512,256]{1,0:T(8,128)S(1)}, u32[]{:S(2)}) copy-start(f32[512,256]{1,0:T(8,128)S(1)} %collective-permute-done.refs_1_) | copy-start | bytes 1572868
  26.8 16.3 %collective-permute-start.1 = (f32[512,256]{1,0:T(8,128)S(1)}, f32[512,256]{1,0:T(8,128)S(1)}, u32[]{:S(2)}, u32[]{:S(2)}) collective-permute-start(f32[512,256]{1,0:T(8,128)S(1)} %collective-permute-done.refs_1_), channel_id=1, source_target_pairs={{0,4},{4,8},{8,12},{12,16},{16,20},{20,24},{24,28},{28,0},{1,5},{5... | collective-permute-start | bytes 1572872 | tf_op jit(solution)/shard_map/ppermute | solution.py:238
  28.7 44.5 %copy-start.3 = (f32[512,256]{1,0:T(8,128)}, f32[512,256]{1,0:T(8,128)S(1)}, u32[]{:S(2)}) copy-start(f32[512,256]{1,0:T(8,128)S(1)} %collective-permute-done.4.refs_2_) | copy-start | bytes 1572868
  28.7 16.3 %collective-permute-start.5 = (f32[512,256]{1,0:T(8,128)S(1)}, f32[512,256]{1,0:T(8,128)S(1)}, u32[]{:S(2)}, u32[]{:S(2)}) collective-permute-start(f32[512,256]{1,0:T(8,128)S(1)} %collective-permute-done.4.refs_2_), channel_id=1, source_target_pairs={{0,28},{4,0},{8,4},{12,8},{16,12},{20,16},{24,20},{28,24},{1,29},{... | collective-permute-start | bytes 1572872 | tf_op jit(solution)/shard_map/ppermute | solution.py:238
  43.1 30.2 %copy-start.4 = (f32[512,256]{1,0:T(8,128)}, f32[512,256]{1,0:T(8,128)S(1)}, u32[]{:S(2)}) copy-start(f32[512,256]{1,0:T(8,128)S(1)} %collective-permute-done.1.refs_3_) | copy-start | bytes 1572868
  43.1 15.5 %collective-permute-start.2 = (f32[512,256]{1,0:T(8,128)S(1)}, f32[512,256]{1,0:T(8,128)S(1)}, u32[]{:S(2)}, u32[]{:S(2)}) collective-permute-start(f32[512,256]{1,0:T(8,128)S(1)} %collective-permute-done.1.refs_3_), channel_id=1, source_target_pairs={{0,4},{4,8},{8,12},{12,16},{16,20},{20,24},{24,28},{28,0},{1,5},{5... | collective-permute-start | bytes 1572872 | tf_op jit(solution)/shard_map/ppermute | solution.py:238
  45.0 28.2 %copy-start.5 = (f32[512,256]{1,0:T(8,128)}, f32[512,256]{1,0:T(8,128)S(1)}, u32[]{:S(2)}) copy-start(f32[512,256]{1,0:T(8,128)S(1)} %collective-permute-done.5.refs_4_) | copy-start | bytes 1572868
  45.0 16.7 %collective-permute-start.6 = (f32[512,256]{1,0:T(8,128)S(1)}, f32[512,256]{1,0:T(8,128)S(1)}, u32[]{:S(2)}, u32[]{:S(2)}) collective-permute-start(f32[512,256]{1,0:T(8,128)S(1)} %collective-permute-done.5.refs_4_), channel_id=1, source_target_pairs={{0,28},{4,0},{8,4},{12,8},{16,12},{20,16},{24,20},{28,24},{1,29},{... | collective-permute-start | bytes 1572872 | tf_op jit(solution)/shard_map/ppermute | solution.py:238
  58.5 14.7 %copy-start.6 = (f32[512,256]{1,0:T(8,128)}, f32[512,256]{1,0:T(8,128)S(1)}, u32[]{:S(2)}) copy-start(f32[512,256]{1,0:T(8,128)S(1)} %collective-permute-done.2.refs_5_) | copy-start | bytes 1572868
  58.5 14.7 %collective-permute-start.3 = (f32[512,256]{1,0:T(8,128)S(1)}, f32[512,256]{1,0:T(8,128)}, u32[]{:S(2)}, u32[]{:S(2)}) collective-permute-start(f32[512,256]{1,0:T(8,128)S(1)} %collective-permute-done.2.refs_5_), channel_id=1, source_target_pairs={{0,4},{4,8},{8,12},{12,16},{16,20},{20,24},{24,28},{28,0},{1,5},{5... | collective-permute-start | bytes 1572872 | tf_op jit(solution)/shard_map/ppermute | solution.py:238
  61.7 11.5 %copy-start.7 = (f32[512,256]{1,0:T(8,128)}, f32[512,256]{1,0:T(8,128)S(1)}, u32[]{:S(2)}) copy-start(f32[512,256]{1,0:T(8,128)S(1)} %collective-permute-done.6.refs_6_) | copy-start | bytes 1572868
  82.1 16.3 %all-to-all-start.1 = ((f32[4,128,512]{2,1,0:T(8,128)}), f32[4,128,512]{2,1,0:T(8,128)S(1)}, u32[]{:S(2)}, u32[]{:S(2)}) async-start(f32[4,128,512]{2,1,0:T(8,128)} %bitcast.14), calls=%async_computation.1 | async-start | bytes 2097152 | tf_op jit(solution)/shard_map/all_to_all | solution.py:257
  98.4 15.1 %copy-start = (f32[4,128,512]{2,1,0:T(8,128)}, f32[4,128,512]{2,1,0:T(8,128)S(1)}, u32[]{:S(2)}) copy-start(f32[4,128,512]{2,1,0:T(8,128)S(1)} %all-to-all-done.1.terms1) | copy-start | bytes 3145732
  98.4 15.1 %all-to-all-start = ((f32[4,128,512]{2,1,0:T(8,128)}), f32[4,128,512]{2,1,0:T(8,128)S(1)}, u32[]{:S(2)}, u32[]{:S(2)}) async-start(f32[4,128,512]{2,1,0:T(8,128)} %bitcast.13), calls=%async_computation | async-start | bytes 2097152 | tf_op jit(solution)/shard_map/all_to_all | solution.py:255
  113.5 1.0 copy-start.1
Sparse Core Ops, SparseCore 0:
  9.5 47.2 all-gather.2

commit v11 on v10

--- a/solution.py
+++ b/solution.py
@@ -13,6 +13,7 @@
 EXTRA = 8
 META = 16
 PACKED = META + 6 * LANES
+ARRIVALS = (0, 7, 1, 6, 2, 5, 3, 4)
 BF = jnp.bfloat16
 F32 = jnp.float32
 
@@ -80,8 +81,9 @@
     return high, (x - high.astype(F32)).astype(BF)
 
 
-def product_kernel(side, first, last, where, packed, *refs):
+def product_kernel(side, first, last, me, packed, *refs):
     steps = range(first, last)
+    where = [(me[0] + by) & 7 for by in ARRIVALS]
     parts, refs = refs[: last - first], refs[last - first :]
     out, tiles, lefts, high0, high1, low0, low1, homes, tile_sems, left_sems, home_sem = refs
     need = tiles.shape[2]
@@ -137,7 +139,7 @@
         out[...] = total
 
 
-def product(side, first, last, parts, where, packed):
+def product(side, first, last, parts, me, packed):
     smem = pl.BlockSpec(memory_space=pltpu.SMEM)
     hbm = pl.BlockSpec(memory_space=pltpu.HBM)
     vmem = pl.BlockSpec(memory_space=pltpu.VMEM)
@@ -163,10 +165,10 @@
         ],
         cost_estimate=pl.CostEstimate(flops=6 * 512 * 512 * 256 * steps, bytes_accessed=steps << 20, transcendentals=0),
         compiler_params=pltpu.CompilerParams(vmem_limit_bytes=56 << 20),
-    )(where, packed, *parts)
-
-
-def last_kernel(where, tiles, left, before, out, rights_high, rights_low):
+    )(me, packed, *parts)
+
+
+def last_kernel(me, tiles, left, before, out, rights_high, rights_low):
     @pl.when(pl.program_id(0) == 0)
     def _():
         for z in range(2):
@@ -184,8 +186,8 @@
     out[...] = before[...] + total
 
 
-def add_last(part, where, packed, before):
-    rows = pl.BlockSpec((256, 512), lambda i, where: (i, 0))
+def add_last(part, me, packed, before):
+    rows = pl.BlockSpec((256, 512), lambda i, me: (i, 0))
     return pl.pallas_call(
         last_kernel,
         out_shape=jax.ShapeDtypeStruct((512, 512), F32),
@@ -193,8 +195,8 @@
             num_scalar_prefetch=1,
             grid=(2,),
             in_specs=[
-                pl.BlockSpec((2, META + 4 * LANES, LANES), lambda i, where: (where[7], 0, 0)),
-                pl.BlockSpec((256, 256), lambda i, where: (i, 0)),
+                pl.BlockSpec((2, META + 4 * LANES, LANES), lambda i, me: ((me[0] + ARRIVALS[7]) & 7, 0, 0)),
+                pl.BlockSpec((256, 256), lambda i, me: (i, 0)),
                 rows,
             ],
             out_specs=rows,
@@ -202,31 +204,33 @@
         ),
         cost_estimate=pl.CostEstimate(flops=6 * 512 * 512 * 256, bytes_accessed=3 << 20, transcendentals=0),
         compiler_params=pltpu.CompilerParams(vmem_limit_bytes=56 << 20),
-    )(where, packed, part, before)
-
-
-def finish_kernel(layer, flags, terms0, terms1, square, out):
+    )(me, packed, part, before)
+
+
+def finish_kernel(side, where, flags, terms, square, *refs):
+    out = refs[-1]
     for b in range(2):
-        for c in range(8):
-            terms = terms1 if c >= 4 else terms0
+        for c in range(4):
             at = (pl.ds(b * BS, BS), pl.ds(c * LANES, LANES))
-            near = (pl.ds(b * BS, BS), pl.ds(c % 4 * LANES, LANES))
-            total = (terms[(0,) + near] + terms[(1,) + near]) + (terms[(2,) + near] + terms[(3,) + near])
-            line = layer[0] * 2 + b
-            mask = pair_mask(flags[line, 2 * c], flags[line, 2 * c + 1])
+            total = (terms[(0,) + at] + terms[(1,) + at]) + (terms[(2,) + at] + terms[(3,) + at])
+            line, column = where[0] * 2 + b, 8 * side + 2 * c
+            mask = pair_mask(flags[line, column], flags[line, column + 1])
             out[at] = mask * (3.0 * square[at] - 2.0 * total)
 
 
-def finish(terms, square, flags, layer):
+def finish(side, terms, square, flags, where, *before):
     smem = pl.BlockSpec(memory_space=pltpu.SMEM)
-    vmem = pl.BlockSpec(memory_space=pltpu.VMEM)
-    return pl.pallas_call(
-        finish_kernel,
+    half = pl.BlockSpec((128, 512), lambda i: (0, side))
+    return pl.pallas_call(
+        functools.partial(finish_kernel, side),
         out_shape=jax.ShapeDtypeStruct(square.shape, F32),
-        in_specs=[smem, smem, vmem, vmem, vmem],
-        out_specs=vmem,
-        cost_estimate=pl.CostEstimate(flops=1 << 20, bytes_accessed=3 << 20, transcendentals=0),
-    )(layer, flags, *terms, square)
+        grid=(1,),
+        in_specs=[smem, smem, pl.BlockSpec((4, 128, 512), lambda i: (0, 0, 0)), half]
+        + [pl.BlockSpec(memory_space=pltpu.HBM)] * len(before),
+        out_specs=half,
+        input_output_aliases={4: 0} if before else {},
+        cost_estimate=pl.CostEstimate(flops=1 << 20, bytes_accessed=2 << 20, transcendentals=0),
+    )(where, flags, terms, square, *before)
 
 
 def shift(n, by):
@@ -247,15 +251,16 @@
     left, packed = prepare(left_slab[0], left_pattern[0].T, right_window[0], right_pattern[0])
     packed = lax.all_gather(packed, "row", axis=0, tiled=False)
     parts = gather_left(left)
-    me = lax.axis_index("col")
-    where = lax.rem(me + jnp.array([8, 7, 9, 6, 10, 5, 11, 12], jnp.int32), 8)
+    me = lax.axis_index("col").reshape((1,))
     layer = lax.axis_index("layer").reshape((1,))
-    cube = product(0, 0, 7, parts[:7], where, packed)
-    cube = add_last(parts[7], where, packed, cube)
-    terms = [lax.all_to_all(cube.reshape(4, 128, 512), "layer", 0, 0)]
-    cube = product(1, 0, 8, parts, where, packed)
-    terms.append(lax.all_to_all(cube.reshape(4, 128, 512), "layer", 0, 0))
-    return finish(terms, square_blocks, result_pattern, layer)
+    cube = product(0, 0, 7, parts[:7], me, packed)
+    cube = add_last(parts[7], me, packed, cube)
+    me, cube = lax.optimization_barrier((me, cube))
+    terms = lax.all_to_all(cube.reshape(4, 128, 512), "layer", 0, 0)
+    out = finish(0, terms, square_blocks, result_pattern, layer)
+    cube = product(1, 0, 8, parts, me, packed)
+    terms = lax.all_to_all(cube.reshape(4, 128, 512), "layer", 0, 0)
+    return finish(1, terms, square_blocks, result_pattern, layer, out)
 
 
 def solution(mesh):

time: 125 us -> 122 us (0.976)
  the two profiles are of different devices: /device:TPU:448 before, /device:TPU:8 now
where the time goes in v11:
time: 122 us; the launch traced here: 121 us
  waiting for transfers between devices  47.5 us (39%)
  starting transfers between devices  35 us (29%)
  Pallas kernels  24.4 us (20%)
  between operations  13.5 us (11%)
    ppermute x7, starting transfers between devices, send(): return lax.ppermute(x, 'col', shift(8, by))  27.2 us
    ppermute x7, waiting for transfers between devices, send(): return lax.ppermute(x, 'col', shift(8, by))  22.3 us
    all_to_all x2, waiting for transfers between devices, local(): terms = lax.all_to_all(cube.reshape(4, 128, 512), 'layer', 0, 0)  20 us
    pallas_call x2, Pallas kernels, product(): pl.pallas_call(functools.partial(product_kernel, side, first, last), out_...  14.4 us
    all_to_all x2, starting transfers between devices, local(): terms = lax.all_to_all(cube.reshape(4, 128, 512), 'layer', 0, 0)  7.78 us
    all_gather x1, waiting for transfers between devices, local(): packed = lax.all_gather(packed, 'row', axis=0, tiled=False)  5.21 us
    pallas_call x2, Pallas kernels, finish(): pl.pallas_call(functools.partial(finish_kernel, side), out_shape=jax.Shap...  4.14 us
    pallas_call x1, Pallas kernels, add_last(): pl.pallas_call(last_kernel, out_shape=jax.ShapeDtypeStruct((512, 512), F3...  3.06 us
  transfers between devices with their start and end apart: 10, of which 8 were waited for; matrix products, arithmetic and copies ran while one was open for 0% of the time, Pallas kernels for 14%

profile of v11, /device:TPU:8, one launch (start us, length us, event | category | flops | bytes accessed | tf_op | source)
XLA Modules:
  0.0 121.4 jit_solution(14229078049147468981)
XLA Ops:
  6.5 0.0 all-gather.3.cloned.1.call-start
  6.5 2.8 %shard_map.64 = (f32[512,256]{1,0:T(8,128)}, f32[784,128]{1,0:T(8,128)}) custom-call(s32[4,8]{1,0:T(4,128)} %bitcast.18, f32[512,256]{1,0:T(8,128)} %bitcast.16, s32[2,16]{1,0:T(2,128)} %bitcast.19, f32[128,1024]{1,0:T(8,128)} %bitcast.17), custom_call_target="tpu_custom_call" | custom-call | tf_op jit(solution)/shard_map/pallas_call | solution.py:70
  9.3 0.0 all-gather.3.cloned.1.call-update
  9.3 3.5 %collective-permute-start = (f32[512,256]{1,0:T(8,128)}, f32[512,256]{1,0:T(8,128)S(1)}, u32[]{:S(2)}, u32[]{:S(2)}) collective-permute-start(f32[512,256]{1,0:T(8,128)} %get-tuple-element.10.refs_0_), channel_id=1, source_target_pairs={{0,4},{4,8},{8,12},{12,16},{16,20},{20,24},{24,28},{28,0},{1,5},{5... | collective-permute-start | bytes 1572872 | tf_op jit(solution)/shard_map/ppermute | solution.py:242
  12.8 6.1 %collective-permute-start.4 = (f32[512,256]{1,0:T(8,128)}, f32[512,256]{1,0:T(8,128)S(1)}, u32[]{:S(2)}, u32[]{:S(2)}) collective-permute-start(f32[512,256]{1,0:T(8,128)} %get-tuple-element.10.refs_0_), channel_id=1, source_target_pairs={{0,28},{4,0},{8,4},{12,8},{16,12},{20,16},{24,20},{28,24},{1,29},{... | collective-permute-start | bytes 1572872 | tf_op jit(solution)/shard_map/ppermute | solution.py:242
  18.9 6.1 %collective-permute-done.refs_1_ = f32[512,256]{1,0:T(8,128)S(1)} collective-permute-done((f32[512,256]{1,0:T(8,128)}, f32[512,256]{1,0:T(8,128)S(1)}, u32[]{:S(2)}, u32[]{:S(2)}) %collective-permute-start) | collective-permute-done | bytes 524320 | tf_op jit(solution)/shard_map/ppermute | solution.py:242
  25.0 3.5 %collective-permute-start.1 = (f32[512,256]{1,0:T(8,128)S(1)}, f32[512,256]{1,0:T(8,128)S(1)}, u32[]{:S(2)}, u32[]{:S(2)}) collective-permute-start(f32[512,256]{1,0:T(8,128)S(1)} %collective-permute-done.refs_1_), channel_id=1, source_target_pairs={{0,4},{4,8},{8,12},{12,16},{16,20},{20,24},{24,28},{28,0},{1,5},{5... | collective-permute-start | bytes 1572872 | tf_op jit(solution)/shard_map/ppermute | solution.py:242
  28.5 0.0 collective-permute-done.4.refs_2_
  28.5 0.0 copy-start.3
  28.5 2.9 %collective-permute-start.5 = (f32[512,256]{1,0:T(8,128)S(1)}, f32[512,256]{1,0:T(8,128)S(1)}, u32[]{:S(2)}, u32[]{:S(2)}) collective-permute-start(f32[512,256]{1,0:T(8,128)S(1)} %collective-permute-done.4.refs_2_), channel_id=1, source_target_pairs={{0,28},{4,0},{8,4},{12,8},{16,12},{20,16},{24,20},{28,24},{1,29},{... | collective-permute-start | bytes 1572872 | tf_op jit(solution)/shard_map/ppermute | solution.py:242
  31.4 7.4 %collective-permute-done.1.refs_3_ = f32[512,256]{1,0:T(8,128)S(1)} collective-permute-done((f32[512,256]{1,0:T(8,128)S(1)}, f32[512,256]{1,0:T(8,128)S(1)}, u32[]{:S(2)}, u32[]{:S(2)}) %collective-permute-start.1) | collective-permute-done | bytes 524320 | tf_op jit(solution)/shard_map/ppermute | solution.py:242
  38.8 4.3 %collective-permute-start.2 = (f32[512,256]{1,0:T(8,128)S(1)}, f32[512,256]{1,0:T(8,128)S(1)}, u32[]{:S(2)}, u32[]{:S(2)}) collective-permute-start(f32[512,256]{1,0:T(8,128)S(1)} %collective-permute-done.1.refs_3_), channel_id=1, source_target_pairs={{0,4},{4,8},{8,12},{12,16},{16,20},{20,24},{24,28},{28,0},{1,5},{5... | collective-permute-start | bytes 1572872 | tf_op jit(solution)/shard_map/ppermute | solution.py:242
  43.1 0.8 collective-permute-done.5.refs_4_
  43.9 1.9 %collective-permute-start.6 = (f32[512,256]{1,0:T(8,128)S(1)}, f32[512,256]{1,0:T(8,128)S(1)}, u32[]{:S(2)}, u32[]{:S(2)}) collective-permute-start(f32[512,256]{1,0:T(8,128)S(1)} %collective-permute-done.5.refs_4_), channel_id=1, source_target_pairs={{0,28},{4,0},{8,4},{12,8},{16,12},{20,16},{24,20},{28,24},{1,29},{... | collective-permute-start | bytes 1572872 | tf_op jit(solution)/shard_map/ppermute | solution.py:242
  45.8 6.7 %collective-permute-done.2.refs_5_ = f32[512,256]{1,0:T(8,128)S(1)} collective-permute-done((f32[512,256]{1,0:T(8,128)S(1)}, f32[512,256]{1,0:T(8,128)S(1)}, u32[]{:S(2)}, u32[]{:S(2)}) %collective-permute-start.2) | collective-permute-done | bytes 524320 | tf_op jit(solution)/shard_map/ppermute | solution.py:242
  52.5 5.1 %collective-permute-start.3 = (f32[512,256]{1,0:T(8,128)S(1)}, f32[512,256]{1,0:T(8,128)}, u32[]{:S(2)}, u32[]{:S(2)}) collective-permute-start(f32[512,256]{1,0:T(8,128)S(1)} %collective-permute-done.2.refs_5_), channel_id=1, source_target_pairs={{0,4},{4,8},{8,12},{12,16},{16,20},{20,24},{24,28},{28,0},{1,5},{5... | collective-permute-start | bytes 1572872 | tf_op jit(solution)/shard_map/ppermute | solution.py:242
  57.6 1.3 %collective-permute-done.6.refs_6_ = f32[512,256]{1,0:T(8,128)S(1)} collective-permute-done((f32[512,256]{1,0:T(8,128)S(1)}, f32[512,256]{1,0:T(8,128)S(1)}, u32[]{:S(2)}, u32[]{:S(2)}) %collective-permute-start.6) | collective-permute-done | bytes 524320 | tf_op jit(solution)/shard_map/ppermute | solution.py:242
  59.0 5.2 %all-gather.3.cloned.1.call-done = f32[12544,128]{1,0:T(8,128)} async-done(((f32[784,128]{1,0:T(8,128)}), f32[12544,128]{1,0:T(8,128)}) %all-gather.3.cloned.1.call-update) | async-done | bytes 6422544 | tf_op jit(solution)/shard_map/all_gather | solution.py:252
  64.2 0.0 copy-done.2
  64.2 0.0 copy-done.3
  64.2 0.0 copy-done.5
  64.2 6.4 %shard_map.65.before = f32[512,512]{1,0:T(8,128)} custom-call(s32[1]{0:T(128)} %bitcast.1.me, f32[16,784,128]{2,1,0:T(8,128)} %bitcast.11, f32[512,256]{1,0:T(8,128)} %get-tuple-element.10.refs_0_, f32[512,256]{1,0:T(8,128)} %copy-done.2, f32[512,256]{1,0:T(8,128)} %copy-done.3, f32[512,256]{1,0:T(8,128)} %copy-done.4, f32[512,256]{1,0:T(8,128)} %copy-done.5, ...), custom_call_target="tpu_custom_call" | custom-call | flops 2818572288 | bytes 7340032 | tf_op jit(solution)/shard_map/pallas_call | solution.py:149
  70.6 0.0 collective-permute-done.3.left.refs_7_
  70.6 3.1 %shard_map.66 = f32[512,512]{1,0:T(8,128)} custom-call(s32[1]{0:T(128)} %bitcast.1.me, f32[16,784,128]{2,1,0:T(8,128)} %bitcast.12, f32[512,256]{1,0:T(8,128)} %collective-permute-done.3.left.refs_7_, f32[512,512]{1,0:T(8,128)} %shard_map.65.before), custom_call_target="tpu_custom_call" | custom-call | flops 402653184 | bytes 3145728 | tf_op jit(solution)/shard_map/pallas_call | solution.py:191
  73.7 4.3 %all-to-all-start.1 = ((f32[4,128,512]{2,1,0:T(8,128)}), f32[4,128,512]{2,1,0:T(8,128)S(1)}, u32[]{:S(2)}, u32[]{:S(2)}) async-start(f32[4,128,512]{2,1,0:T(8,128)} %bitcast.14), calls=%async_computation.1 | async-start | bytes 2097152 | tf_op jit(solution)/shard_map/all_to_all | solution.py:259
  77.9 8.0 %shard_map.67 = f32[512,512]{1,0:T(8,128)} custom-call(s32[1]{0:T(128)} %bitcast.1.me, f32[16,784,128]{2,1,0:T(8,128)} %bitcast.13, f32[512,256]{1,0:T(8,128)} %get-tuple-element.10.refs_0_, f32[512,256]{1,0:T(8,128)} %copy-done.2, f32[512,256]{1,0:T(8,128)} %copy-done.3, f32[512,256]{1,0:T(8,128)} %copy-done.4, f32[512,256]{1,0:T(8,128)} %copy-done.5, ...), custom_call_target="tpu_custom_call" | custom-call | flops 3221225472 | bytes 8388608 | tf_op jit(solution)/shard_map/pallas_call | solution.py:149
  86.0 7.5 %all-to-all-done.1.terms = f32[4,128,512]{2,1,0:T(8,128)S(1)} async-done(((f32[4,128,512]{2,1,0:T(8,128)}), f32[4,128,512]{2,1,0:T(8,128)S(1)}, u32[]{:S(2)}, u32[]{:S(2)}) %all-to-all-start.1) | async-done | bytes 1048608 | tf_op jit(solution)/shard_map/all_to_all | solution.py:259
  93.4 3.5 %all-to-all-start = ((f32[4,128,512]{2,1,0:T(8,128)}), f32[4,128,512]{2,1,0:T(8,128)S(1)}, u32[]{:S(2)}, u32[]{:S(2)}) async-start(f32[4,128,512]{2,1,0:T(8,128)} %bitcast.15), calls=%async_computation | async-start | bytes 2097152 | tf_op jit(solution)/shard_map/all_to_all | solution.py:262
  97.0 2.1 %shard_map.68.refs_0_ = f32[128,1024]{1,0:T(8,128)} custom-call(s32[1]{0:T(128)} %bitcast.where, s32[8,16]{1,0:T(8,128)} %flags.3, f32[4,128,512]{2,1,0:T(8,128)} %copy-done, f32[128,1024]{1,0:T(8,128)} %square.3), custom_call_target="tpu_custom_call" | custom-call | flops 1048576 | bytes 2097152 | tf_op jit(solution)/shard_map/pallas_call | solution.py:224
  99.0 12.5 %all-to-all-done.terms = f32[4,128,512]{2,1,0:T(8,128)S(1)} async-done(((f32[4,128,512]{2,1,0:T(8,128)}), f32[4,128,512]{2,1,0:T(8,128)S(1)}, u32[]{:S(2)}, u32[]{:S(2)}) %all-to-all-start) | async-done | bytes 1048608 | tf_op jit(solution)/shard_map/all_to_all | solution.py:262
  111.5 1.0 copy-done.1
  112.5 2.1 %shard_map.69 = f32[128,1024]{1,0:T(8,128)} custom-call(s32[1]{0:T(128)} %bitcast.where, s32[8,16]{1,0:T(8,128)} %flags.3, f32[4,128,512]{2,1,0:T(8,128)} %copy-done.1, f32[128,1024]{1,0:T(8,128)} %square.3, f32[128,1024]{1,0:T(8,128)} %shard_map.68.refs_0_), custom_call_target="tpu_custom_call", output_to_operand_aliasing={{}: (4, {})} | custom-call | flops 1048576 | bytes 2097152 | tf_op jit(solution)/shard_map/pallas_call | solution.py:224
  (11 shorter events, 0.0 us)
Async XLA Ops:
  6.5 57.6 %all-gather.3.cloned.1.call-start = ((), (), s32[]{:S(2)}) async-start(), calls=%async_computation.2 | async-start | bytes 6823936 | tf_op jit(solution)/shard_map/all_gather | solution.py:252
  9.3 15.7 %collective-permute-start = (f32[512,256]{1,0:T(8,128)}, f32[512,256]{1,0:T(8,128)S(1)}, u32[]{:S(2)}, u32[]{:S(2)}) collective-permute-start(f32[512,256]{1,0:T(8,128)} %get-tuple-element.10.refs_0_), channel_id=1, source_target_pairs={{0,4},{4,8},{8,12},{12,16},{16,20},{20,24},{24,28},{28,0},{1,5},{5... | collective-permute-start | bytes 1572872 | tf_op jit(solution)/shard_map/ppermute | solution.py:242
  12.8 15.7 %collective-permute-start.4 = (f32[512,256]{1,0:T(8,128)}, f32[512,256]{1,0:T(8,128)S(1)}, u32[]{:S(2)}, u32[]{:S(2)}) collective-permute-start(f32[512,256]{1,0:T(8,128)} %get-tuple-element.10.refs_0_), channel_id=1, source_target_pairs={{0,28},{4,0},{8,4},{12,8},{16,12},{20,16},{24,20},{28,24},{1,29},{... | collective-permute-start | bytes 1572872 | tf_op jit(solution)/shard_map/ppermute | solution.py:242
  25.0 39.1 %copy-start.2 = (f32[512,256]{1,0:T(8,128)}, f32[512,256]{1,0:T(8,128)S(1)}, u32[]{:S(2)}) copy-start(f32[512,256]{1,0:T(8,128)S(1)} %collective-permute-done.refs_1_) | copy-start | bytes 1572868
  25.0 13.8 %collective-permute-start.1 = (f32[512,256]{1,0:T(8,128)S(1)}, f32[512,256]{1,0:T(8,128)S(1)}, u32[]{:S(2)}, u32[]{:S(2)}) collective-permute-start(f32[512,256]{1,0:T(8,128)S(1)} %collective-permute-done.refs_1_), channel_id=1, source_target_pairs={{0,4},{4,8},{8,12},{12,16},{16,20},{20,24},{24,28},{28,0},{1,5},{5... | collective-permute-start | bytes 1572872 | tf_op jit(solution)/shard_map/ppermute | solution.py:242
  28.5 35.6 %copy-start.3 = (f32[512,256]{1,0:T(8,128)}, f32[512,256]{1,0:T(8,128)S(1)}, u32[]{:S(2)}) copy-start(f32[512,256]{1,0:T(8,128)S(1)} %collective-permute-done.4.refs_2_) | copy-start | bytes 1572868
  28.5 15.3 %collective-permute-start.5 = (f32[512,256]{1,0:T(8,128)S(1)}, f32[512,256]{1,0:T(8,128)S(1)}, u32[]{:S(2)}, u32[]{:S(2)}) collective-permute-start(f32[512,256]{1,0:T(8,128)S(1)} %collective-permute-done.4.refs_2_), channel_id=1, source_target_pairs={{0,28},{4,0},{8,4},{12,8},{16,12},{20,16},{24,20},{28,24},{1,29},{... | collective-permute-start | bytes 1572872 | tf_op jit(solution)/shard_map/ppermute | solution.py:242
  38.8 25.3 %copy-start.4 = (f32[512,256]{1,0:T(8,128)}, f32[512,256]{1,0:T(8,128)S(1)}, u32[]{:S(2)}) copy-start(f32[512,256]{1,0:T(8,128)S(1)} %collective-permute-done.1.refs_3_) | copy-start | bytes 1572868
  38.8 13.7 %collective-permute-start.2 = (f32[512,256]{1,0:T(8,128)S(1)}, f32[512,256]{1,0:T(8,128)S(1)}, u32[]{:S(2)}, u32[]{:S(2)}) collective-permute-start(f32[512,256]{1,0:T(8,128)S(1)} %collective-permute-done.1.refs_3_), channel_id=1, source_target_pairs={{0,4},{4,8},{8,12},{12,16},{16,20},{20,24},{24,28},{28,0},{1,5},{5... | collective-permute-start | bytes 1572872 | tf_op jit(solution)/shard_map/ppermute | solution.py:242
  43.9 20.3 %copy-start.5 = (f32[512,256]{1,0:T(8,128)}, f32[512,256]{1,0:T(8,128)S(1)}, u32[]{:S(2)}) copy-start(f32[512,256]{1,0:T(8,128)S(1)} %collective-permute-done.5.refs_4_) | copy-start | bytes 1572868
  43.9 15.1 %collective-permute-start.6 = (f32[512,256]{1,0:T(8,128)S(1)}, f32[512,256]{1,0:T(8,128)S(1)}, u32[]{:S(2)}, u32[]{:S(2)}) collective-permute-start(f32[512,256]{1,0:T(8,128)S(1)} %collective-permute-done.5.refs_4_), channel_id=1, source_target_pairs={{0,28},{4,0},{8,4},{12,8},{16,12},{20,16},{24,20},{28,24},{1,29},{... | collective-permute-start | bytes 1572872 | tf_op jit(solution)/shard_map/ppermute | solution.py:242
  52.5 11.7 %copy-start.6 = (f32[512,256]{1,0:T(8,128)}, f32[512,256]{1,0:T(8,128)S(1)}, u32[]{:S(2)}) copy-start(f32[512,256]{1,0:T(8,128)S(1)} %collective-permute-done.2.refs_5_) | copy-start | bytes 1572868
  52.5 18.1 %collective-permute-start.3 = (f32[512,256]{1,0:T(8,128)S(1)}, f32[512,256]{1,0:T(8,128)}, u32[]{:S(2)}, u32[]{:S(2)}) collective-permute-start(f32[512,256]{1,0:T(8,128)S(1)} %collective-permute-done.2.refs_5_), channel_id=1, source_target_pairs={{0,4},{4,8},{8,12},{12,16},{16,20},{20,24},{24,28},{28,0},{1,5},{5... | collective-permute-start | bytes 1572872 | tf_op jit(solution)/shard_map/ppermute | solution.py:242
  59.0 5.2 %copy-start.7 = (f32[512,256]{1,0:T(8,128)}, f32[512,256]{1,0:T(8,128)S(1)}, u32[]{:S(2)}) copy-start(f32[512,256]{1,0:T(8,128)S(1)} %collective-permute-done.6.refs_6_) | copy-start | bytes 1572868
  73.7 19.8 %all-to-all-start.1 = ((f32[4,128,512]{2,1,0:T(8,128)}), f32[4,128,512]{2,1,0:T(8,128)S(1)}, u32[]{:S(2)}, u32[]{:S(2)}) async-start(f32[4,128,512]{2,1,0:T(8,128)} %bitcast.14), calls=%async_computation.1 | async-start | bytes 2097152 | tf_op jit(solution)/shard_map/all_to_all | solution.py:259
  93.4 3.5 %copy-start = (f32[4,128,512]{2,1,0:T(8,128)}, f32[4,128,512]{2,1,0:T(8,128)S(1)}, u32[]{:S(2)}) copy-start(f32[4,128,512]{2,1,0:T(8,128)S(1)} %all-to-all-done.1.terms) | copy-start | bytes 3145732
  93.4 18.1 %all-to-all-start = ((f32[4,128,512]{2,1,0:T(8,128)}), f32[4,128,512]{2,1,0:T(8,128)S(1)}, u32[]{:S(2)}, u32[]{:S(2)}) async-start(f32[4,128,512]{2,1,0:T(8,128)} %bitcast.15), calls=%async_computation | async-start | bytes 2097152 | tf_op jit(solution)/shard_map/all_to_all | solution.py:262
  111.5 1.0 copy-start.1
Sparse Core Ops, SparseCore 0:
  9.5 54.6 all-gather.2

commit v12 on v11

--- a/solution.py
+++ b/solution.py
@@ -225,7 +225,7 @@
         functools.partial(finish_kernel, side),
         out_shape=jax.ShapeDtypeStruct(square.shape, F32),
         grid=(1,),
-        in_specs=[smem, smem, pl.BlockSpec((4, 128, 512), lambda i: (0, 0, 0)), half]
+        in_specs=[smem, smem, pl.BlockSpec(memory_space=pltpu.VMEM), half]
         + [pl.BlockSpec(memory_space=pltpu.HBM)] * len(before),
         out_specs=half,
         input_output_aliases={4: 0} if before else {},

time: 122 us -> 122 us (level)
  no operation moved by 1% of the time
where the time goes in v12:
time: 122 us; the launch traced here: 121 us
  waiting for transfers between devices  47.6 us (39%)
  starting transfers between devices  35.1 us (29%)
  Pallas kernels  24.2 us (20%)
  between operations  13.5 us (11%)
    ppermute x7, starting transfers between devices, send(): return lax.ppermute(x, 'col', shift(8, by))  27.4 us
    ppermute x7, waiting for transfers between devices, send(): return lax.ppermute(x, 'col', shift(8, by))  22.2 us
    all_to_all x2, waiting for transfers between devices, local(): terms = lax.all_to_all(cube.reshape(4, 128, 512), 'layer', 0, 0)  20 us
    pallas_call x2, Pallas kernels, product(): pl.pallas_call(functools.partial(product_kernel, side, first, last), out_...  14.4 us
    all_to_all x2, starting transfers between devices, local(): terms = lax.all_to_all(cube.reshape(4, 128, 512), 'layer', 0, 0)  7.76 us
    all_gather x1, waiting for transfers between devices, local(): packed = lax.all_gather(packed, 'row', axis=0, tiled=False)  5.33 us
    pallas_call x2, Pallas kernels, finish(): pl.pallas_call(functools.partial(finish_kernel, side), out_shape=jax.Shap...  4.14 us
    pallas_call x1, Pallas kernels, add_last(): pl.pallas_call(last_kernel, out_shape=jax.ShapeDtypeStruct((512, 512), F3...  3.06 us
  transfers between devices with their start and end apart: 10, of which 8 were waited for; matrix products, arithmetic and copies ran while one was open for 0% of the time, Pallas kernels for 14%

profile of v12, /device:TPU:8, one launch (start us, length us, event | category | flops | bytes accessed | tf_op | source)
XLA Modules:
  0.0 121.5 jit_solution(14229078049147468981)
XLA Ops:
  6.5 0.0 all-gather.3.cloned.1.call-start
  6.5 2.6 %shard_map.64 = (f32[512,256]{1,0:T(8,128)}, f32[784,128]{1,0:T(8,128)}) custom-call(s32[4,8]{1,0:T(4,128)} %bitcast.18, f32[512,256]{1,0:T(8,128)} %bitcast.16, s32[2,16]{1,0:T(2,128)} %bitcast.19, f32[128,1024]{1,0:T(8,128)} %bitcast.17), custom_call_target="tpu_custom_call" | custom-call | tf_op jit(solution)/shard_map/pallas_call | solution.py:70
  9.2 0.0 all-gather.3.cloned.1.call-update
  9.2 3.4 %collective-permute-start = (f32[512,256]{1,0:T(8,128)}, f32[512,256]{1,0:T(8,128)S(1)}, u32[]{:S(2)}, u32[]{:S(2)}) collective-permute-start(f32[512,256]{1,0:T(8,128)} %get-tuple-element.10.refs_0_), channel_id=1, source_target_pairs={{0,4},{4,8},{8,12},{12,16},{16,20},{20,24},{24,28},{28,0},{1,5},{5... | collective-permute-start | bytes 1572872 | tf_op jit(solution)/shard_map/ppermute | solution.py:242
  12.6 6.3 %collective-permute-start.4 = (f32[512,256]{1,0:T(8,128)}, f32[512,256]{1,0:T(8,128)S(1)}, u32[]{:S(2)}, u32[]{:S(2)}) collective-permute-start(f32[512,256]{1,0:T(8,128)} %get-tuple-element.10.refs_0_), channel_id=1, source_target_pairs={{0,28},{4,0},{8,4},{12,8},{16,12},{20,16},{24,20},{28,24},{1,29},{... | collective-permute-start | bytes 1572872 | tf_op jit(solution)/shard_map/ppermute | solution.py:242
  18.9 6.0 %collective-permute-done.refs_1_ = f32[512,256]{1,0:T(8,128)S(1)} collective-permute-done((f32[512,256]{1,0:T(8,128)}, f32[512,256]{1,0:T(8,128)S(1)}, u32[]{:S(2)}, u32[]{:S(2)}) %collective-permute-start) | collective-permute-done | bytes 524320 | tf_op jit(solution)/shard_map/ppermute | solution.py:242
  25.0 3.3 %collective-permute-start.1 = (f32[512,256]{1,0:T(8,128)S(1)}, f32[512,256]{1,0:T(8,128)S(1)}, u32[]{:S(2)}, u32[]{:S(2)}) collective-permute-start(f32[512,256]{1,0:T(8,128)S(1)} %collective-permute-done.refs_1_), channel_id=1, source_target_pairs={{0,4},{4,8},{8,12},{12,16},{16,20},{20,24},{24,28},{28,0},{1,5},{5... | collective-permute-start | bytes 1572872 | tf_op jit(solution)/shard_map/ppermute | solution.py:242
  28.3 0.0 collective-permute-done.4.refs_2_
  28.3 0.0 copy-start.3
  28.3 3.1 %collective-permute-start.5 = (f32[512,256]{1,0:T(8,128)S(1)}, f32[512,256]{1,0:T(8,128)S(1)}, u32[]{:S(2)}, u32[]{:S(2)}) collective-permute-start(f32[512,256]{1,0:T(8,128)S(1)} %collective-permute-done.4.refs_2_), channel_id=1, source_target_pairs={{0,28},{4,0},{8,4},{12,8},{16,12},{20,16},{24,20},{28,24},{1,29},{... | collective-permute-start | bytes 1572872 | tf_op jit(solution)/shard_map/ppermute | solution.py:242
  31.4 7.2 %collective-permute-done.1.refs_3_ = f32[512,256]{1,0:T(8,128)S(1)} collective-permute-done((f32[512,256]{1,0:T(8,128)S(1)}, f32[512,256]{1,0:T(8,128)S(1)}, u32[]{:S(2)}, u32[]{:S(2)}) %collective-permute-start.1) | collective-permute-done | bytes 524320 | tf_op jit(solution)/shard_map/ppermute | solution.py:242
  38.6 4.3 %collective-permute-start.2 = (f32[512,256]{1,0:T(8,128)S(1)}, f32[512,256]{1,0:T(8,128)S(1)}, u32[]{:S(2)}, u32[]{:S(2)}) collective-permute-start(f32[512,256]{1,0:T(8,128)S(1)} %collective-permute-done.1.refs_3_), channel_id=1, source_target_pairs={{0,4},{4,8},{8,12},{12,16},{16,20},{20,24},{24,28},{28,0},{1,5},{5... | collective-permute-start | bytes 1572872 | tf_op jit(solution)/shard_map/ppermute | solution.py:242
  42.9 0.9 collective-permute-done.5.refs_4_
  43.8 2.0 %collective-permute-start.6 = (f32[512,256]{1,0:T(8,128)S(1)}, f32[512,256]{1,0:T(8,128)S(1)}, u32[]{:S(2)}, u32[]{:S(2)}) collective-permute-start(f32[512,256]{1,0:T(8,128)S(1)} %collective-permute-done.5.refs_4_), channel_id=1, source_target_pairs={{0,28},{4,0},{8,4},{12,8},{16,12},{20,16},{24,20},{28,24},{1,29},{... | collective-permute-start | bytes 1572872 | tf_op jit(solution)/shard_map/ppermute | solution.py:242
  45.8 6.8 %collective-permute-done.2.refs_5_ = f32[512,256]{1,0:T(8,128)S(1)} collective-permute-done((f32[512,256]{1,0:T(8,128)S(1)}, f32[512,256]{1,0:T(8,128)S(1)}, u32[]{:S(2)}, u32[]{:S(2)}) %collective-permute-start.2) | collective-permute-done | bytes 524320 | tf_op jit(solution)/shard_map/ppermute | solution.py:242
  52.6 4.9 %collective-permute-start.3 = (f32[512,256]{1,0:T(8,128)S(1)}, f32[512,256]{1,0:T(8,128)}, u32[]{:S(2)}, u32[]{:S(2)}) collective-permute-start(f32[512,256]{1,0:T(8,128)S(1)} %collective-permute-done.2.refs_5_), channel_id=1, source_target_pairs={{0,4},{4,8},{8,12},{12,16},{16,20},{20,24},{24,28},{28,0},{1,5},{5... | collective-permute-start | bytes 1572872 | tf_op jit(solution)/shard_map/ppermute | solution.py:242
  57.5 1.3 %collective-permute-done.6.refs_6_ = f32[512,256]{1,0:T(8,128)S(1)} collective-permute-done((f32[512,256]{1,0:T(8,128)S(1)}, f32[512,256]{1,0:T(8,128)S(1)}, u32[]{:S(2)}, u32[]{:S(2)}) %collective-permute-start.6) | collective-permute-done | bytes 524320 | tf_op jit(solution)/shard_map/ppermute | solution.py:242
  58.9 5.3 %all-gather.3.cloned.1.call-done = f32[12544,128]{1,0:T(8,128)} async-done(((f32[784,128]{1,0:T(8,128)}), f32[12544,128]{1,0:T(8,128)}) %all-gather.3.cloned.1.call-update) | async-done | bytes 6422544 | tf_op jit(solution)/shard_map/all_gather | solution.py:252
  64.2 0.0 copy-done.2
  64.2 0.0 copy-done.4
  64.2 6.4 %shard_map.65.before = f32[512,512]{1,0:T(8,128)} custom-call(s32[1]{0:T(128)} %bitcast.1.me, f32[16,784,128]{2,1,0:T(8,128)} %bitcast.11, f32[512,256]{1,0:T(8,128)} %get-tuple-element.10.refs_0_, f32[512,256]{1,0:T(8,128)} %copy-done.2, f32[512,256]{1,0:T(8,128)} %copy-done.3, f32[512,256]{1,0:T(8,128)} %copy-done.4, f32[512,256]{1,0:T(8,128)} %copy-done.5, ...), custom_call_target="tpu_custom_call" | custom-call | flops 2818572288 | bytes 7340032 | tf_op jit(solution)/shard_map/pallas_call | solution.py:149
  70.6 0.0 collective-permute-done.3.left.refs_7_
  70.6 3.1 %shard_map.66 = f32[512,512]{1,0:T(8,128)} custom-call(s32[1]{0:T(128)} %bitcast.1.me, f32[16,784,128]{2,1,0:T(8,128)} %bitcast.12, f32[512,256]{1,0:T(8,128)} %collective-permute-done.3.left.refs_7_, f32[512,512]{1,0:T(8,128)} %shard_map.65.before), custom_call_target="tpu_custom_call" | custom-call | flops 402653184 | bytes 3145728 | tf_op jit(solution)/shard_map/pallas_call | solution.py:191
  73.7 4.2 %all-to-all-start.1 = ((f32[4,128,512]{2,1,0:T(8,128)}), f32[4,128,512]{2,1,0:T(8,128)S(1)}, u32[]{:S(2)}, u32[]{:S(2)}) async-start(f32[4,128,512]{2,1,0:T(8,128)} %bitcast.14), calls=%async_computation.1 | async-start | bytes 2097152 | tf_op jit(solution)/shard_map/all_to_all | solution.py:259
  77.9 8.0 %shard_map.67 = f32[512,512]{1,0:T(8,128)} custom-call(s32[1]{0:T(128)} %bitcast.1.me, f32[16,784,128]{2,1,0:T(8,128)} %bitcast.13, f32[512,256]{1,0:T(8,128)} %get-tuple-element.10.refs_0_, f32[512,256]{1,0:T(8,128)} %copy-done.2, f32[512,256]{1,0:T(8,128)} %copy-done.3, f32[512,256]{1,0:T(8,128)} %copy-done.4, f32[512,256]{1,0:T(8,128)} %copy-done.5, ...), custom_call_target="tpu_custom_call" | custom-call | flops 3221225472 | bytes 8388608 | tf_op jit(solution)/shard_map/pallas_call | solution.py:149
  86.0 7.5 %all-to-all-done.1.terms = f32[4,128,512]{2,1,0:T(8,128)S(1)} async-done(((f32[4,128,512]{2,1,0:T(8,128)}), f32[4,128,512]{2,1,0:T(8,128)S(1)}, u32[]{:S(2)}, u32[]{:S(2)}) %all-to-all-start.1) | async-done | bytes 1048608 | tf_op jit(solution)/shard_map/all_to_all | solution.py:259
  93.4 3.5 %all-to-all-start = ((f32[4,128,512]{2,1,0:T(8,128)}), f32[4,128,512]{2,1,0:T(8,128)S(1)}, u32[]{:S(2)}, u32[]{:S(2)}) async-start(f32[4,128,512]{2,1,0:T(8,128)} %bitcast.15), calls=%async_computation | async-start | bytes 2097152 | tf_op jit(solution)/shard_map/all_to_all | solution.py:262
  97.0 0.0 copy-done
  97.0 2.1 %shard_map.68.refs_0_ = f32[128,1024]{1,0:T(8,128)} custom-call(s32[1]{0:T(128)} %bitcast.where, s32[8,16]{1,0:T(8,128)} %flags.3, f32[4,128,512]{2,1,0:T(8,128)} %copy-done, f32[128,1024]{1,0:T(8,128)} %square.3), custom_call_target="tpu_custom_call" | custom-call | flops 1048576 | bytes 2097152 | tf_op jit(solution)/shard_map/pallas_call | solution.py:224
  99.0 12.5 %all-to-all-done.terms = f32[4,128,512]{2,1,0:T(8,128)S(1)} async-done(((f32[4,128,512]{2,1,0:T(8,128)}), f32[4,128,512]{2,1,0:T(8,128)S(1)}, u32[]{:S(2)}, u32[]{:S(2)}) %all-to-all-start) | async-done | bytes 1048608 | tf_op jit(solution)/shard_map/all_to_all | solution.py:262
  111.6 1.0 copy-done.1
  112.6 2.1 %shard_map.69 = f32[128,1024]{1,0:T(8,128)} custom-call(s32[1]{0:T(128)} %bitcast.where, s32[8,16]{1,0:T(8,128)} %flags.3, f32[4,128,512]{2,1,0:T(8,128)} %copy-done.1, f32[128,1024]{1,0:T(8,128)} %square.3, f32[128,1024]{1,0:T(8,128)} %shard_map.68.refs_0_), custom_call_target="tpu_custom_call", output_to_operand_aliasing={{}: (4, {})} | custom-call | flops 1048576 | bytes 2097152 | tf_op jit(solution)/shard_map/pallas_call | solution.py:224
  (11 shorter events, 0.0 us)
Async XLA Ops:
  6.5 57.7 %all-gather.3.cloned.1.call-start = ((), (), s32[]{:S(2)}) async-start(), calls=%async_computation.2 | async-start | bytes 6823936 | tf_op jit(solution)/shard_map/all_gather | solution.py:252
  9.2 15.8 %collective-permute-start = (f32[512,256]{1,0:T(8,128)}, f32[512,256]{1,0:T(8,128)S(1)}, u32[]{:S(2)}, u32[]{:S(2)}) collective-permute-start(f32[512,256]{1,0:T(8,128)} %get-tuple-element.10.refs_0_), channel_id=1, source_target_pairs={{0,4},{4,8},{8,12},{12,16},{16,20},{20,24},{24,28},{28,0},{1,5},{5... | collective-permute-start | bytes 1572872 | tf_op jit(solution)/shard_map/ppermute | solution.py:242
  12.6 15.7 %collective-permute-start.4 = (f32[512,256]{1,0:T(8,128)}, f32[512,256]{1,0:T(8,128)S(1)}, u32[]{:S(2)}, u32[]{:S(2)}) collective-permute-start(f32[512,256]{1,0:T(8,128)} %get-tuple-element.10.refs_0_), channel_id=1, source_target_pairs={{0,28},{4,0},{8,4},{12,8},{16,12},{20,16},{24,20},{28,24},{1,29},{... | collective-permute-start | bytes 1572872 | tf_op jit(solution)/shard_map/ppermute | solution.py:242
  25.0 39.2 %copy-start.2 = (f32[512,256]{1,0:T(8,128)}, f32[512,256]{1,0:T(8,128)S(1)}, u32[]{:S(2)}) copy-start(f32[512,256]{1,0:T(8,128)S(1)} %collective-permute-done.refs_1_) | copy-start | bytes 1572868
  25.0 13.6 %collective-permute-start.1 = (f32[512,256]{1,0:T(8,128)S(1)}, f32[512,256]{1,0:T(8,128)S(1)}, u32[]{:S(2)}, u32[]{:S(2)}) collective-permute-start(f32[512,256]{1,0:T(8,128)S(1)} %collective-permute-done.refs_1_), channel_id=1, source_target_pairs={{0,4},{4,8},{8,12},{12,16},{16,20},{20,24},{24,28},{28,0},{1,5},{5... | collective-permute-start | bytes 1572872 | tf_op jit(solution)/shard_map/ppermute | solution.py:242
  28.3 35.9 %copy-start.3 = (f32[512,256]{1,0:T(8,128)}, f32[512,256]{1,0:T(8,128)S(1)}, u32[]{:S(2)}) copy-start(f32[512,256]{1,0:T(8,128)S(1)} %collective-permute-done.4.refs_2_) | copy-start | bytes 1572868
  28.3 15.4 %collective-permute-start.5 = (f32[512,256]{1,0:T(8,128)S(1)}, f32[512,256]{1,0:T(8,128)S(1)}, u32[]{:S(2)}, u32[]{:S(2)}) collective-permute-start(f32[512,256]{1,0:T(8,128)S(1)} %collective-permute-done.4.refs_2_), channel_id=1, source_target_pairs={{0,28},{4,0},{8,4},{12,8},{16,12},{20,16},{24,20},{28,24},{1,29},{... | collective-permute-start | bytes 1572872 | tf_op jit(solution)/shard_map/ppermute | solution.py:242
  38.6 25.6 %copy-start.4 = (f32[512,256]{1,0:T(8,128)}, f32[512,256]{1,0:T(8,128)S(1)}, u32[]{:S(2)}) copy-start(f32[512,256]{1,0:T(8,128)S(1)} %collective-permute-done.1.refs_3_) | copy-start | bytes 1572868
  38.6 14.0 %collective-permute-start.2 = (f32[512,256]{1,0:T(8,128)S(1)}, f32[512,256]{1,0:T(8,128)S(1)}, u32[]{:S(2)}, u32[]{:S(2)}) collective-permute-start(f32[512,256]{1,0:T(8,128)S(1)} %collective-permute-done.1.refs_3_), channel_id=1, source_target_pairs={{0,4},{4,8},{8,12},{12,16},{16,20},{20,24},{24,28},{28,0},{1,5},{5... | collective-permute-start | bytes 1572872 | tf_op jit(solution)/shard_map/ppermute | solution.py:242
  43.8 20.4 %copy-start.5 = (f32[512,256]{1,0:T(8,128)}, f32[512,256]{1,0:T(8,128)S(1)}, u32[]{:S(2)}) copy-start(f32[512,256]{1,0:T(8,128)S(1)} %collective-permute-done.5.refs_4_) | copy-start | bytes 1572868
  43.8 15.1 %collective-permute-start.6 = (f32[512,256]{1,0:T(8,128)S(1)}, f32[512,256]{1,0:T(8,128)S(1)}, u32[]{:S(2)}, u32[]{:S(2)}) collective-permute-start(f32[512,256]{1,0:T(8,128)S(1)} %collective-permute-done.5.refs_4_), channel_id=1, source_target_pairs={{0,28},{4,0},{8,4},{12,8},{16,12},{20,16},{24,20},{28,24},{1,29},{... | collective-permute-start | bytes 1572872 | tf_op jit(solution)/shard_map/ppermute | solution.py:242
  52.6 11.6 %copy-start.6 = (f32[512,256]{1,0:T(8,128)}, f32[512,256]{1,0:T(8,128)S(1)}, u32[]{:S(2)}) copy-start(f32[512,256]{1,0:T(8,128)S(1)} %collective-permute-done.2.refs_5_) | copy-start | bytes 1572868
  52.6 18.0 %collective-permute-start.3 = (f32[512,256]{1,0:T(8,128)S(1)}, f32[512,256]{1,0:T(8,128)}, u32[]{:S(2)}, u32[]{:S(2)}) collective-permute-start(f32[512,256]{1,0:T(8,128)S(1)} %collective-permute-done.2.refs_5_), channel_id=1, source_target_pairs={{0,4},{4,8},{8,12},{12,16},{16,20},{20,24},{24,28},{28,0},{1,5},{5... | collective-permute-start | bytes 1572872 | tf_op jit(solution)/shard_map/ppermute | solution.py:242
  58.9 5.4 %copy-start.7 = (f32[512,256]{1,0:T(8,128)}, f32[512,256]{1,0:T(8,128)S(1)}, u32[]{:S(2)}) copy-start(f32[512,256]{1,0:T(8,128)S(1)} %collective-permute-done.6.refs_6_) | copy-start | bytes 1572868
  73.7 19.8 %all-to-all-start.1 = ((f32[4,128,512]{2,1,0:T(8,128)}), f32[4,128,512]{2,1,0:T(8,128)S(1)}, u32[]{:S(2)}, u32[]{:S(2)}) async-start(f32[4,128,512]{2,1,0:T(8,128)} %bitcast.14), calls=%async_computation.1 | async-start | bytes 2097152 | tf_op jit(solution)/shard_map/all_to_all | solution.py:259
  93.4 3.5 %copy-start = (f32[4,128,512]{2,1,0:T(8,128)}, f32[4,128,512]{2,1,0:T(8,128)S(1)}, u32[]{:S(2)}) copy-start(f32[4,128,512]{2,1,0:T(8,128)S(1)} %all-to-all-done.1.terms) | copy-start | bytes 3145732
  93.4 18.1 %all-to-all-start = ((f32[4,128,512]{2,1,0:T(8,128)}), f32[4,128,512]{2,1,0:T(8,128)S(1)}, u32[]{:S(2)}, u32[]{:S(2)}) async-start(f32[4,128,512]{2,1,0:T(8,128)} %bitcast.15), calls=%async_computation | async-start | bytes 2097152 | tf_op jit(solution)/shard_map/all_to_all | solution.py:262
  111.6 1.0 copy-start.1
Sparse Core Ops, SparseCore 0:
  9.5 54.6 all-gather.2
